TPU v7x, 32 devices: a whole 2x2x4 slice. The times are simulated.
32 devices in a mesh: lat: 4 (over y, x), lon: 8 (over z, core).
Axes of the slice: x: 2, y: 2, z: 4, core: 2. Of those that a mesh axis runs over, the one named last changes fastest.
Arguments:
- field_in: bfloat16 [128, 512, 256], P('lat', 'lon'), may hold values from -6 to 6
- kernel_one: bfloat16 [3, 3, 256, 256], replicated, may hold values from -0.125 to 0.125
- kernel_two: bfloat16 [3, 3, 256, 256], replicated, may hold values from -0.125 to 0.125
- cotangent: bfloat16 [128, 512, 256], P('lat', 'lon'), may hold values from -6 to 6
Outputs:
- field_out: bfloat16 [128, 512, 256], P('lat', 'lon')
- grad_in: bfloat16 [128, 512, 256], P('lat', 'lon')
- grad_kernel_one: float32 [3, 3, 256, 256], replicated
- grad_kernel_two: float32 [3, 3, 256, 256], replicated
All inputs are finite; a program needn't handle non-finite values.
Results may differ from a plain program's by a relative error of at most 0.0056.
Values may be sent and summed in bfloat16 or wider, within the bound.
No kernel may reach another device: no remote copies, remote signals or barrier semaphores. Data moves between devices by JAX's collectives and lax.ppermute only.
A program may use at most 128 MiB of HBM per device.

v0:
```python
import functools

import jax
import jax.numpy as jnp
from jax import lax
from jax.experimental import pallas as pl
from jax.experimental.pallas import tpu as pltpu
from jax.sharding import PartitionSpec as P

BOTH = ("lat", "lon")
F32, BF16 = jnp.float32, jnp.bfloat16


def kernel_call(body, name, outs, ins, flops=0, scratch=(), aliases=None, limit=24):
    out_shape, out_specs, in_specs, arrays = [], [], [], []
    for shape, kind, *place in outs:
        out_shape.append(pltpu.HBM(shape, kind) if place else pltpu.VMEM(shape, kind))
        out_specs.append(pl.BlockSpec(memory_space=pltpu.HBM if place else pltpu.VMEM))
    for x in ins:
        far = isinstance(x, tuple)
        arrays.append(x[0] if far else x)
        in_specs.append(pl.BlockSpec(memory_space=pltpu.HBM if far else pltpu.VMEM))
    moved = sum(x.size * x.dtype.itemsize for x in arrays)
    return pl.pallas_call(
        body,
        out_shape=out_shape,
        in_specs=in_specs,
        out_specs=out_specs,
        scratch_shapes=list(scratch),
        input_output_aliases=aliases or {},
        compiler_params=pltpu.CompilerParams(vmem_limit_bytes=limit << 20),
        cost_estimate=pl.CostEstimate(flops=flops, bytes_accessed=moved, transcendentals=0),
        name=name,
    )(*arrays)


def in_hbm(x):
    return (pltpu.with_memory_space_constraint(x, pltpu.HBM),)


def sigmoid(value):
    return 1.0 / (1.0 + jnp.exp(-value))


def silu(value):
    return value / (1.0 + jnp.exp(-value))


def same(value):
    return value


def silu_grad(value):
    sig = sigmoid(value)
    return sig * (1.0 + value * (1.0 - sig))


def aligned(start, step):
    return pl.multiple_of(start, step)


def is_odd(axis):
    return lax.axis_index(axis) % 2 == 1


def put_shifted(out, start, x, cols, left=None, right=None):
    chans = x.shape[1]
    col = lax.broadcasted_iota(jnp.int32, x.shape, 0)
    before = pltpu.roll(x, 1, 0)
    after = pltpu.roll(x, cols - 1, 0)
    if left is not None:
        before = jnp.where(col == 0, left, before)
        after = jnp.where(col == cols - 1, right, after)
    where = pl.ds(start, cols)
    out[where, :chans] = before.astype(BF16)
    out[where, chans : 2 * chans] = x.astype(BF16)
    out[where, 2 * chans :] = after.astype(BF16)


def conv_rows(shifted, weights, start, count, cols):
    piece = jnp.concatenate([shifted[pl.ds(start + i * cols, count), :] for i in range(3)], axis=1)
    return jnp.dot(piece, weights[...], preferred_element_type=F32)


def ends_kernel(cols, field_hbm, cot_hbm, field, cot, near, far, lines, sems):
    rows = field.shape[0] // cols
    copies = [
        pltpu.make_async_copy(field_hbm, field, sems.at[0]),
        pltpu.make_async_copy(cot_hbm, cot, sems.at[1]),
    ]
    for copy in copies:
        copy.start()
    odd = is_odd("lon")
    for n, (copy, source) in enumerate(zip(copies, (field, cot))):
        copy.wait()
        for r in range(rows):
            first = source[r * cols : r * cols + 16, :].astype(F32)[:1]
            last = source[(r + 1) * cols - 16 : (r + 1) * cols, :].astype(F32)[15:]
            lines[n * rows + r : n * rows + r + 1, :] = jnp.where(odd, first, last)
            lines[(2 + n) * rows + r : (2 + n) * rows + r + 1, :] = jnp.where(odd, last, first)
    near[...] = lines[: 2 * rows, :].astype(BF16)
    far[...] = lines[2 * rows :, :].astype(BF16)


def prep_kernel(cols, field, one_hbm, two_hbm, act3, k_one, k_two, t_one, t_two, sems):
    rows = field.shape[0] // cols
    chans = field.shape[1]
    copies = [
        pltpu.make_async_copy(one_hbm, k_one, sems.at[0]),
        pltpu.make_async_copy(two_hbm, k_two, sems.at[1]),
    ]
    for copy in copies:
        copy.start()

    def body(r, carry):
        at = aligned(r * cols, cols)
        to = aligned((r + 1) * cols, cols)
        put_shifted(act3, to, silu(field[pl.ds(at, cols), :].astype(F32)), cols)
        return carry

    lax.fori_loop(0, rows, body, 0, unroll=2)
    for copy in copies:
        copy.wait()
    for tap in range(9):
        to = slice((8 - tap) * chans, (9 - tap) * chans)
        at = slice(tap * chans, (tap + 1) * chans)
        t_one[to, :] = k_one[at, :].T
        t_two[to, :] = k_two[at, :].T


def edge_kernel(cols, field, cot, near, far, send_near, send_far):
    rows = field.shape[0] // cols
    chans = field.shape[1]
    odd = is_odd("lon")
    odd_lat = lax.axis_index("lat") % 2
    low, high = near[...].astype(F32), far[...].astype(F32)
    left, right = jnp.where(odd, low, high), jnp.where(odd, high, low)
    for out, first in ((send_near, odd_lat), (send_far, 1 - odd_lat)):
        start = aligned((1 - first) * (rows - 2) * cols, cols)
        out[: 2 * cols, :] = field[pl.ds(start, 2 * cols), :]
        out[2 * cols : 4 * cols, :] = cot[pl.ds(start, 2 * cols), :]
        lines = []
        for base in (0, rows):
            for r in range(2):
                for side in (left, right):
                    top = side[base + r : base + r + 1]
                    bottom = side[base + rows - 2 + r : base + rows - 1 + r]
                    lines.append(jnp.where(first == 1, top, bottom))
        lines.append(jnp.zeros((8, chans), F32))
        out[4 * cols :, :] = jnp.concatenate(lines, axis=0).astype(BF16)


def inner_kernel(cols, near, far, cot, k_one, _a, act3, cot3, hid, mid, turned, edges):
    rows = near.shape[0] // 2
    chans = near.shape[1]
    odd = is_odd("lon")
    low, high = near[...].astype(F32), far[...].astype(F32)
    edges[: 2 * rows, :] = jnp.where(odd, low, high)
    edges[2 * rows :, :] = jnp.where(odd, high, low)
    line = lax.broadcasted_iota(jnp.int32, (16, chans), 0)

    def patch(r, carry):
        start = aligned((r + 1) * cols, cols)
        end = aligned((r + 2) * cols - 16, 16)
        left = silu(edges[pl.ds(r, 1), :]).astype(BF16).astype(F32)
        right = silu(edges[pl.ds(2 * rows + r, 1), :]).astype(BF16).astype(F32)
        old = act3[pl.ds(start, 16), :chans].astype(F32)
        act3[pl.ds(start, 16), :chans] = jnp.where(line == 0, left, old).astype(BF16)
        old = act3[pl.ds(end, 16), 2 * chans :].astype(F32)
        act3[pl.ds(end, 16), 2 * chans :] = jnp.where(line == 15, right, old).astype(BF16)
        x = cot[pl.ds(aligned(r * cols, cols), cols), :].astype(F32)
        left, right = edges[pl.ds(rows + r, 1), :], edges[pl.ds(3 * rows + r, 1), :]
        put_shifted(cot3, start, x, cols, left, right)
        return carry

    lax.fori_loop(0, rows, patch, 0, unroll=4)
    for r, count in row_blocks(1, rows - 1):
        to = pl.ds((r + 1) * cols, count * cols)
        got = conv_rows(act3, k_one, r * cols, count * cols, cols)
        hid[to, :] = got
        mid[to, :] = silu(got).astype(BF16)
    own = slice(3 * cols, (rows - 1) * cols)
    turned[:, 2 * cols : (rows - 2) * cols] = mid[own, :].T


def row_blocks(first, end):
    count = -(-(end - first) // 3)
    return [(r, min(count, end - r)) for r in range(first, end, count)]


def halo_rows(near, far):
    odd = is_odd("lat")
    low, high = near[...].astype(F32), far[...].astype(F32)
    return jnp.where(odd, low, high), jnp.where(odd, high, low)


def put_halo(part, halos, n, cols, fix, source):
    rows = source.shape[0] // cols - 2
    for half, halo in enumerate(halos):
        base = half * 4 * cols
        inside = rows - 1 if half else 1
        own = slice(inside * cols, (inside + 2) * cols)
        part[base + (1 - half) * 2 * cols : base + (2 - half) * 2 * cols, :] = source[own, :]
        for r in range(2):
            x = fix(halo[(2 * n + r) * cols : (2 * n + r + 1) * cols])
            corner = 4 * cols + 4 * n + 2 * r
            left, right = fix(halo[corner : corner + 1]), fix(halo[corner + 1 : corner + 2])
            put_shifted(part, base + (half * 2 + r) * cols, x, cols, left, right)


def edge_mask(half, cols, shape):
    lat = lax.axis_index("lat")
    there = lat < lax.axis_size("lat") - 1 if half else lat > 0
    line = lax.broadcasted_iota(jnp.int32, shape, 0)
    inner = line < cols if half else line >= cols
    return jnp.logical_or(inner, there)


def outer_kernel(
    cols, near, far, k_one, _a, _c, _h, _m, _t,
    act3, cot3, hid, mid, turned, keep, send, part, term,
):
    chans = mid.shape[1]
    rows = mid.shape[0] // cols - 2
    halos = halo_rows(near, far)
    put_halo(part, halos, 1, cols, same, cot3)
    cot3[:cols, :] = part[cols : 2 * cols, :]
    cot3[(rows + 1) * cols :, :] = part[6 * cols : 7 * cols, :]
    put_halo(part, halos, 0, cols, silu, act3)
    act3[:cols, :] = part[cols : 2 * cols, :]
    act3[(rows + 1) * cols :, :] = part[6 * cols : 7 * cols, :]
    for half in range(2):
        to = half * rows * cols
        got = conv_rows(part, k_one, half * 4 * cols, 2 * cols, cols)
        hid[to : to + 2 * cols, :] = got
        value = jnp.where(edge_mask(half, cols, got.shape), silu(got), 0.0)
        mid[to : to + 2 * cols, :] = value.astype(BF16)
    turned[:, : 2 * cols] = mid[cols : 3 * cols, :].T
    turned[:, (rows - 2) * cols :] = mid[(rows - 1) * cols : (rows + 1) * cols, :].T
    for i in range(3):
        got = jnp.dot(
            turned[...], cot3[i * cols : (i + rows) * cols, :], preferred_element_type=F32
        )
        for j in range(3):
            tap = (2 - i) * 3 + 2 - j
            term[tap * chans : (tap + 1) * chans, :] = got[:, j * chans : (j + 1) * chans]
    split(term, keep, send)


def split(term, keep, send):
    half = keep.shape[0]
    bit = lax.axis_index("lon") % 2
    keep[...] = term[pl.ds(aligned(bit * half, 16), half), :]
    send[...] = term[pl.ds(aligned((1 - bit) * half, 16), half), :].astype(BF16)


def back_kernel(cols, near, far, t_two, cot3, hid, mid, ghid, turned, side_near, side_far, part, lines):
    chans = mid.shape[1]
    rows = mid.shape[0] // cols - 2
    for r, count in row_blocks(1, rows - 1):
        to = pl.ds((r + 1) * cols, count * cols)
        got = conv_rows(cot3, t_two, r * cols, count * cols, cols)
        ghid[to, :] = (got * silu_grad(hid[to, :])).astype(BF16)
    put_halo(part, halo_rows(near, far), 1, cols, same, cot3)
    for half in range(2):
        to = slice(half * rows * cols, half * rows * cols + 2 * cols)
        got = conv_rows(part, t_two, half * 4 * cols, 2 * cols, cols)
        value = jnp.where(edge_mask(half, cols, got.shape), got * silu_grad(hid[to, :]), 0.0)
        ghid[to, :] = value.astype(BF16)
    turned[...] = ghid[cols : (rows + 1) * cols, :].T
    lanes = side_near.shape[0] // 2
    odd = is_odd("lon")
    for n, source in enumerate((mid, ghid)):
        for r in range(rows + 2):
            first = source[r * cols : r * cols + 16, :].astype(F32)[:1]
            last = source[(r + 1) * cols - 16 : (r + 1) * cols, :].astype(F32)[15:]
            at = n * lanes + r
            lines[at : at + 1, :] = jnp.where(odd, first, last)
            lines[2 * lanes + at : 2 * lanes + at + 1, :] = jnp.where(odd, last, first)
        for base in (n * lanes, (2 + n) * lanes):
            lines[base + rows + 2 : base + lanes, :] = jnp.zeros((lanes - rows - 2, chans), F32)
    side_near[...] = lines[: 2 * lanes, :].astype(BF16)
    side_far[...] = lines[2 * lanes :, :].astype(BF16)


def grad_one_kernel(cols, turned, act3, keep, send, term):
    chans, cells = turned.shape
    for i in range(3):
        got = jnp.dot(
            turned[...], act3[i * cols : i * cols + cells, :], preferred_element_type=F32
        )
        for j in range(3):
            tap = i * 3 + j
            term[tap * chans : (tap + 1) * chans, :] = got[:, j * chans : (j + 1) * chans].T
    split(term, keep, send)


def last_kernel(backward, first, count, cols, near, far, value, weights, field, cot, *rest):
    out, edges, shifted, result, sems = rest[-5:]
    lanes = near.shape[0] // 2
    odd = is_odd("lon")
    part = slice(lanes, None) if backward else slice(0, lanes)
    low, high = near[part, :].astype(F32), far[part, :].astype(F32)
    edges[:lanes, :] = jnp.where(odd, low, high)
    edges[lanes:, :] = jnp.where(odd, high, low)

    def body(r, carry):
        x = value[pl.ds(aligned((first + r) * cols, cols), cols), :].astype(F32)
        left, right = edges[pl.ds(first + r, 1), :], edges[pl.ds(lanes + first + r, 1), :]
        put_shifted(shifted, aligned(r * cols, cols), x, cols, left, right)
        return carry

    lax.fori_loop(0, count + 2, body, 0, unroll=2)
    step = max(count // 2, 1)
    copies = []
    for n, r in enumerate(range(0, count, step)):
        at = slice((first + r) * cols, (first + r + step) * cols)
        to = slice(r * cols, (r + step) * cols)
        got = conv_rows(shifted, weights, r * cols, step * cols, cols)
        x = field[at, :].astype(F32)
        if backward:
            result[to, :] = (cot[at, :].astype(F32) + got * silu_grad(x)).astype(BF16)
        else:
            result[to, :] = (x + got).astype(BF16)
        copies.append(pltpu.make_async_copy(result.at[to, :], out.at[at, :], sems.at[n]))
        copies[-1].start()
    for copy in copies:
        copy.wait()


def step_bit(step):
    lat_count, lon_count = lax.axis_size("lat"), lax.axis_size("lon")
    even, odd, _ = swap_plan(lat_count, lon_count)
    me = lax.axis_index("lat") * lon_count + lax.axis_index("lon")
    return jnp.where(me % 2 == 1, (me >> odd[step]) & 1, (me >> even[step]) & 1)


def halves(bit, half):
    mine = pl.ds(aligned(bit * half, 16), half)
    other = pl.ds(aligned((1 - bit) * half, 16), half)
    return mine, other


def add_split_kernel(step, keep, got, out, send):
    mine, other = halves(step_bit(step), out.shape[0])
    out[...] = keep[mine, :] + got[mine, :].astype(F32)
    send[...] = (keep[other, :] + got[other, :].astype(F32)).astype(BF16)


def add_round_kernel(keep, got, out):
    out[...] = (keep[...].astype(F32) + got[...].astype(F32)).astype(BF16)


def join_kernel(step, value, got, out):
    mine, other = halves(step_bit(step), value.shape[0])
    out[mine, :] = value[...]
    out[other, :] = got[...]


def final_kernel(factor, own, value, *rest):
    out, scaled, sems = rest[-3:]
    half, chunks = value.shape[0], sems.shape[0]
    bit = step_bit(0)
    base = (bit if own else 1 - bit) * half
    copies = []
    for n in range(chunks):
        at = pl.ds(n * (half // chunks), half // chunks)
        to = pl.ds(aligned(base + n * (half // chunks), 16), half // chunks)
        scaled[at, :] = value[at, :].astype(F32) * factor
        copies.append(pltpu.make_async_copy(scaled.at[at, :], out.at[to, :], sems.at[n]))
        copies[-1].start()
    for copy in copies:
        copy.wait()


def paired(count, offset, periodic):
    pairs = []
    for low in range(offset, count, 2):
        high = low + 1
        if high == count:
            if not periodic:
                continue
            high = 0
        pairs += [(low, high), (high, low)]
    return pairs


def log2(count):
    assert count & (count - 1) == 0
    return count.bit_length() - 1


def swap_plan(lat_count, lon_count):
    lon_bits = log2(lon_count)
    lat = list(range(lon_bits, lon_bits + log2(lat_count)))
    lon = list(range(1, lon_bits))
    even = [0] + lat + lon
    odd = [0] + lat[::-1] + lon[::-1]
    pairs = [
        [(d, d ^ (1 << (o if d & 1 else e))) for d in range(lat_count * lon_count)]
        for e, o in zip(even, odd)
    ]
    return even, odd, pairs


def swapped(value, pairs):
    return lax.ppermute(value, BOTH, pairs)


def after(value, *others):
    return lax.optimization_barrier((value, *others))[0]


class Summed:
    def __init__(self, keep, send, pairs, factor):
        self.keep, self.send, self.pairs, self.factor = keep, send, pairs, factor
        self.count, self.step, self.value = len(pairs), 0, None
        self.bits = [step_bit(step) for step in range(self.count)]

    @property
    def sent(self):
        return self.send if self.step < self.count - 1 else self.value

    def start(self):
        step, last = self.step, self.count - 1
        if self.running:
            self.got = swapped(self.sent, self.pairs[step if step <= last else 2 * last - step])

    def finish(self, *others):
        got = after(self.got, *others) if others else self.got
        keep, count, step = self.keep, self.count, self.step
        chans = keep.shape[1]
        self.step += 1
        if step < count - 2:
            half = keep.shape[0] // 2
            if half % 16:
                value = keep + got.astype(F32)
                bit = self.bits[step + 1]
                self.keep = lax.dynamic_slice_in_dim(value, bit * half, half)
                send = lax.dynamic_slice_in_dim(value, (1 - bit) * half, half)
                self.send = send.astype(BF16)
            else:
                body = functools.partial(add_split_kernel, step + 1)
                outs = [((half, chans), F32), ((half, chans), BF16)]
                self.keep, self.send = kernel_call(body, "sum_step", outs, [keep, got], limit=16)
        elif step < count:
            mine = keep if step == count - 2 else self.value
            outs = [(keep.shape, BF16)]
            (self.value,) = kernel_call(add_round_kernel, "sum_round", outs, [mine, got], limit=16)
        else:
            back = 2 * count - 2 - step
            value = self.value
            half = value.shape[0]
            if back == 0:
                out = ((2 * half, chans), F32, "hbm")
                scratch = [pltpu.VMEM((half, chans), F32), pltpu.SemaphoreType.DMA((4,))]
                result = None
                for own in (True, False):
                    body = functools.partial(final_kernel, self.factor, own)
                    x, extra = (value, []) if own else (after(got, result), [0])
                    (result,) = kernel_call(
                        body,
                        "scaled",
                        [out],
                        [x] + [in_hbm(result) for _ in extra],
                        scratch=scratch,
                        aliases={1: 0} if extra else None,
                        limit=16,
                    )
                self.value = result
            elif half % 16:
                low = jnp.where(self.bits[back] == 1, got, value)
                high = jnp.where(self.bits[back] == 1, value, got)
                self.value = jnp.concatenate([low, high])
            else:
                body = functools.partial(join_kernel, back)
                outs = [((2 * half, chans), BF16)]
                (self.value,) = kernel_call(body, "join", outs, [value, got], limit=16)

    @property
    def running(self):
        return self.step < 2 * self.count - 1


def shards(field_in, kernel_one, kernel_two, cotangent):
    rows, cols, chans = field_in.shape
    cells, tall = rows * cols, (rows + 2) * cols
    lat_count, lon_count = lax.axis_size("lat"), lax.axis_size("lon")
    _, _, pairs = swap_plan(lat_count, lon_count)
    factor = float(rows * lat_count * cols * lon_count) ** (-0.5)
    flops = 2 * cells * 9 * chans * chans
    sems = pltpu.SemaphoreType.DMA((2,))

    def call(body, *args, **kwargs):
        return kernel_call(functools.partial(body, cols), *args, **kwargs)

    near_lon, far_lon = paired(lon_count, 0, True), paired(lon_count, 1, True)
    near_lat, far_lat = paired(lat_count, 0, False), paired(lat_count, 1, False)

    tile = ((cells, chans), BF16)
    line = ((2 * rows, chans), BF16)
    field, cot, near, far = call(
        ends_kernel,
        "ends",
        [tile, tile, line, line],
        [in_hbm(field_in.reshape(cells, chans)), in_hbm(cotangent.reshape(cells, chans))],
        scratch=[pltpu.VMEM((4 * rows, chans), F32), sems],
    )
    lon_near = lax.ppermute(near, "lon", near_lon)
    lon_far = lax.ppermute(far, "lon", far_lon)
    wide = ((tall, 3 * chans), BF16)
    square = ((9 * chans, chans), BF16)
    act3, k_one, k_two, t_one, t_two = call(
        prep_kernel,
        "prep",
        [wide, square, square, square, square],
        [field] + [in_hbm(k.reshape(9 * chans, chans)) for k in (kernel_one, kernel_two)],
        flops=flops,
        scratch=[sems],
    )

    strip = ((4 * cols + 16, chans), BF16)
    send_near, send_far = call(
        edge_kernel, "edges", [strip, strip], [field, cot, after(lon_near, act3), lon_far]
    )
    lat_near = lax.ppermute(send_near, "lat", near_lat)
    lat_far = lax.ppermute(send_far, "lat", far_lat)

    high = ((tall, chans), F32)
    flat = ((tall, chans), BF16)
    turned = ((chans, cells), BF16)
    act3, cot3, hid, mid, mid_t = call(
        inner_kernel,
        "inner_rows",
        [wide, wide, high, flat, turned],
        [lon_near, lon_far, cot, k_one, after(act3, send_near, send_far)],
        flops=flops,
        scratch=[pltpu.VMEM((4 * rows, chans), F32)],
        aliases={4: 0},
    )
    half = 9 * chans // 2
    parts = [((half, chans), F32), ((half, chans), BF16)]
    part = pltpu.VMEM((8 * cols, 3 * chans), BF16)
    term = pltpu.VMEM((9 * chans, chans), F32)
    act3, cot3, hid, mid, _, keep, send = call(
        outer_kernel,
        "grad_two",
        [wide, wide, high, flat, turned] + parts,
        [lat_near, lat_far, k_one, act3, cot3, hid, mid, mid_t],
        flops=flops,
        scratch=[part, term],
        aliases={3: 0, 4: 1, 5: 2, 6: 3, 7: 4},
    )
    two = Summed(keep, send, pairs, factor)
    two.start()

    lanes = -(-(rows + 2) // 16) * 16
    sides = ((2 * lanes, chans), BF16)
    ghid, ghid_t, side_near, side_far = call(
        back_kernel,
        "grad_hid",
        [flat, turned, sides, sides],
        [lat_near, lat_far, t_two, cot3, hid, mid],
        flops=flops,
        scratch=[part, pltpu.VMEM((4 * lanes, chans), F32)],
    )
    two.finish(ghid)

    side_near, side_far = after(side_near, two.sent), after(side_far, two.sent)
    two.start()
    side_near = lax.ppermute(side_near, "lon", near_lon)
    side_far = lax.ppermute(side_far, "lon", far_lon)
    keep, send = call(
        grad_one_kernel,
        "grad_one",
        parts,
        [after(ghid_t, two.sent), act3],
        flops=flops,
        scratch=[term],
    )
    side_near, side_far = after(side_near, keep), after(side_far, keep)
    two.finish(keep)
    one = Summed(keep, after(send, two.sent, side_near, side_far), pairs, factor)
    one.start()
    two.start()

    results = [None, None]
    pieces = [(0, 0), (0, 1), (1, 0), (1, 1)]

    def piece(which, part, *others):
        count = rows // 2
        old = results[which]
        ins = [side_near, side_far, after((mid, ghid)[which], *others)]
        ins += [(k_two, t_one)[which], field, cot]
        (results[which],) = call(
            functools.partial(last_kernel, bool(which), part * count, count),
            ("field_out", "grad_in")[which],
            [((cells, chans), BF16, "hbm")],
            ins + ([in_hbm(old)] if part else []),
            flops=flops // 2,
            scratch=[
                pltpu.VMEM((2 * lanes, chans), F32),
                pltpu.VMEM(((count + 2) * cols, 3 * chans), BF16),
                pltpu.VMEM((count * cols, chans), BF16),
                sems,
            ],
            aliases={len(ins): 0} if part else None,
        )
        return results[which]

    for which, half in pieces:
        fill = piece(which, half, one.sent, two.sent)
        one.finish(fill)
        two.finish(fill, one.sent)
        one.start()
        two.start()
    while one.running:
        one.finish(two.sent)
        one.start()
        if two.running:
            two.finish(one.sent)
            two.start()
    shape = (3, 3, chans, chans)
    return (
        results[0].reshape(rows, cols, chans),
        results[1].reshape(rows, cols, chans),
        one.value.reshape(shape),
        two.value.reshape(shape),
    )


def solution(mesh):
    return jax.shard_map(
        shards,
        mesh=mesh,
        in_specs=(P("lat", "lon", None), P(), P(), P("lat", "lon", None)),
        out_specs=(P("lat", "lon", None), P("lat", "lon", None), P(), P()),
        check_vma=False,
    )
```

profile of v0, /device:TPU:1, one launch (start us, length us, event | category | flops | bytes accessed | tf_op | source)
XLA Modules:
  0.0 90.4 jit_solution(16578707276984273788)
XLA Ops:
  0.6 1.7 %ends.1 = (bf16[2048,256]{1,0:T(8,128)(2,1)S(1)}, bf16[2048,256]{1,0:T(8,128)(2,1)S(1)}, bf16[64,256]{1,0:T(8,128)(2,1)S(1)}, bf16[64,256]{1,0:T(8,128)(2,1)S(1)}) custom-call(bf16[2048,256]{1,0:T(8,128)(2,1)} %bitcast.12, bf16[2048,256]{1,0:T(8,128)(2,1)} %bitcast.13), custom_call_target="tpu_custom_call" | custom-call | bytes 2097152 | tf_op jit(solution)/shard_map/ends/pallas_call | solution.py:24
  2.4 2.7 %collective-permute-start.1 = (bf16[64,256]{1,0:T(8,128)(2,1)S(1)}, bf16[64,256]{1,0:T(8,128)(2,1)S(1)}, u32[]{:S(2)}, u32[]{:S(2)}) collective-permute-start(bf16[64,256]{1,0:T(8,128)(2,1)S(1)} %get-tuple-element.81), channel_id=1, source_target_pairs={{1,2},{2,1},{3,4},{4,3},{5,6},{6,5},{7,0},{0,7},{9,10},{10,9},{11,... | collective-permute-start | bytes 98312 | tf_op jit(solution)/shard_map/ppermute | solution.py:510
  5.1 2.3 %prep.1 = (bf16[2176,768]{1,0:T(8,128)(2,1)S(1)}, bf16[2304,256]{1,0:T(8,128)(2,1)S(1)}, bf16[2304,256]{1,0:T(8,128)(2,1)S(1)}, bf16[2304,256]{1,0:T(8,128)(2,1)S(1)}, bf16[2304,256]{1,0:T(8,128)(2,1)S(1)}) custom-call(bf16[2048,256]{1,0:T(8,128)(2,1)S(1)} %get-tuple-element.76.field, bf16[2304,256]{1,0:T(8,128)(2,1)} %bitcast.14, bf16[2304,256]{1,0:T(8,128)(2,1)} %bitcast.15), custom_call_target="tpu_custom_call" | custom-call | flops 2415919104 | bytes 3407872 | tf_op jit(solution)/shard_map/prep/pallas_call | solution.py:24
  7.5 1.3 %collective-permute-start.2 = (bf16[272,256]{1,0:T(8,128)(2,1)S(1)}, bf16[272,256]{1,0:T(8,128)(2,1)S(1)}, u32[]{:S(2)}, u32[]{:S(2)}) collective-permute-start(bf16[272,256]{1,0:T(8,128)(2,1)S(1)} %get-tuple-element.82), channel_id=1, source_target_pairs={{0,8},{8,0},{16,24},{24,16},{1,9},{9,1},{17,25},{25,17},{2,10},{10... | collective-permute-start | bytes 417800 | tf_op jit(solution)/shard_map/ppermute | solution.py:526
  9.4 3.5 %inner_rows.1 = (bf16[2176,768]{1,0:T(8,128)(2,1)S(1)}, bf16[2176,768]{1,0:T(8,128)(2,1)S(1)}, f32[2176,256]{1,0:T(8,128)S(1)}, bf16[2176,256]{1,0:T(8,128)(2,1)S(1)}, bf16[256,2048]{1,0:T(8,128)(2,1)S(1)}) custom-call(bf16[64,256]{1,0:T(8,128)(2,1)S(1)} %collective-permute-done.near, ...), custom_call_target="tpu_custom_call", output_to_operand_aliasing={{0}: (4, {})} | custom-call | flops 2415919104 | bytes 5636096 | tf_op jit(solution)/shard_map/inner_rows/pallas_call | solution.py:24
  12.9 3.5 %grad_two.1 = (bf16[2176,768]{1,0:T(8,128)(2,1)S(1)}, bf16[2176,768]{1,0:T(8,128)(2,1)S(1)}, f32[2176,256]{1,0:T(8,128)S(1)}, bf16[2176,256]{1,0:T(8,128)(2,1)S(...) custom-call(bf16[272,256]{1,0:T(8,128)(2,1)S(1)} %collective-permute, ...), custom_call_target="tpu_custom_call", output_to_operand_aliasing={{0}: (3, {}), {1}: (4, {}), {2}: (5, {}), {3}: (6, {}), {4}... | custom-call | flops 2415919104 | bytes 12533760 | tf_op jit(solution)/shard_map/grad_two/pallas_call | solution.py:24
  16.5 2.8 %collective-permute-start.4 = (bf16[1152,256]{1,0:T(8,128)(2,1)S(1)}, bf16[1152,256]{1,0:T(8,128)(2,1)S(1)}, u32[]{:S(2)}, u32[]{:S(2)}) collective-permute-start(bf16[1152,256]{1,0:T(8,128)(2,1)S(1)} %get-tuple-element.97), channel_id=1, source_target_pairs={{0,1},{1,0},{2,3},{3,2},{4,5},{5,4},{6,7},{7,6},{8,9},{9,8},{10,11... | collective-permute-start | bytes 1769480 | tf_op jit(solution)/shard_map/ppermute | solution.py:407
  19.3 3.1 %grad_hid.1 = (bf16[2176,256]{1,0:T(8,128)(2,1)S(1)}, bf16[256,2048]{1,0:T(8,128)(2,1)S(1)}, bf16[96,256]{1,0:T(8,128)(2,1)S(1)}, bf16[96,256]{1,0:T(8,128)(2,1)S(1)}) custom-call(bf16[272,256]{1,0:T(8,128)(2,1)S(1)} %collective-permute-done.2.near, bf16[272,256]{1,0:T(8,128)(2,1)S(1)} %collective-permute-done.3.far, ...), custom_call_target="tpu_custom_call" | custom-call | flops 2415919104 | bytes 8142848 | tf_op jit(solution)/shard_map/grad_hid/pallas_call | solution.py:24
  22.6 5.0 %collective-permute-start.7 = (bf16[576,256]{1,0:T(8,128)(2,1)S(1)}, bf16[576,256]{1,0:T(8,128)(2,1)S(1)}, u32[]{:S(2)}, u32[]{:S(2)}) collective-permute-start(bf16[576,256]{1,0:T(8,128)(2,1)S(1)} %get-tuple-element.100), channel_id=1, source_target_pairs={{0,8},{1,17},{2,10},{3,19},{4,12},{5,21},{6,14},{7,23},{8,0},{9,25... | collective-permute-start | bytes 884744 | tf_op jit(solution)/shard_map/ppermute | solution.py:407
  27.6 3.2 %grad_one.1 = (f32[1152,256]{1,0:T(8,128)S(1)}, bf16[1152,256]{1,0:T(8,128)(2,1)S(1)}) custom-call(bf16[256,2048]{1,0:T(8,128)(2,1)S(1)} %get-tuple-element.103.turned, bf16[2176,768]{1,0:T(8,128)(2,1)S(1)} %get-tuple-element.104.act3), custom_call_target="tpu_custom_call" | custom-call | flops 2415919104 | bytes 4390912 | tf_op jit(solution)/shard_map/grad_one/pallas_call | solution.py:24
  31.7 1.8 %collective-permute-start.8 = (bf16[1152,256]{1,0:T(8,128)(2,1)S(1)}, bf16[1152,256]{1,0:T(8,128)(2,1)S(1)}, u32[]{:S(2)}, u32[]{:S(2)}) collective-permute-start(bf16[1152,256]{1,0:T(8,128)(2,1)S(1)} %get-tuple-element.114), channel_id=1, source_target_pairs={{0,1},{1,0},{2,3},{3,2},{4,5},{5,4},{6,7},{7,6},{8,9},{9,8},{10,11... | collective-permute-start | bytes 1769480 | tf_op jit(solution)/shard_map/ppermute | solution.py:407
  33.5 2.5 %field_out.2.rest_0_ = bf16[2048,256]{1,0:T(8,128)(2,1)} custom-call(bf16[96,256]{1,0:T(8,128)(2,1)S(1)} %collective-permute-done.5.near, bf16[96,256]{1,0:T(8,128)(2,1)S(1)} %collective-permute-done.6.far, bf16[2176,256]{1,0:T(8,128)(2,1)S(1)} %get-tuple-element.122.mid.value, bf16[2304,256]{1,0:T(8,128)(2,1)S(1)} %get-tuple-element.116.weights, ...), custom_call_target="tpu_custom_call" | custom-call | flops 1207959552 | bytes 4489216 | tf_op jit(solution)/shard_map/field_out/pallas_call | solution.py:24
  37.7 5.2 %collective-permute-done.9.got = bf16[288,256]{1,0:T(8,128)(2,1)S(1)} collective-permute-done((bf16[288,256]{1,0:T(8,128)(2,1)S(1)}, bf16[288,256]{1,0:T(8,128)(2,1)S(1)}, u32[]{:S(2)}, u32[]{:S(2)}) %collective-permute-start.9) | collective-permute-done | bytes 147488 | tf_op jit(solution)/shard_map/ppermute | solution.py:407
  43.7 2.7 %field_out.3 = bf16[2048,256]{1,0:T(8,128)(2,1)} custom-call(bf16[96,256]{1,0:T(8,128)(2,1)S(1)} %collective-permute-done.5.near, bf16[96,256]{1,0:T(8,128)(2,1)S(1)} %collective-permute-done.6.far, bf16[2176,256]{1,0:T(8,128)(2,1)S(1)} %get-tuple-element.122.mid.value, ...), custom_call_target="tpu_custom_call", output_to_operand_aliasing={{}: (6, {})} | custom-call | flops 1207959552 | bytes 5537792 | tf_op jit(solution)/shard_map/field_out/pallas_call | solution.py:24
  48.6 2.8 %grad_in.2.rest_0_ = bf16[2048,256]{1,0:T(8,128)(2,1)} custom-call(bf16[96,256]{1,0:T(8,128)(2,1)S(1)} %collective-permute-done.5.near, bf16[96,256]{1,0:T(8,128)(2,1)S(1)} %collective-permute-done.6.far, bf16[2176,256]{1,0:T(8,128)(2,1)S(1)} %get-tuple-element.134.value, bf16[2304,256]{1,0:T(8,128)(2,1)S(1)} %get-tuple-element.130.weights, ...), custom_call_target="tpu_custom_call" | custom-call | flops 1207959552 | bytes 4489216 | tf_op jit(solution)/shard_map/grad_in/pallas_call | solution.py:24
  51.5 1.5 %collective-permute-start.16 = (bf16[144,256]{1,0:T(8,128)(2,1)S(1)}, bf16[144,256]{1,0:T(8,128)(2,1)S(1)}, u32[]{:S(2)}, u32[]{:S(2)}) collective-permute-start(bf16[144,256]{1,0:T(8,128)(2,1)S(1)} %sum_round.5.value), channel_id=1, source_target_pairs={{0,2},{1,5},{2,0},{3,7},{4,6},{5,1},{6,4},{7,3},{8,10},{9,13},{10,... | collective-permute-start | bytes 221192 | tf_op jit(solution)/shard_map/ppermute | solution.py:407
  54.0 2.8 %grad_in.3 = bf16[2048,256]{1,0:T(8,128)(2,1)} custom-call(bf16[96,256]{1,0:T(8,128)(2,1)S(1)} %collective-permute-done.5.near, bf16[96,256]{1,0:T(8,128)(2,1)S(1)} %collective-permute-done.6.far, bf16[2176,256]{1,0:T(8,128)(2,1)S(1)} %get-tuple-element.134.value, bf16[2304,256]{1,0:T(8,128)(2,1)S(1)} %get-tuple-element.130.weights, ...), custom_call_target="tpu_custom_call", output_to_operand_aliasing={{}: (6, {})} | custom-call | flops 1207959552 | bytes 5537792 | tf_op jit(solution)/shard_map/grad_in/pallas_call | solution.py:24
  56.8 1.4 %collective-permute-done.14.got = bf16[144,256]{1,0:T(8,128)(2,1)S(1)} collective-permute-done((bf16[144,256]{1,0:T(8,128)(2,1)S(1)}, bf16[144,256]{1,0:T(8,128)(2,1)S(1)}, u32[]{:S(2)}, u32[]{:S(2)}) %collective-permute-start.14) | collective-permute-done | bytes 73760 | tf_op jit(solution)/shard_map/ppermute | solution.py:407
  59.3 3.2 %collective-permute-done.15.got = bf16[144,256]{1,0:T(8,128)(2,1)S(1)} collective-permute-done((bf16[144,256]{1,0:T(8,128)(2,1)S(1)}, bf16[144,256]{1,0:T(8,128)(2,1)S(1)}, u32[]{:S(2)}, u32[]{:S(2)}) %collective-permute-start.15) | collective-permute-done | bytes 73760 | tf_op jit(solution)/shard_map/ppermute | solution.py:407
  63.3 4.9 %collective-permute-done.17.got = bf16[144,256]{1,0:T(8,128)(2,1)S(1)} collective-permute-done((bf16[144,256]{1,0:T(8,128)(2,1)S(1)}, bf16[144,256]{1,0:T(8,128)(2,1)S(1)}, u32[]{:S(2)}, u32[]{:S(2)}) %collective-permute-start.17) | collective-permute-done | bytes 73760 | tf_op jit(solution)/shard_map/ppermute | solution.py:407
  68.3 7.0 %collective-permute-start.22 = (bf16[1152,256]{1,0:T(8,128)(2,1)S(1)}, bf16[1152,256]{1,0:T(8,128)(2,1)S(1)}, u32[]{:S(2)}, u32[]{:S(2)}) collective-permute-start(bf16[1152,256]{1,0:T(8,128)(2,1)S(1)} %join.9.value), channel_id=1, source_target_pairs={{0,1},{1,0},{2,3},{3,2},{4,5},{5,4},{6,7},{7,6},{8,9},{9,8},{10,11... | collective-permute-start | bytes 1769480 | tf_op jit(solution)/shard_map/ppermute | solution.py:407
  75.6 4.0 %collective-permute-done.19.got = bf16[288,256]{1,0:T(8,128)(2,1)S(1)} collective-permute-done((bf16[288,256]{1,0:T(8,128)(2,1)S(1)}, bf16[288,256]{1,0:T(8,128)(2,1)S(1)}, u32[]{:S(2)}, u32[]{:S(2)}) %collective-permute-start.19) | collective-permute-done | bytes 147488 | tf_op jit(solution)/shard_map/ppermute | solution.py:407
  82.1 3.5 %collective-permute-done.21.got = bf16[576,256]{1,0:T(8,128)(2,1)S(1)} collective-permute-done((bf16[576,256]{1,0:T(8,128)(2,1)S(1)}, bf16[576,256]{1,0:T(8,128)(2,1)S(1)}, u32[]{:S(2)}, u32[]{:S(2)}) %collective-permute-start.21) | collective-permute-done | bytes 294944 | tf_op jit(solution)/shard_map/ppermute | solution.py:407
  85.7 1.9 %collective-permute-start.23 = (bf16[1152,256]{1,0:T(8,128)(2,1)S(1)}, bf16[1152,256]{1,0:T(8,128)(2,1)S(1)}, u32[]{:S(2)}, u32[]{:S(2)}) collective-permute-start(bf16[1152,256]{1,0:T(8,128)(2,1)S(1)} %join.11.value), channel_id=1, source_target_pairs={{0,1},{1,0},{2,3},{3,2},{4,5},{5,4},{6,7},{7,6},{8,9},{9,8},{10,11... | collective-permute-start | bytes 1769480 | tf_op jit(solution)/shard_map/ppermute | solution.py:407
  (55 shorter events, 15.1 us)
Async XLA Ops:
  2.3 5.1 %collective-permute-start = (bf16[64,256]{1,0:T(8,128)(2,1)S(1)}, bf16[64,256]{1,0:T(8,128)(2,1)S(1)}, u32[]{:S(2)}, u32[]{:S(2)}) collective-permute-start(bf16[64,256]{1,0:T(8,128)(2,1)S(1)} %get-tuple-element.78), channel_id=1, source_target_pairs={{0,1},{1,0},{2,3},{3,2},{4,5},{5,4},{6,7},{7,6},{8,9},{9,8},{10,11... | collective-permute-start | bytes 98312 | tf_op jit(solution)/shard_map/ppermute | solution.py:509
  2.4 5.0 %collective-permute-start.1 = (bf16[64,256]{1,0:T(8,128)(2,1)S(1)}, bf16[64,256]{1,0:T(8,128)(2,1)S(1)}, u32[]{:S(2)}, u32[]{:S(2)}) collective-permute-start(bf16[64,256]{1,0:T(8,128)(2,1)S(1)} %get-tuple-element.81), channel_id=1, source_target_pairs={{1,2},{2,1},{3,4},{4,3},{5,6},{6,5},{7,0},{0,7},{9,10},{10,9},{11,... | collective-permute-start | bytes 98312 | tf_op jit(solution)/shard_map/ppermute | solution.py:510
  7.5 5.4 %collective-permute-start.2 = (bf16[272,256]{1,0:T(8,128)(2,1)S(1)}, bf16[272,256]{1,0:T(8,128)(2,1)S(1)}, u32[]{:S(2)}, u32[]{:S(2)}) collective-permute-start(bf16[272,256]{1,0:T(8,128)(2,1)S(1)} %get-tuple-element.82), channel_id=1, source_target_pairs={{0,8},{8,0},{16,24},{24,16},{1,9},{9,1},{17,25},{25,17},{2,10},{10... | collective-permute-start | bytes 417800 | tf_op jit(solution)/shard_map/ppermute | solution.py:526
  8.8 4.1 %collective-permute-start.3 = (bf16[272,256]{1,0:T(8,128)(2,1)S(1)}, bf16[272,256]{1,0:T(8,128)(2,1)S(1)}, u32[]{:S(2)}, u32[]{:S(2)}) collective-permute-start(bf16[272,256]{1,0:T(8,128)(2,1)S(1)} %get-tuple-element.83), channel_id=1, source_target_pairs={{8,16},{16,8},{9,17},{17,9},{10,18},{18,10},{11,19},{19,11},{12,20... | collective-permute-start | bytes 417800 | tf_op jit(solution)/shard_map/ppermute | solution.py:527
  16.5 6.0 %collective-permute-start.4 = (bf16[1152,256]{1,0:T(8,128)(2,1)S(1)}, bf16[1152,256]{1,0:T(8,128)(2,1)S(1)}, u32[]{:S(2)}, u32[]{:S(2)}) collective-permute-start(bf16[1152,256]{1,0:T(8,128)(2,1)S(1)} %get-tuple-element.97), channel_id=1, source_target_pairs={{0,1},{1,0},{2,3},{3,2},{4,5},{5,4},{6,7},{7,6},{8,9},{9,8},{10,11... | collective-permute-start | bytes 1769480 | tf_op jit(solution)/shard_map/ppermute | solution.py:407
  22.6 9.1 %collective-permute-start.7 = (bf16[576,256]{1,0:T(8,128)(2,1)S(1)}, bf16[576,256]{1,0:T(8,128)(2,1)S(1)}, u32[]{:S(2)}, u32[]{:S(2)}) collective-permute-start(bf16[576,256]{1,0:T(8,128)(2,1)S(1)} %get-tuple-element.100), channel_id=1, source_target_pairs={{0,8},{1,17},{2,10},{3,19},{4,12},{5,21},{6,14},{7,23},{8,0},{9,25... | collective-permute-start | bytes 884744 | tf_op jit(solution)/shard_map/ppermute | solution.py:407
  27.6 3.2 %collective-permute-start.5 = (bf16[96,256]{1,0:T(8,128)(2,1)S(1)}, bf16[96,256]{1,0:T(8,128)(2,1)S(1)}, u32[]{:S(2)}, u32[]{:S(2)}) collective-permute-start(bf16[96,256]{1,0:T(8,128)(2,1)S(1)} %get-tuple-element.101), channel_id=1, source_target_pairs={{0,1},{1,0},{2,3},{3,2},{4,5},{5,4},{6,7},{7,6},{8,9},{9,8},{10,11... | collective-permute-start | bytes 147464 | tf_op jit(solution)/shard_map/ppermute | solution.py:571
  27.6 3.6 %collective-permute-start.6 = (bf16[96,256]{1,0:T(8,128)(2,1)S(1)}, bf16[96,256]{1,0:T(8,128)(2,1)S(1)}, u32[]{:S(2)}, u32[]{:S(2)}) collective-permute-start(bf16[96,256]{1,0:T(8,128)(2,1)S(1)} %get-tuple-element.108), channel_id=1, source_target_pairs={{1,2},{2,1},{3,4},{4,3},{5,6},{6,5},{7,0},{0,7},{9,10},{10,9},{11,... | collective-permute-start | bytes 147464 | tf_op jit(solution)/shard_map/ppermute | solution.py:572
  31.7 4.3 %collective-permute-start.8 = (bf16[1152,256]{1,0:T(8,128)(2,1)S(1)}, bf16[1152,256]{1,0:T(8,128)(2,1)S(1)}, u32[]{:S(2)}, u32[]{:S(2)}) collective-permute-start(bf16[1152,256]{1,0:T(8,128)(2,1)S(1)} %get-tuple-element.114), channel_id=1, source_target_pairs={{0,1},{1,0},{2,3},{3,2},{4,5},{5,4},{6,7},{7,6},{8,9},{9,8},{10,11... | collective-permute-start | bytes 1769480 | tf_op jit(solution)/shard_map/ppermute | solution.py:407
  36.2 10.3 %collective-permute-start.10 = (bf16[576,256]{1,0:T(8,128)(2,1)S(1)}, bf16[576,256]{1,0:T(8,128)(2,1)S(1)}, u32[]{:S(2)}, u32[]{:S(2)}) collective-permute-start(bf16[576,256]{1,0:T(8,128)(2,1)S(1)} %get-tuple-element.118), channel_id=1, source_target_pairs={{0,8},{1,17},{2,10},{3,19},{4,12},{5,21},{6,14},{7,23},{8,0},{9,25... | collective-permute-start | bytes 884744 | tf_op jit(solution)/shard_map/ppermute | solution.py:407
  37.1 5.8 %collective-permute-start.9 = (bf16[288,256]{1,0:T(8,128)(2,1)S(1)}, bf16[288,256]{1,0:T(8,128)(2,1)S(1)}, u32[]{:S(2)}, u32[]{:S(2)}) collective-permute-start(bf16[288,256]{1,0:T(8,128)(2,1)S(1)} %get-tuple-element.113), channel_id=1, source_target_pairs={{0,16},{1,9},{2,18},{3,11},{4,20},{5,13},{6,22},{7,15},{8,24},{9,1... | collective-permute-start | bytes 442376 | tf_op jit(solution)/shard_map/ppermute | solution.py:407
  43.0 4.7 %collective-permute-start.12 = (bf16[144,256]{1,0:T(8,128)(2,1)S(1)}, bf16[144,256]{1,0:T(8,128)(2,1)S(1)}, u32[]{:S(2)}, u32[]{:S(2)}) collective-permute-start(bf16[144,256]{1,0:T(8,128)(2,1)S(1)} %get-tuple-element.121), channel_id=1, source_target_pairs={{0,2},{1,5},{2,0},{3,7},{4,6},{5,1},{6,4},{7,3},{8,10},{9,13},{10,... | collective-permute-start | bytes 221192 | tf_op jit(solution)/shard_map/ppermute | solution.py:407
  46.5 4.9 %collective-permute-start.11 = (bf16[288,256]{1,0:T(8,128)(2,1)S(1)}, bf16[288,256]{1,0:T(8,128)(2,1)S(1)}, u32[]{:S(2)}, u32[]{:S(2)}) collective-permute-start(bf16[288,256]{1,0:T(8,128)(2,1)S(1)} %get-tuple-element.126), channel_id=1, source_target_pairs={{0,16},{1,9},{2,18},{3,11},{4,20},{5,13},{6,22},{7,15},{8,24},{9,1... | collective-permute-start | bytes 442376 | tf_op jit(solution)/shard_map/ppermute | solution.py:407
  47.6 3.8 %collective-permute-start.13 = (bf16[144,256]{1,0:T(8,128)(2,1)S(1)}, bf16[144,256]{1,0:T(8,128)(2,1)S(1)}, u32[]{:S(2)}, u32[]{:S(2)}) collective-permute-start(bf16[144,256]{1,0:T(8,128)(2,1)S(1)} %sum_round.4.keep), channel_id=1, source_target_pairs={{0,4},{1,3},{2,6},{3,1},{4,0},{5,7},{6,2},{7,5},{8,12},{9,11},{10,... | collective-permute-start | bytes 221192 | tf_op jit(solution)/shard_map/ppermute | solution.py:407
  51.5 6.7 %collective-permute-start.16 = (bf16[144,256]{1,0:T(8,128)(2,1)S(1)}, bf16[144,256]{1,0:T(8,128)(2,1)S(1)}, u32[]{:S(2)}, u32[]{:S(2)}) collective-permute-start(bf16[144,256]{1,0:T(8,128)(2,1)S(1)} %sum_round.5.value), channel_id=1, source_target_pairs={{0,2},{1,5},{2,0},{3,7},{4,6},{5,1},{6,4},{7,3},{8,10},{9,13},{10,... | collective-permute-start | bytes 221192 | tf_op jit(solution)/shard_map/ppermute | solution.py:407
  53.0 5.2 %collective-permute-start.14 = (bf16[144,256]{1,0:T(8,128)(2,1)S(1)}, bf16[144,256]{1,0:T(8,128)(2,1)S(1)}, u32[]{:S(2)}, u32[]{:S(2)}) collective-permute-start(bf16[144,256]{1,0:T(8,128)(2,1)S(1)} %get-tuple-element.132), channel_id=1, source_target_pairs={{0,2},{1,5},{2,0},{3,7},{4,6},{5,1},{6,4},{7,3},{8,10},{9,13},{10,... | collective-permute-start | bytes 221192 | tf_op jit(solution)/shard_map/ppermute | solution.py:407
  58.2 4.3 %collective-permute-start.18 = (bf16[288,256]{1,0:T(8,128)(2,1)S(1)}, bf16[288,256]{1,0:T(8,128)(2,1)S(1)}, u32[]{:S(2)}, u32[]{:S(2)}) collective-permute-start(bf16[288,256]{1,0:T(8,128)(2,1)S(1)} %join.6.value), channel_id=1, source_target_pairs={{0,16},{1,9},{2,18},{3,11},{4,20},{5,13},{6,22},{7,15},{8,24},{9,1... | collective-permute-start | bytes 442376 | tf_op jit(solution)/shard_map/ppermute | solution.py:407
  59.3 3.2 %collective-permute-start.15 = (bf16[144,256]{1,0:T(8,128)(2,1)S(1)}, bf16[144,256]{1,0:T(8,128)(2,1)S(1)}, u32[]{:S(2)}, u32[]{:S(2)}) collective-permute-start(bf16[144,256]{1,0:T(8,128)(2,1)S(1)} %sum_round.6.keep), channel_id=1, source_target_pairs={{0,4},{1,3},{2,6},{3,1},{4,0},{5,7},{6,2},{7,5},{8,12},{9,11},{10,... | collective-permute-start | bytes 221192 | tf_op jit(solution)/shard_map/ppermute | solution.py:407
  62.6 5.6 %collective-permute-start.20 = (bf16[576,256]{1,0:T(8,128)(2,1)S(1)}, bf16[576,256]{1,0:T(8,128)(2,1)S(1)}, u32[]{:S(2)}, u32[]{:S(2)}) collective-permute-start(bf16[576,256]{1,0:T(8,128)(2,1)S(1)} %join.7.value), channel_id=1, source_target_pairs={{0,8},{1,17},{2,10},{3,19},{4,12},{5,21},{6,14},{7,23},{8,0},{9,25... | collective-permute-start | bytes 884744 | tf_op jit(solution)/shard_map/ppermute | solution.py:407
  62.9 5.4 %collective-permute-start.17 = (bf16[144,256]{1,0:T(8,128)(2,1)S(1)}, bf16[144,256]{1,0:T(8,128)(2,1)S(1)}, u32[]{:S(2)}, u32[]{:S(2)}) collective-permute-start(bf16[144,256]{1,0:T(8,128)(2,1)S(1)} %sum_round.7.value), channel_id=1, source_target_pairs={{0,2},{1,5},{2,0},{3,7},{4,6},{5,1},{6,4},{7,3},{8,10},{9,13},{10,... | collective-permute-start | bytes 221192 | tf_op jit(solution)/shard_map/ppermute | solution.py:407
  68.3 12.7 %collective-permute-start.22 = (bf16[1152,256]{1,0:T(8,128)(2,1)S(1)}, bf16[1152,256]{1,0:T(8,128)(2,1)S(1)}, u32[]{:S(2)}, u32[]{:S(2)}) collective-permute-start(bf16[1152,256]{1,0:T(8,128)(2,1)S(1)} %join.9.value), channel_id=1, source_target_pairs={{0,1},{1,0},{2,3},{3,2},{4,5},{5,4},{6,7},{7,6},{8,9},{9,8},{10,11... | collective-permute-start | bytes 1769480 | tf_op jit(solution)/shard_map/ppermute | solution.py:407
  75.4 4.3 %collective-permute-start.19 = (bf16[288,256]{1,0:T(8,128)(2,1)S(1)}, bf16[288,256]{1,0:T(8,128)(2,1)S(1)}, u32[]{:S(2)}, u32[]{:S(2)}) collective-permute-start(bf16[288,256]{1,0:T(8,128)(2,1)S(1)} %join.8.value), channel_id=1, source_target_pairs={{0,16},{1,9},{2,18},{3,11},{4,20},{5,13},{6,22},{7,15},{8,24},{9,1... | collective-permute-start | bytes 442376 | tf_op jit(solution)/shard_map/ppermute | solution.py:407
  79.7 5.9 %collective-permute-start.21 = (bf16[576,256]{1,0:T(8,128)(2,1)S(1)}, bf16[576,256]{1,0:T(8,128)(2,1)S(1)}, u32[]{:S(2)}, u32[]{:S(2)}) collective-permute-start(bf16[576,256]{1,0:T(8,128)(2,1)S(1)} %join.10.value), channel_id=1, source_target_pairs={{0,8},{1,17},{2,10},{3,19},{4,12},{5,21},{6,14},{7,23},{8,0},{9,25... | collective-permute-start | bytes 884744 | tf_op jit(solution)/shard_map/ppermute | solution.py:407
  85.7 3.5 %collective-permute-start.23 = (bf16[1152,256]{1,0:T(8,128)(2,1)S(1)}, bf16[1152,256]{1,0:T(8,128)(2,1)S(1)}, u32[]{:S(2)}, u32[]{:S(2)}) collective-permute-start(bf16[1152,256]{1,0:T(8,128)(2,1)S(1)} %join.11.value), channel_id=1, source_target_pairs={{0,1},{1,0},{2,3},{3,2},{4,5},{5,4},{6,7},{7,6},{8,9},{9,8},{10,11... | collective-permute-start | bytes 1769480 | tf_op jit(solution)/shard_map/ppermute | solution.py:407
where the time goes:
time: 90.9 us; the launch traced here: 90.4 us
  Pallas kernels  33.1 us (36%)
  starting transfers between devices  31.4 us (35%)
  waiting for transfers between devices  24.8 us (27%)
  between operations  1.1 us (1%)
    pallas_call x31, Pallas kernels, kernel_call(): pl.pallas_call(body, out_shape=out_shape, in_specs=in_specs, out_specs=ou...  33.1 us
    ppermute x18, starting transfers between devices, swapped(): return lax.ppermute(value, BOTH, pairs)  26.7 us
    ppermute x18, waiting for transfers between devices, swapped(): return lax.ppermute(value, BOTH, pairs)  24.4 us
    ppermute x1, starting transfers between devices, shards(): lon_far = lax.ppermute(far, 'lon', far_lon)  2.71 us
  transfers between devices with their start and end apart: 24, of which 10 were waited for; matrix products, arithmetic and copies ran while one was open for 0% of the time, Pallas kernels for 29%

commit v1 on v0

--- a/solution.py
+++ b/solution.py
@@ -328,39 +328,49 @@
         copy.wait()
 
 
-def step_bit(step):
-    lat_count, lon_count = lax.axis_size("lat"), lax.axis_size("lon")
-    even, odd, _ = swap_plan(lat_count, lon_count)
-    me = lax.axis_index("lat") * lon_count + lax.axis_index("lon")
-    return jnp.where(me % 2 == 1, (me >> odd[step]) & 1, (me >> even[step]) & 1)
-
-
-def halves(bit, half):
-    mine = pl.ds(aligned(bit * half, 16), half)
-    other = pl.ds(aligned((1 - bit) * half, 16), half)
-    return mine, other
-
-
-def add_split_kernel(step, keep, got, out, send):
-    mine, other = halves(step_bit(step), out.shape[0])
-    out[...] = keep[mine, :] + got[mine, :].astype(F32)
-    send[...] = (keep[other, :] + got[other, :].astype(F32)).astype(BF16)
-
-
-def add_round_kernel(keep, got, out):
-    out[...] = (keep[...].astype(F32) + got[...].astype(F32)).astype(BF16)
-
-
-def join_kernel(step, value, got, out):
-    mine, other = halves(step_bit(step), value.shape[0])
-    out[mine, :] = value[...]
-    out[other, :] = got[...]
+def place():
+    return lax.axis_index("lat"), lax.axis_index("lon") % 2
+
+
+def partner(n):
+    lat, odd = place()
+    even_mask, odd_mask = group_masks(lax.axis_size("lat"))[n]
+    return lat ^ jnp.where(odd == 1, odd_mask, even_mask)
+
+
+def chunk(index, rows):
+    return pl.ds(aligned(index * rows, 16), rows)
+
+
+def spread_kernel(keep, got, own, *sends):
+    rows = own.shape[0]
+    at = chunk(place()[0], rows)
+    own[...] = keep[at, :] + got[at, :].astype(F32)
+    for n, send in enumerate(sends):
+        at = chunk(partner(n), rows)
+        send[...] = (keep[at, :] + got[at, :].astype(F32)).astype(BF16)
+
+
+def add_round_kernel(own, *rest):
+    out = rest[-1]
+    total = own[...].astype(F32)
+    for got in rest[:-1]:
+        total = total + got[...].astype(F32)
+    out[...] = total.astype(BF16)
+
+
+def join_kernel(value, *rest):
+    out = rest[-1]
+    rows = value.shape[0]
+    out[chunk(place()[0], rows), :] = value[...]
+    for n, got in enumerate(rest[:-1]):
+        out[chunk(partner(n), rows), :] = got[...]
 
 
 def final_kernel(factor, own, value, *rest):
     out, scaled, sems = rest[-3:]
     half, chunks = value.shape[0], sems.shape[0]
-    bit = step_bit(0)
+    bit = place()[1]
     base = (bit if own else 1 - bit) * half
     copies = []
     for n in range(chunks):
@@ -390,103 +400,118 @@
     return count.bit_length() - 1
 
 
-def swap_plan(lat_count, lon_count):
-    lon_bits = log2(lon_count)
-    lat = list(range(lon_bits, lon_bits + log2(lat_count)))
-    lon = list(range(1, lon_bits))
-    even = [0] + lat + lon
-    odd = [0] + lat[::-1] + lon[::-1]
-    pairs = [
-        [(d, d ^ (1 << (o if d & 1 else e))) for d in range(lat_count * lon_count)]
-        for e, o in zip(even, odd)
-    ]
-    return even, odd, pairs
-
-
-def swapped(value, pairs):
-    return lax.ppermute(value, BOTH, pairs)
-
-
-def after(value, *others):
-    return lax.optimization_barrier((value, *others))[0]
+def reversed_bits(value, width):
+    return int(format(value, f"0{width}b")[::-1], 2)
+
+
+def group_masks(count):
+    return [(k, reversed_bits(k, log2(count))) for k in range(1, count)]
+
+
+def flat_pairs(lat_count, lon_count, move):
+    pairs = []
+    for lat in range(lat_count):
+        for lon in range(lon_count):
+            to_lat, to_lon = move(lat, lon)
+            pairs.append((lat * lon_count + lon, to_lat * lon_count + to_lon))
+    return pairs
+
+
+def after(values, *others):
+    return list(lax.optimization_barrier((*values, *others)))[: len(values)]
 
 
 class Summed:
-    def __init__(self, keep, send, pairs, factor):
-        self.keep, self.send, self.pairs, self.factor = keep, send, pairs, factor
-        self.count, self.step, self.value = len(pairs), 0, None
-        self.bits = [step_bit(step) for step in range(self.count)]
-
-    @property
-    def sent(self):
-        return self.send if self.step < self.count - 1 else self.value
+    def __init__(self, keep, send, factor):
+        lat_count, lon_count = lax.axis_size("lat"), lax.axis_size("lon")
+        self.keep, self.sent, self.factor, self.result = keep, [send], factor, None
+        core = flat_pairs(lat_count, lon_count, lambda lat, lon: (lat, lon ^ 1))
+        group = [
+            flat_pairs(
+                lat_count, lon_count, lambda lat, lon, m=m: (lat ^ (m[1] if lon & 1 else m[0]), lon)
+            )
+            for m in group_masks(lat_count)
+        ]
+        width = log2(lon_count) - 1
+        line = [
+            flat_pairs(
+                lat_count,
+                lon_count,
+                lambda lat, lon, n=n: (lat, lon ^ (2 << (width - 1 - n if lon & 1 else n))),
+            )
+            for n in range(width)
+        ]
+        self.steps = [("core", [core]), ("lat", group)]
+        self.steps += [("lon", [pairs]) for pairs in line]
+        self.steps += [("join", group), ("last", [core])]
 
     def start(self):
-        step, last = self.step, self.count - 1
-        if self.running:
-            self.got = swapped(self.sent, self.pairs[step if step <= last else 2 * last - step])
-
-    def finish(self, *others):
-        got = after(self.got, *others) if others else self.got
-        keep, count, step = self.keep, self.count, self.step
-        chans = keep.shape[1]
-        self.step += 1
-        if step < count - 2:
-            half = keep.shape[0] // 2
-            if half % 16:
-                value = keep + got.astype(F32)
-                bit = self.bits[step + 1]
-                self.keep = lax.dynamic_slice_in_dim(value, bit * half, half)
-                send = lax.dynamic_slice_in_dim(value, (1 - bit) * half, half)
-                self.send = send.astype(BF16)
-            else:
-                body = functools.partial(add_split_kernel, step + 1)
-                outs = [((half, chans), F32), ((half, chans), BF16)]
-                self.keep, self.send = kernel_call(body, "sum_step", outs, [keep, got], limit=16)
-        elif step < count:
-            mine = keep if step == count - 2 else self.value
-            outs = [(keep.shape, BF16)]
-            (self.value,) = kernel_call(add_round_kernel, "sum_round", outs, [mine, got], limit=16)
+        kind, pairs = self.steps[0]
+        sent = self.sent if kind == "lat" else self.sent * len(pairs)
+        self.got = [lax.ppermute(x, BOTH, p) for x, p in zip(sent, pairs)]
+
+    def finish(self):
+        kind = self.steps.pop(0)[0]
+        got, (rows, chans) = self.got, self.keep.shape
+        if kind == "core":
+            count = lax.axis_size("lat")
+            piece = rows // count
+            assert piece % 16 == 0
+            outs = [((piece, chans), F32)] + [((piece, chans), BF16)] * (count - 1)
+            self.keep, *self.sent = kernel_call(
+                spread_kernel, "spread", outs, [self.keep, *got], limit=16
+            )
+        elif kind == "join":
+            outs = [((rows * lax.axis_size("lat"), chans), BF16)]
+            self.sent = kernel_call(join_kernel, "join", outs, [*self.sent, *got], limit=16)
+        elif kind == "last":
+            if self.result is None:
+                self.scale(self.sent[0], True)
+            self.sent = [self.scale(got[0], False)]
         else:
-            back = 2 * count - 2 - step
-            value = self.value
-            half = value.shape[0]
-            if back == 0:
-                out = ((2 * half, chans), F32, "hbm")
-                scratch = [pltpu.VMEM((half, chans), F32), pltpu.SemaphoreType.DMA((4,))]
-                result = None
-                for own in (True, False):
-                    body = functools.partial(final_kernel, self.factor, own)
-                    x, extra = (value, []) if own else (after(got, result), [0])
-                    (result,) = kernel_call(
-                        body,
-                        "scaled",
-                        [out],
-                        [x] + [in_hbm(result) for _ in extra],
-                        scratch=scratch,
-                        aliases={1: 0} if extra else None,
-                        limit=16,
-                    )
-                self.value = result
-            elif half % 16:
-                low = jnp.where(self.bits[back] == 1, got, value)
-                high = jnp.where(self.bits[back] == 1, value, got)
-                self.value = jnp.concatenate([low, high])
-            else:
-                body = functools.partial(join_kernel, back)
-                outs = [((2 * half, chans), BF16)]
-                (self.value,) = kernel_call(body, "join", outs, [value, got], limit=16)
-
-    @property
-    def running(self):
-        return self.step < 2 * self.count - 1
+            mine = self.keep if kind == "lat" else self.sent[0]
+            outs = [((rows, chans), BF16)]
+            self.sent = kernel_call(add_round_kernel, "add", outs, [mine, *got], limit=16)
+
+    def scale(self, value, own):
+        rows, chans = value.shape
+        ins = [value] if own else [value, in_hbm(self.result)]
+        (self.result,) = kernel_call(
+            functools.partial(final_kernel, self.factor, own),
+            "scaled",
+            [((2 * rows, chans), F32, "hbm")],
+            ins,
+            scratch=[pltpu.VMEM((rows, chans), F32), pltpu.SemaphoreType.DMA((4,))],
+            aliases=None if own else {1: 0},
+            limit=16,
+        )
+        return self.result
+
+
+class Turns:
+    def __init__(self):
+        self.last = []
+
+    def run(self, work):
+        result = work(self.last)
+        self.last = list(result)
+        return result
+
+    def start(self, chain):
+        chain.sent = after(chain.sent, *self.last)
+        self.last = list(chain.sent)
+        chain.start()
+
+    def finish(self, chain):
+        chain.got = after(chain.got, *self.last)
+        chain.finish()
+        self.last = list(chain.sent)
 
 
 def shards(field_in, kernel_one, kernel_two, cotangent):
     rows, cols, chans = field_in.shape
     cells, tall = rows * cols, (rows + 2) * cols
     lat_count, lon_count = lax.axis_size("lat"), lax.axis_size("lon")
-    _, _, pairs = swap_plan(lat_count, lon_count)
     factor = float(rows * lat_count * cols * lon_count) ** (-0.5)
     flops = 2 * cells * 9 * chans * chans
     sems = pltpu.SemaphoreType.DMA((2,))
@@ -521,7 +546,7 @@
 
     strip = ((4 * cols + 16, chans), BF16)
     send_near, send_far = call(
-        edge_kernel, "edges", [strip, strip], [field, cot, after(lon_near, act3), lon_far]
+        edge_kernel, "edges", [strip, strip], [field, cot, *after([lon_near, lon_far], act3)]
     )
     lat_near = lax.ppermute(send_near, "lat", near_lat)
     lat_far = lax.ppermute(send_far, "lat", far_lat)
@@ -533,7 +558,7 @@
         inner_kernel,
         "inner_rows",
         [wide, wide, high, flat, turned],
-        [lon_near, lon_far, cot, k_one, after(act3, send_near, send_far)],
+        [lon_near, lon_far, cot, k_one, *after([act3], send_near, send_far)],
         flops=flops,
         scratch=[pltpu.VMEM((4 * rows, chans), F32)],
         aliases={4: 0},
@@ -551,52 +576,60 @@
         scratch=[part, term],
         aliases={3: 0, 4: 1, 5: 2, 6: 3, 7: 4},
     )
-    two = Summed(keep, send, pairs, factor)
-    two.start()
+    turns = Turns()
+    two = Summed(keep, send, factor)
+    turns.start(two)
 
     lanes = -(-(rows + 2) // 16) * 16
     sides = ((2 * lanes, chans), BF16)
-    ghid, ghid_t, side_near, side_far = call(
-        back_kernel,
-        "grad_hid",
-        [flat, turned, sides, sides],
-        [lat_near, lat_far, t_two, cot3, hid, mid],
-        flops=flops,
-        scratch=[part, pltpu.VMEM((4 * lanes, chans), F32)],
-    )
-    two.finish(ghid)
-
-    side_near, side_far = after(side_near, two.sent), after(side_far, two.sent)
-    two.start()
-    side_near = lax.ppermute(side_near, "lon", near_lon)
-    side_far = lax.ppermute(side_far, "lon", far_lon)
-    keep, send = call(
-        grad_one_kernel,
-        "grad_one",
-        parts,
-        [after(ghid_t, two.sent), act3],
-        flops=flops,
-        scratch=[term],
-    )
-    side_near, side_far = after(side_near, keep), after(side_far, keep)
-    two.finish(keep)
-    one = Summed(keep, after(send, two.sent, side_near, side_far), pairs, factor)
-    one.start()
-    two.start()
+
+    def grad_hid_part(waits):
+        return call(
+            back_kernel,
+            "grad_hid",
+            [flat, turned, sides, sides],
+            [*after([lat_near], *waits), lat_far, t_two, cot3, hid, mid],
+            flops=flops,
+            scratch=[part, pltpu.VMEM((4 * lanes, chans), F32)],
+        )
+
+    def grad_one_part(waits):
+        return call(
+            grad_one_kernel,
+            "grad_one",
+            parts,
+            [*after([ghid_t], *waits), act3],
+            flops=flops,
+            scratch=[term],
+        )
+
+    ghid, ghid_t, side_near, side_far = turns.run(grad_hid_part)
+    keep, send = turns.run(grad_one_part)
+    one = Summed(keep, send, factor)
+    turns.start(one)
+    turns.finish(two)
+    turns.start(two)
+    side_near, side_far = after([side_near, side_far], *turns.last)
+    got_near = lax.ppermute(side_near, "lon", near_lon)
+    got_far = lax.ppermute(side_far, "lon", far_lon)
+    turns.finish(one)
+    turns.start(one)
+    got_near, got_far = after([got_near, got_far], *turns.last)
+    turns.last = [got_near, got_far]
+    turns.finish(two)
+    turns.start(two)
 
     results = [None, None]
-    pieces = [(0, 0), (0, 1), (1, 0), (1, 1)]
-
-    def piece(which, part, *others):
+
+    def piece(which, half, waits):
         count = rows // 2
-        old = results[which]
-        ins = [side_near, side_far, after((mid, ghid)[which], *others)]
+        ins = [got_near, got_far, *after([(mid, ghid)[which]], *waits)]
         ins += [(k_two, t_one)[which], field, cot]
         (results[which],) = call(
-            functools.partial(last_kernel, bool(which), part * count, count),
+            functools.partial(last_kernel, bool(which), half * count, count),
             ("field_out", "grad_in")[which],
             [((cells, chans), BF16, "hbm")],
-            ins + ([in_hbm(old)] if part else []),
+            ins + ([in_hbm(results[which])] if half else []),
             flops=flops // 2,
             scratch=[
                 pltpu.VMEM((2 * lanes, chans), F32),
@@ -604,28 +637,32 @@
                 pltpu.VMEM((count * cols, chans), BF16),
                 sems,
             ],
-            aliases={len(ins): 0} if part else None,
+            aliases={len(ins): 0} if half else None,
         )
-        return results[which]
-
-    for which, half in pieces:
-        fill = piece(which, half, one.sent, two.sent)
-        one.finish(fill)
-        two.finish(fill, one.sent)
-        one.start()
-        two.start()
-    while one.running:
-        one.finish(two.sent)
-        one.start()
-        if two.running:
-            two.finish(one.sent)
-            two.start()
+        return [results[which]]
+
+    def scaling(chain):
+        return lambda waits: [chain.scale(*after(chain.sent, *waits), True)]
+
+    work = [functools.partial(piece, which, half) for which in (0, 1) for half in (0, 1)]
+    while one.steps:
+        if work:
+            turns.run(work.pop(0))
+        for chain in (one, two):
+            if chain.steps:
+                turns.finish(chain)
+                if chain.steps:
+                    turns.start(chain)
+                if chain.steps and chain.steps[0][0] == "last":
+                    turns.run(scaling(chain))
+    while work:
+        turns.run(work.pop(0))
     shape = (3, 3, chans, chans)
     return (
         results[0].reshape(rows, cols, chans),
         results[1].reshape(rows, cols, chans),
-        one.value.reshape(shape),
-        two.value.reshape(shape),
+        one.result.reshape(shape),
+        two.result.reshape(shape),
     )
 
 

time: 90.9 us -> 75 us (0.83)
  waiting for transfers between devices: 24.8 us -> 5.97 us
  starting transfers between devices: 31.4 us -> 34.8 us
    ppermute x20 -> x22, waiting for transfers between devices: 24.8 us -> 5.96 us  [the longest x20 4.3 us: start(): self.got = [lax.ppermute(x, BOTH, p) for x, p in zip(sent, pairs)]]
    ppermute x20 -> x22, starting transfers between devices: 26.7 us -> 30 us  [the longest x20 29.1 us: start(): self.got = [lax.ppermute(x, BOTH, p) for x, p in zip(sent, pairs)]]
    pallas_call x31 -> x25, Pallas kernels: 33.1 us -> 32.9 us  [kernel_call(): pl.pallas_call(body, out_shape=out_shape, in_specs=in_specs, out_specs=ou...]
  transfers between devices with their start and end apart: 24 -> 26, of which waited for: 10 -> 6; matrix products, arithmetic and copies ran while one was open for 0% -> 0% of each run, Pallas kernels for 29% -> 36%
where the time goes in v1:
time: 75 us; the launch traced here: 74.8 us
  starting transfers between devices  34.8 us (46%)
  Pallas kernels  32.9 us (44%)
  waiting for transfers between devices  5.97 us (8%)
  between operations  1.08 us (1%)
    pallas_call x25, Pallas kernels, kernel_call(): pl.pallas_call(body, out_shape=out_shape, in_specs=in_specs, out_specs=ou...  32.9 us
    ppermute x20, starting transfers between devices, start(): self.got = [lax.ppermute(x, BOTH, p) for x, p in zip(sent, pairs)]  29.1 us
    ppermute x20, waiting for transfers between devices, start(): self.got = [lax.ppermute(x, BOTH, p) for x, p in zip(sent, pairs)]  4.3 us
    ppermute x1, starting transfers between devices, shards(): lon_far = lax.ppermute(far, 'lon', far_lon)  2.71 us
  transfers between devices with their start and end apart: 26, of which 6 were waited for; matrix products, arithmetic and copies ran while one was open for 0% of the time, Pallas kernels for 36%

profile of v1, /device:TPU:1, one launch (start us, length us, event | category | flops | bytes accessed | tf_op | source)
XLA Modules:
  0.0 74.8 jit_solution(15277954174066635106)
XLA Ops:
  0.6 1.7 %ends.1 = (bf16[2048,256]{1,0:T(8,128)(2,1)S(1)}, bf16[2048,256]{1,0:T(8,128)(2,1)S(1)}, bf16[64,256]{1,0:T(8,128)(2,1)S(1)}, bf16[64,256]{1,0:T(8,128)(2,1)S(1)}) custom-call(bf16[2048,256]{1,0:T(8,128)(2,1)} %bitcast.12, bf16[2048,256]{1,0:T(8,128)(2,1)} %bitcast.13), custom_call_target="tpu_custom_call" | custom-call | bytes 2097152 | tf_op jit(solution)/shard_map/ends/pallas_call | solution.py:24
  2.4 2.7 %collective-permute-start.1 = (bf16[64,256]{1,0:T(8,128)(2,1)S(1)}, bf16[64,256]{1,0:T(8,128)(2,1)S(1)}, u32[]{:S(2)}, u32[]{:S(2)}) collective-permute-start(bf16[64,256]{1,0:T(8,128)(2,1)S(1)} %get-tuple-element.85), channel_id=1, source_target_pairs={{1,2},{2,1},{3,4},{4,3},{5,6},{6,5},{7,0},{0,7},{9,10},{10,9},{11,... | collective-permute-start | bytes 98312 | tf_op jit(solution)/shard_map/ppermute | solution.py:535
  5.1 2.3 %prep.1 = (bf16[2176,768]{1,0:T(8,128)(2,1)S(1)}, bf16[2304,256]{1,0:T(8,128)(2,1)S(1)}, bf16[2304,256]{1,0:T(8,128)(2,1)S(1)}, bf16[2304,256]{1,0:T(8,128)(2,1)S(1)}, bf16[2304,256]{1,0:T(8,128)(2,1)S(1)}) custom-call(bf16[2048,256]{1,0:T(8,128)(2,1)S(1)} %get-tuple-element.82.field, bf16[2304,256]{1,0:T(8,128)(2,1)} %bitcast.14, bf16[2304,256]{1,0:T(8,128)(2,1)} %bitcast.15), custom_call_target="tpu_custom_call" | custom-call | flops 2415919104 | bytes 3407872 | tf_op jit(solution)/shard_map/prep/pallas_call | solution.py:24
  7.5 1.3 %collective-permute-start.2 = (bf16[272,256]{1,0:T(8,128)(2,1)S(1)}, bf16[272,256]{1,0:T(8,128)(2,1)S(1)}, u32[]{:S(2)}, u32[]{:S(2)}) collective-permute-start(bf16[272,256]{1,0:T(8,128)(2,1)S(1)} %get-tuple-element.89), channel_id=1, source_target_pairs={{0,8},{8,0},{16,24},{24,16},{1,9},{9,1},{17,25},{25,17},{2,10},{10... | collective-permute-start | bytes 417800 | tf_op jit(solution)/shard_map/ppermute | solution.py:551
  9.4 3.5 %inner_rows.1 = (bf16[2176,768]{1,0:T(8,128)(2,1)S(1)}, bf16[2176,768]{1,0:T(8,128)(2,1)S(1)}, f32[2176,256]{1,0:T(8,128)S(1)}, bf16[2176,256]{1,0:T(8,128)(2,1)S(1)}, bf16[256,2048]{1,0:T(8,128)(2,1)S(1)}) custom-call(bf16[64,256]{1,0:T(8,128)(2,1)S(1)} %collective-permute-done.near, ...), custom_call_target="tpu_custom_call", output_to_operand_aliasing={{0}: (4, {})} | custom-call | flops 2415919104 | bytes 5636096 | tf_op jit(solution)/shard_map/inner_rows/pallas_call | solution.py:24
  12.9 3.5 %grad_two.1 = (bf16[2176,768]{1,0:T(8,128)(2,1)S(1)}, bf16[2176,768]{1,0:T(8,128)(2,1)S(1)}, f32[2176,256]{1,0:T(8,128)S(1)}, bf16[2176,256]{1,0:T(8,128)(2,1)S(...) custom-call(bf16[272,256]{1,0:T(8,128)(2,1)S(1)} %collective-permute, ...), custom_call_target="tpu_custom_call", output_to_operand_aliasing={{0}: (3, {}), {1}: (4, {}), {2}: (5, {}), {3}: (6, {}), {4}... | custom-call | flops 2415919104 | bytes 12533760 | tf_op jit(solution)/shard_map/grad_two/pallas_call | solution.py:24
  16.5 2.8 %collective-permute-start.4 = (bf16[1152,256]{1,0:T(8,128)(2,1)S(1)}, bf16[1152,256]{1,0:T(8,128)(2,1)S(1)}, u32[]{:S(2)}, u32[]{:S(2)}) collective-permute-start(bf16[1152,256]{1,0:T(8,128)(2,1)S(1)} %get-tuple-element.98), channel_id=1, source_target_pairs={{0,1},{1,0},{2,3},{3,2},{4,5},{5,4},{6,7},{7,6},{8,9},{9,8},{10,11... | collective-permute-start | bytes 1769480 | tf_op jit(solution)/shard_map/ppermute | solution.py:451
  19.3 3.1 %grad_hid.1 = (bf16[2176,256]{1,0:T(8,128)(2,1)S(1)}, bf16[256,2048]{1,0:T(8,128)(2,1)S(1)}, bf16[96,256]{1,0:T(8,128)(2,1)S(1)}, bf16[96,256]{1,0:T(8,128)(2,1)S(1)}) custom-call(bf16[272,256]{1,0:T(8,128)(2,1)S(1)} %collective-permute-done.2.near, bf16[272,256]{1,0:T(8,128)(2,1)S(1)} %collective-permute-done.3.far, ...), custom_call_target="tpu_custom_call" | custom-call | flops 2415919104 | bytes 8142848 | tf_op jit(solution)/shard_map/grad_hid/pallas_call | solution.py:24
  22.4 3.2 %grad_one.1 = (f32[1152,256]{1,0:T(8,128)S(1)}, bf16[1152,256]{1,0:T(8,128)(2,1)S(1)}) custom-call(bf16[256,2048]{1,0:T(8,128)(2,1)S(1)} %get-tuple-element.109.turned, bf16[2176,768]{1,0:T(8,128)(2,1)S(1)} %get-tuple-element.110.act3), custom_call_target="tpu_custom_call" | custom-call | flops 2415919104 | bytes 4390912 | tf_op jit(solution)/shard_map/grad_one/pallas_call | solution.py:24
  25.9 5.0 %collective-permute-start.8 = (bf16[288,256]{1,0:T(8,128)(2,1)S(1)}, bf16[288,256]{1,0:T(8,128)(2,1)S(1)}, u32[]{:S(2)}, u32[]{:S(2)}) collective-permute-start(bf16[288,256]{1,0:T(8,128)(2,1)S(1)} %get-tuple-element.118), channel_id=1, source_target_pairs={{0,8},{1,17},{2,10},{3,19},{4,12},{5,21},{6,14},{7,23},{8,0},{9,25... | collective-permute-start | bytes 442376 | tf_op jit(solution)/shard_map/ppermute | solution.py:451
  30.9 1.3 %collective-permute-start.10 = (bf16[288,256]{1,0:T(8,128)(2,1)S(1)}, bf16[288,256]{1,0:T(8,128)(2,1)S(1)}, u32[]{:S(2)}, u32[]{:S(2)}) collective-permute-start(bf16[288,256]{1,0:T(8,128)(2,1)S(1)} %get-tuple-element.120), channel_id=1, source_target_pairs={{0,24},{1,25},{2,26},{3,27},{4,28},{5,29},{6,30},{7,31},{8,16},{9,... | collective-permute-start | bytes 442376 | tf_op jit(solution)/shard_map/ppermute | solution.py:451
  34.0 1.7 %collective-permute-start.12 = (bf16[288,256]{1,0:T(8,128)(2,1)S(1)}, bf16[288,256]{1,0:T(8,128)(2,1)S(1)}, u32[]{:S(2)}, u32[]{:S(2)}) collective-permute-start(bf16[288,256]{1,0:T(8,128)(2,1)S(1)} %get-tuple-element.127), channel_id=1, source_target_pairs={{0,8},{1,17},{2,10},{3,19},{4,12},{5,21},{6,14},{7,23},{8,0},{9,25... | collective-permute-start | bytes 442376 | tf_op jit(solution)/shard_map/ppermute | solution.py:451
  37.7 2.2 %collective-permute-start.14 = (bf16[288,256]{1,0:T(8,128)(2,1)S(1)}, bf16[288,256]{1,0:T(8,128)(2,1)S(1)}, u32[]{:S(2)}, u32[]{:S(2)}) collective-permute-start(bf16[288,256]{1,0:T(8,128)(2,1)S(1)} %get-tuple-element.129), channel_id=1, source_target_pairs={{0,24},{1,25},{2,26},{3,27},{4,28},{5,29},{6,30},{7,31},{8,16},{9,... | collective-permute-start | bytes 442376 | tf_op jit(solution)/shard_map/ppermute | solution.py:451
  40.6 2.7 %field_out.2.rest_0_ = bf16[2048,256]{1,0:T(8,128)(2,1)} custom-call(bf16[96,256]{1,0:T(8,128)(2,1)S(1)} %collective-permute-done.5.near, bf16[96,256]{1,0:T(8,128)(2,1)S(1)} %collective-permute-done.6.far, bf16[2176,256]{1,0:T(8,128)(2,1)S(1)} %get-tuple-element.143.mid.value, bf16[2304,256]{1,0:T(8,128)(2,1)S(1)} %get-tuple-element.138.weights, ...), custom_call_target="tpu_custom_call" | custom-call | flops 1207959552 | bytes 4489216 | tf_op jit(solution)/shard_map/field_out/pallas_call | solution.py:24
  44.4 2.3 %collective-permute-start.16 = (bf16[288,256]{1,0:T(8,128)(2,1)S(1)}, bf16[288,256]{1,0:T(8,128)(2,1)S(1)}, u32[]{:S(2)}, u32[]{:S(2)}) collective-permute-start(bf16[288,256]{1,0:T(8,128)(2,1)S(1)} %add.7.own), channel_id=1, source_target_pairs={{0,2},{1,5},{2,0},{3,7},{4,6},{5,1},{6,4},{7,3},{8,10},{9,13},{10,... | collective-permute-start | bytes 442376 | tf_op jit(solution)/shard_map/ppermute | solution.py:451
  46.7 2.3 %collective-permute-start.15 = (bf16[288,256]{1,0:T(8,128)(2,1)S(1)}, bf16[288,256]{1,0:T(8,128)(2,1)S(1)}, u32[]{:S(2)}, u32[]{:S(2)}) collective-permute-start(bf16[288,256]{1,0:T(8,128)(2,1)S(1)} %add.8.own), channel_id=1, source_target_pairs={{0,4},{1,3},{2,6},{3,1},{4,0},{5,7},{6,2},{7,5},{8,12},{9,11},{10,... | collective-permute-start | bytes 442376 | tf_op jit(solution)/shard_map/ppermute | solution.py:451
  49.0 2.5 %field_out.3 = bf16[2048,256]{1,0:T(8,128)(2,1)} custom-call(bf16[96,256]{1,0:T(8,128)(2,1)S(1)} %collective-permute-done.5.near, bf16[96,256]{1,0:T(8,128)(2,1)S(1)} %collective-permute-done.6.far, bf16[2176,256]{1,0:T(8,128)(2,1)S(1)} %get-tuple-element.143.mid.value, ...), custom_call_target="tpu_custom_call", output_to_operand_aliasing={{}: (6, {})} | custom-call | flops 1207959552 | bytes 5537792 | tf_op jit(solution)/shard_map/field_out/pallas_call | solution.py:24
  51.6 2.4 %collective-permute-start.20 = (bf16[288,256]{1,0:T(8,128)(2,1)S(1)}, bf16[288,256]{1,0:T(8,128)(2,1)S(1)}, u32[]{:S(2)}, u32[]{:S(2)}) collective-permute-start(bf16[288,256]{1,0:T(8,128)(2,1)S(1)} %add.9.own), channel_id=1, source_target_pairs={{0,4},{1,3},{2,6},{3,1},{4,0},{5,7},{6,2},{7,5},{8,12},{9,11},{10,... | collective-permute-start | bytes 442376 | tf_op jit(solution)/shard_map/ppermute | solution.py:451
  54.6 1.7 %collective-permute-start.19 = (bf16[288,256]{1,0:T(8,128)(2,1)S(1)}, bf16[288,256]{1,0:T(8,128)(2,1)S(1)}, u32[]{:S(2)}, u32[]{:S(2)}) collective-permute-start(bf16[288,256]{1,0:T(8,128)(2,1)S(1)} %add.10.value), channel_id=1, source_target_pairs={{0,24},{1,25},{2,26},{3,27},{4,28},{5,29},{6,30},{7,31},{8,16},{9,... | collective-permute-start | bytes 442376 | tf_op jit(solution)/shard_map/ppermute | solution.py:451
  57.3 2.8 %grad_in.2.rest_0_ = bf16[2048,256]{1,0:T(8,128)(2,1)} custom-call(bf16[96,256]{1,0:T(8,128)(2,1)S(1)} %collective-permute-done.5.near, bf16[96,256]{1,0:T(8,128)(2,1)S(1)} %collective-permute-done.6.far, bf16[2176,256]{1,0:T(8,128)(2,1)S(1)} %get-tuple-element.153.value, bf16[2304,256]{1,0:T(8,128)(2,1)S(1)} %get-tuple-element.147.weights, ...), custom_call_target="tpu_custom_call" | custom-call | flops 1207959552 | bytes 4489216 | tf_op jit(solution)/shard_map/grad_in/pallas_call | solution.py:24
  60.1 1.7 %collective-permute-start.23 = (bf16[288,256]{1,0:T(8,128)(2,1)S(1)}, bf16[288,256]{1,0:T(8,128)(2,1)S(1)}, u32[]{:S(2)}, u32[]{:S(2)}) collective-permute-start(bf16[288,256]{1,0:T(8,128)(2,1)S(1)} %add.11.value), channel_id=1, source_target_pairs={{0,24},{1,25},{2,26},{3,27},{4,28},{5,29},{6,30},{7,31},{8,16},{9,... | collective-permute-start | bytes 442376 | tf_op jit(solution)/shard_map/ppermute | solution.py:451
  62.8 2.2 %collective-permute-done.17.rest_0_ = bf16[288,256]{1,0:T(8,128)(2,1)S(1)} collective-permute-done((bf16[288,256]{1,0:T(8,128)(2,1)S(1)}, bf16[288,256]{1,0:T(8,128)(2,1)S(1)}, u32[]{:S(2)}, u32[]{:S(2)}) %collective-permute-start.17) | collective-permute-done | bytes 147488 | tf_op jit(solution)/shard_map/ppermute | solution.py:451
  67.0 2.8 %grad_in.3 = bf16[2048,256]{1,0:T(8,128)(2,1)} custom-call(bf16[96,256]{1,0:T(8,128)(2,1)S(1)} %collective-permute-done.5.near, bf16[96,256]{1,0:T(8,128)(2,1)S(1)} %collective-permute-done.6.far, bf16[2176,256]{1,0:T(8,128)(2,1)S(1)} %get-tuple-element.153.value, bf16[2304,256]{1,0:T(8,128)(2,1)S(1)} %get-tuple-element.147.weights, ...), custom_call_target="tpu_custom_call", output_to_operand_aliasing={{}: (6, {})} | custom-call | flops 1207959552 | bytes 5537792 | tf_op jit(solution)/shard_map/grad_in/pallas_call | solution.py:24
  70.3 1.1 %collective-permute-start.24 = (bf16[1152,256]{1,0:T(8,128)(2,1)S(1)}, bf16[1152,256]{1,0:T(8,128)(2,1)S(1)}, u32[]{:S(2)}, u32[]{:S(2)}) collective-permute-start(bf16[1152,256]{1,0:T(8,128)(2,1)S(1)} %join.3.value), channel_id=1, source_target_pairs={{0,1},{1,0},{2,3},{3,2},{4,5},{5,4},{6,7},{7,6},{8,9},{9,8},{10,11... | collective-permute-start | bytes 1769480 | tf_op jit(solution)/shard_map/ppermute | solution.py:451
  (53 shorter events, 14.9 us)
Async XLA Ops:
  2.3 5.1 %collective-permute-start = (bf16[64,256]{1,0:T(8,128)(2,1)S(1)}, bf16[64,256]{1,0:T(8,128)(2,1)S(1)}, u32[]{:S(2)}, u32[]{:S(2)}) collective-permute-start(bf16[64,256]{1,0:T(8,128)(2,1)S(1)} %get-tuple-element.84), channel_id=1, source_target_pairs={{0,1},{1,0},{2,3},{3,2},{4,5},{5,4},{6,7},{7,6},{8,9},{9,8},{10,11... | collective-permute-start | bytes 98312 | tf_op jit(solution)/shard_map/ppermute | solution.py:534
  2.4 5.0 %collective-permute-start.1 = (bf16[64,256]{1,0:T(8,128)(2,1)S(1)}, bf16[64,256]{1,0:T(8,128)(2,1)S(1)}, u32[]{:S(2)}, u32[]{:S(2)}) collective-permute-start(bf16[64,256]{1,0:T(8,128)(2,1)S(1)} %get-tuple-element.85), channel_id=1, source_target_pairs={{1,2},{2,1},{3,4},{4,3},{5,6},{6,5},{7,0},{0,7},{9,10},{10,9},{11,... | collective-permute-start | bytes 98312 | tf_op jit(solution)/shard_map/ppermute | solution.py:535
  7.5 5.4 %collective-permute-start.2 = (bf16[272,256]{1,0:T(8,128)(2,1)S(1)}, bf16[272,256]{1,0:T(8,128)(2,1)S(1)}, u32[]{:S(2)}, u32[]{:S(2)}) collective-permute-start(bf16[272,256]{1,0:T(8,128)(2,1)S(1)} %get-tuple-element.89), channel_id=1, source_target_pairs={{0,8},{8,0},{16,24},{24,16},{1,9},{9,1},{17,25},{25,17},{2,10},{10... | collective-permute-start | bytes 417800 | tf_op jit(solution)/shard_map/ppermute | solution.py:551
  8.8 4.1 %collective-permute-start.3 = (bf16[272,256]{1,0:T(8,128)(2,1)S(1)}, bf16[272,256]{1,0:T(8,128)(2,1)S(1)}, u32[]{:S(2)}, u32[]{:S(2)}) collective-permute-start(bf16[272,256]{1,0:T(8,128)(2,1)S(1)} %get-tuple-element.90), channel_id=1, source_target_pairs={{8,16},{16,8},{9,17},{17,9},{10,18},{18,10},{11,19},{19,11},{12,20... | collective-permute-start | bytes 417800 | tf_op jit(solution)/shard_map/ppermute | solution.py:552
  16.5 9.3 %collective-permute-start.4 = (bf16[1152,256]{1,0:T(8,128)(2,1)S(1)}, bf16[1152,256]{1,0:T(8,128)(2,1)S(1)}, u32[]{:S(2)}, u32[]{:S(2)}) collective-permute-start(bf16[1152,256]{1,0:T(8,128)(2,1)S(1)} %get-tuple-element.98), channel_id=1, source_target_pairs={{0,1},{1,0},{2,3},{3,2},{4,5},{5,4},{6,7},{7,6},{8,9},{9,8},{10,11... | collective-permute-start | bytes 1769480 | tf_op jit(solution)/shard_map/ppermute | solution.py:451
  25.7 7.4 %collective-permute-start.7 = (bf16[1152,256]{1,0:T(8,128)(2,1)S(1)}, bf16[1152,256]{1,0:T(8,128)(2,1)S(1)}, u32[]{:S(2)}, u32[]{:S(2)}) collective-permute-start(bf16[1152,256]{1,0:T(8,128)(2,1)S(1)} %get-tuple-element.113), channel_id=1, source_target_pairs={{0,1},{1,0},{2,3},{3,2},{4,5},{5,4},{6,7},{7,6},{8,9},{9,8},{10,11... | collective-permute-start | bytes 1769480 | tf_op jit(solution)/shard_map/ppermute | solution.py:451
  25.9 11.8 %collective-permute-start.8 = (bf16[288,256]{1,0:T(8,128)(2,1)S(1)}, bf16[288,256]{1,0:T(8,128)(2,1)S(1)}, u32[]{:S(2)}, u32[]{:S(2)}) collective-permute-start(bf16[288,256]{1,0:T(8,128)(2,1)S(1)} %get-tuple-element.118), channel_id=1, source_target_pairs={{0,8},{1,17},{2,10},{3,19},{4,12},{5,21},{6,14},{7,23},{8,0},{9,25... | collective-permute-start | bytes 442376 | tf_op jit(solution)/shard_map/ppermute | solution.py:451
  30.9 9.0 %collective-permute-start.9 = (bf16[288,256]{1,0:T(8,128)(2,1)S(1)}, bf16[288,256]{1,0:T(8,128)(2,1)S(1)}, u32[]{:S(2)}, u32[]{:S(2)}) collective-permute-start(bf16[288,256]{1,0:T(8,128)(2,1)S(1)} %get-tuple-element.119), channel_id=1, source_target_pairs={{0,16},{1,9},{2,18},{3,11},{4,20},{5,13},{6,22},{7,15},{8,24},{9,1... | collective-permute-start | bytes 442376 | tf_op jit(solution)/shard_map/ppermute | solution.py:451
  30.9 9.0 %collective-permute-start.10 = (bf16[288,256]{1,0:T(8,128)(2,1)S(1)}, bf16[288,256]{1,0:T(8,128)(2,1)S(1)}, u32[]{:S(2)}, u32[]{:S(2)}) collective-permute-start(bf16[288,256]{1,0:T(8,128)(2,1)S(1)} %get-tuple-element.120), channel_id=1, source_target_pairs={{0,24},{1,25},{2,26},{3,27},{4,28},{5,29},{6,30},{7,31},{8,16},{9,... | collective-permute-start | bytes 442376 | tf_op jit(solution)/shard_map/ppermute | solution.py:451
  33.1 3.5 %collective-permute-start.6 = (bf16[96,256]{1,0:T(8,128)(2,1)S(1)}, bf16[96,256]{1,0:T(8,128)(2,1)S(1)}, u32[]{:S(2)}, u32[]{:S(2)}) collective-permute-start(bf16[96,256]{1,0:T(8,128)(2,1)S(1)} %get-tuple-element.122), channel_id=1, source_target_pairs={{1,2},{2,1},{3,4},{4,3},{5,6},{6,5},{7,0},{0,7},{9,10},{10,9},{11,... | collective-permute-start | bytes 147464 | tf_op jit(solution)/shard_map/ppermute | solution.py:614
  34.0 9.3 %collective-permute-start.12 = (bf16[288,256]{1,0:T(8,128)(2,1)S(1)}, bf16[288,256]{1,0:T(8,128)(2,1)S(1)}, u32[]{:S(2)}, u32[]{:S(2)}) collective-permute-start(bf16[288,256]{1,0:T(8,128)(2,1)S(1)} %get-tuple-element.127), channel_id=1, source_target_pairs={{0,8},{1,17},{2,10},{3,19},{4,12},{5,21},{6,14},{7,23},{8,0},{9,25... | collective-permute-start | bytes 442376 | tf_op jit(solution)/shard_map/ppermute | solution.py:451
  36.6 6.7 %collective-permute-start.13 = (bf16[288,256]{1,0:T(8,128)(2,1)S(1)}, bf16[288,256]{1,0:T(8,128)(2,1)S(1)}, u32[]{:S(2)}, u32[]{:S(2)}) collective-permute-start(bf16[288,256]{1,0:T(8,128)(2,1)S(1)} %get-tuple-element.128), channel_id=1, source_target_pairs={{0,16},{1,9},{2,18},{3,11},{4,20},{5,13},{6,22},{7,15},{8,24},{9,1... | collective-permute-start | bytes 442376 | tf_op jit(solution)/shard_map/ppermute | solution.py:451
  37.7 6.6 %collective-permute-start.14 = (bf16[288,256]{1,0:T(8,128)(2,1)S(1)}, bf16[288,256]{1,0:T(8,128)(2,1)S(1)}, u32[]{:S(2)}, u32[]{:S(2)}) collective-permute-start(bf16[288,256]{1,0:T(8,128)(2,1)S(1)} %get-tuple-element.129), channel_id=1, source_target_pairs={{0,24},{1,25},{2,26},{3,27},{4,28},{5,29},{6,30},{7,31},{8,16},{9,... | collective-permute-start | bytes 442376 | tf_op jit(solution)/shard_map/ppermute | solution.py:451
  39.9 6.8 %collective-permute-start.11 = (bf16[288,256]{1,0:T(8,128)(2,1)S(1)}, bf16[288,256]{1,0:T(8,128)(2,1)S(1)}, u32[]{:S(2)}, u32[]{:S(2)}) collective-permute-start(bf16[288,256]{1,0:T(8,128)(2,1)S(1)} %add.6.own), channel_id=1, source_target_pairs={{0,2},{1,5},{2,0},{3,7},{4,6},{5,1},{6,4},{7,3},{8,10},{9,13},{10,... | collective-permute-start | bytes 442376 | tf_op jit(solution)/shard_map/ppermute | solution.py:451
  44.4 7.2 %collective-permute-start.16 = (bf16[288,256]{1,0:T(8,128)(2,1)S(1)}, bf16[288,256]{1,0:T(8,128)(2,1)S(1)}, u32[]{:S(2)}, u32[]{:S(2)}) collective-permute-start(bf16[288,256]{1,0:T(8,128)(2,1)S(1)} %add.7.own), channel_id=1, source_target_pairs={{0,2},{1,5},{2,0},{3,7},{4,6},{5,1},{6,4},{7,3},{8,10},{9,13},{10,... | collective-permute-start | bytes 442376 | tf_op jit(solution)/shard_map/ppermute | solution.py:451
  46.7 7.8 %collective-permute-start.15 = (bf16[288,256]{1,0:T(8,128)(2,1)S(1)}, bf16[288,256]{1,0:T(8,128)(2,1)S(1)}, u32[]{:S(2)}, u32[]{:S(2)}) collective-permute-start(bf16[288,256]{1,0:T(8,128)(2,1)S(1)} %add.8.own), channel_id=1, source_target_pairs={{0,4},{1,3},{2,6},{3,1},{4,0},{5,7},{6,2},{7,5},{8,12},{9,11},{10,... | collective-permute-start | bytes 442376 | tf_op jit(solution)/shard_map/ppermute | solution.py:451
  51.6 8.5 %collective-permute-start.20 = (bf16[288,256]{1,0:T(8,128)(2,1)S(1)}, bf16[288,256]{1,0:T(8,128)(2,1)S(1)}, u32[]{:S(2)}, u32[]{:S(2)}) collective-permute-start(bf16[288,256]{1,0:T(8,128)(2,1)S(1)} %add.9.own), channel_id=1, source_target_pairs={{0,4},{1,3},{2,6},{3,1},{4,0},{5,7},{6,2},{7,5},{8,12},{9,11},{10,... | collective-permute-start | bytes 442376 | tf_op jit(solution)/shard_map/ppermute | solution.py:451
  54.6 7.3 %collective-permute-start.19 = (bf16[288,256]{1,0:T(8,128)(2,1)S(1)}, bf16[288,256]{1,0:T(8,128)(2,1)S(1)}, u32[]{:S(2)}, u32[]{:S(2)}) collective-permute-start(bf16[288,256]{1,0:T(8,128)(2,1)S(1)} %add.10.value), channel_id=1, source_target_pairs={{0,24},{1,25},{2,26},{3,27},{4,28},{5,29},{6,30},{7,31},{8,16},{9,... | collective-permute-start | bytes 442376 | tf_op jit(solution)/shard_map/ppermute | solution.py:451
  56.3 6.5 %collective-permute-start.18 = (bf16[288,256]{1,0:T(8,128)(2,1)S(1)}, bf16[288,256]{1,0:T(8,128)(2,1)S(1)}, u32[]{:S(2)}, u32[]{:S(2)}) collective-permute-start(bf16[288,256]{1,0:T(8,128)(2,1)S(1)} %add.10.value), channel_id=1, source_target_pairs={{0,16},{1,9},{2,18},{3,11},{4,20},{5,13},{6,22},{7,15},{8,24},{9,1... | collective-permute-start | bytes 442376 | tf_op jit(solution)/shard_map/ppermute | solution.py:451
  56.3 8.8 %collective-permute-start.17 = (bf16[288,256]{1,0:T(8,128)(2,1)S(1)}, bf16[288,256]{1,0:T(8,128)(2,1)S(1)}, u32[]{:S(2)}, u32[]{:S(2)}) collective-permute-start(bf16[288,256]{1,0:T(8,128)(2,1)S(1)} %add.10.value), channel_id=1, source_target_pairs={{0,8},{1,17},{2,10},{3,19},{4,12},{5,21},{6,14},{7,23},{8,0},{9,25... | collective-permute-start | bytes 442376 | tf_op jit(solution)/shard_map/ppermute | solution.py:451
  60.1 9.7 %collective-permute-start.23 = (bf16[288,256]{1,0:T(8,128)(2,1)S(1)}, bf16[288,256]{1,0:T(8,128)(2,1)S(1)}, u32[]{:S(2)}, u32[]{:S(2)}) collective-permute-start(bf16[288,256]{1,0:T(8,128)(2,1)S(1)} %add.11.value), channel_id=1, source_target_pairs={{0,24},{1,25},{2,26},{3,27},{4,28},{5,29},{6,30},{7,31},{8,16},{9,... | collective-permute-start | bytes 442376 | tf_op jit(solution)/shard_map/ppermute | solution.py:451
  61.9 7.9 %collective-permute-start.22 = (bf16[288,256]{1,0:T(8,128)(2,1)S(1)}, bf16[288,256]{1,0:T(8,128)(2,1)S(1)}, u32[]{:S(2)}, u32[]{:S(2)}) collective-permute-start(bf16[288,256]{1,0:T(8,128)(2,1)S(1)} %add.11.value), channel_id=1, source_target_pairs={{0,16},{1,9},{2,18},{3,11},{4,20},{5,13},{6,22},{7,15},{8,24},{9,1... | collective-permute-start | bytes 442376 | tf_op jit(solution)/shard_map/ppermute | solution.py:451
  61.9 8.3 %collective-permute-start.21 = (bf16[288,256]{1,0:T(8,128)(2,1)S(1)}, bf16[288,256]{1,0:T(8,128)(2,1)S(1)}, u32[]{:S(2)}, u32[]{:S(2)}) collective-permute-start(bf16[288,256]{1,0:T(8,128)(2,1)S(1)} %add.11.value), channel_id=1, source_target_pairs={{0,8},{1,17},{2,10},{3,19},{4,12},{5,21},{6,14},{7,23},{8,0},{9,25... | collective-permute-start | bytes 442376 | tf_op jit(solution)/shard_map/ppermute | solution.py:451
  65.1 7.3 %collective-permute-start.25 = (bf16[1152,256]{1,0:T(8,128)(2,1)S(1)}, bf16[1152,256]{1,0:T(8,128)(2,1)S(1)}, u32[]{:S(2)}, u32[]{:S(2)}) collective-permute-start(bf16[1152,256]{1,0:T(8,128)(2,1)S(1)} %join.2.value), channel_id=1, source_target_pairs={{0,1},{1,0},{2,3},{3,2},{4,5},{5,4},{6,7},{7,6},{8,9},{9,8},{10,11... | collective-permute-start | bytes 1769480 | tf_op jit(solution)/shard_map/ppermute | solution.py:451
  (2 other events, 5.1 us)

commit v2 on v1

--- a/solution.py
+++ b/solution.py
@@ -11,11 +11,25 @@
 F32, BF16 = jnp.float32, jnp.bfloat16
 
 
-def kernel_call(body, name, outs, ins, flops=0, scratch=(), aliases=None, limit=24):
+def kernel_call(body, name, outs, ins, flops=0, scratch=(), aliases=None, limit=24, flush=()):
+    outs, ins, scratch, aliases = list(outs), list(ins), list(scratch), dict(aliases or {})
+    counts = len(ins), len(outs), len(scratch)
+    rows, given = [], []
+    for array, buffer, row, total in flush:
+        ins.append(array)
+        rows.append((row, array.shape[0]))
+        given.append(buffer is not None)
+        outs.append(((total, array.shape[1]), array.dtype, "hbm"))
+        if buffer is not None:
+            aliases[len(ins)] = len(outs) - 1
+            ins.append(in_hbm(buffer))
+        scratch.append(pltpu.SemaphoreType.DMA)
+    if flush:
+        body = functools.partial(flushing_kernel, body, counts, rows, given)
     out_shape, out_specs, in_specs, arrays = [], [], [], []
-    for shape, kind, *place in outs:
-        out_shape.append(pltpu.HBM(shape, kind) if place else pltpu.VMEM(shape, kind))
-        out_specs.append(pl.BlockSpec(memory_space=pltpu.HBM if place else pltpu.VMEM))
+    for shape, kind, *spot in outs:
+        out_shape.append(pltpu.HBM(shape, kind) if spot else pltpu.VMEM(shape, kind))
+        out_specs.append(pl.BlockSpec(memory_space=pltpu.HBM if spot else pltpu.VMEM))
     for x in ins:
         far = isinstance(x, tuple)
         arrays.append(x[0] if far else x)
@@ -26,12 +40,37 @@
         out_shape=out_shape,
         in_specs=in_specs,
         out_specs=out_specs,
-        scratch_shapes=list(scratch),
-        input_output_aliases=aliases or {},
+        scratch_shapes=scratch,
+        input_output_aliases=aliases,
         compiler_params=pltpu.CompilerParams(vmem_limit_bytes=limit << 20),
         cost_estimate=pl.CostEstimate(flops=flops, bytes_accessed=moved, transcendentals=0),
         name=name,
     )(*arrays)
+
+
+def flushing_kernel(body, counts, rows, given, *refs):
+    refs = list(refs)
+
+    def take(count):
+        taken = refs[:count]
+        del refs[:count]
+        return taken
+
+    ins = take(counts[0])
+    sources = []
+    for has_buffer in given:
+        sources.append(take(1 + has_buffer)[0])
+    outs, buffers = take(counts[1]), take(len(rows))
+    scratch, sems = take(counts[2]), take(len(rows))
+    copies = [
+        pltpu.make_async_copy(source, buffer.at[pl.ds(row, count), :], sem)
+        for source, buffer, sem, (row, count) in zip(sources, buffers, sems, rows)
+    ]
+    for copy in copies:
+        copy.start()
+    body(*ins, *outs, *scratch)
+    for copy in copies:
+        copy.wait()
 
 
 def in_hbm(x):
@@ -91,18 +130,22 @@
     for copy in copies:
         copy.start()
     odd = is_odd("lon")
+    half = 4 * rows
     for n, (copy, source) in enumerate(zip(copies, (field, cot))):
         copy.wait()
         for r in range(rows):
-            first = source[r * cols : r * cols + 16, :].astype(F32)[:1]
-            last = source[(r + 1) * cols - 16 : (r + 1) * cols, :].astype(F32)[15:]
-            lines[n * rows + r : n * rows + r + 1, :] = jnp.where(odd, first, last)
-            lines[(2 + n) * rows + r : (2 + n) * rows + r + 1, :] = jnp.where(odd, last, first)
-    near[...] = lines[: 2 * rows, :].astype(BF16)
-    far[...] = lines[2 * rows :, :].astype(BF16)
-
-
-def prep_kernel(cols, field, one_hbm, two_hbm, act3, k_one, k_two, t_one, t_two, sems):
+            first = source[r * cols : r * cols + 16, :].astype(F32)
+            last = source[(r + 1) * cols - 16 : (r + 1) * cols, :].astype(F32)
+            for k in range(2):
+                at = (2 * n + k) * rows + r
+                lines[at : at + 1, :] = jnp.where(odd, first[k : k + 1], last[14 + k : 15 + k])
+                at += half
+                lines[at : at + 1, :] = jnp.where(odd, last[14 + k : 15 + k], first[k : k + 1])
+    near[...] = lines[:half, :].astype(BF16)
+    far[...] = lines[half:, :].astype(BF16)
+
+
+def prep_kernel(cols, field, cot, one_hbm, two_hbm, act3, cot3, k_one, k_two, t_one, t_two, sems):
     rows = field.shape[0] // cols
     chans = field.shape[1]
     copies = [
@@ -116,6 +159,7 @@
         at = aligned(r * cols, cols)
         to = aligned((r + 1) * cols, cols)
         put_shifted(act3, to, silu(field[pl.ds(at, cols), :].astype(F32)), cols)
+        put_shifted(cot3, to, cot[pl.ds(at, cols), :].astype(F32), cols)
         return carry
 
     lax.fori_loop(0, rows, body, 0, unroll=2)
@@ -140,37 +184,38 @@
         out[: 2 * cols, :] = field[pl.ds(start, 2 * cols), :]
         out[2 * cols : 4 * cols, :] = cot[pl.ds(start, 2 * cols), :]
         lines = []
-        for base in (0, rows):
+        for n in range(2):
             for r in range(2):
                 for side in (left, right):
-                    top = side[base + r : base + r + 1]
-                    bottom = side[base + rows - 2 + r : base + rows - 1 + r]
-                    lines.append(jnp.where(first == 1, top, bottom))
-        lines.append(jnp.zeros((8, chans), F32))
+                    for k in range(2):
+                        base = (2 * n + k) * rows
+                        top = side[base + r : base + r + 1]
+                        bottom = side[base + rows - 2 + r : base + rows - 1 + r]
+                        lines.append(jnp.where(first == 1, top, bottom))
         out[4 * cols :, :] = jnp.concatenate(lines, axis=0).astype(BF16)
 
 
-def inner_kernel(cols, near, far, cot, k_one, _a, act3, cot3, hid, mid, turned, edges):
-    rows = near.shape[0] // 2
+def inner_kernel(
+    cols, near, far, k_one, t_two, _a, _c, act3, cot3, hid, mid, ghid, turned, edges
+):
+    rows = near.shape[0] // 4
     chans = near.shape[1]
     odd = is_odd("lon")
     low, high = near[...].astype(F32), far[...].astype(F32)
-    edges[: 2 * rows, :] = jnp.where(odd, low, high)
-    edges[2 * rows :, :] = jnp.where(odd, high, low)
+    edges[: 4 * rows, :] = jnp.where(odd, low, high)
+    edges[4 * rows :, :] = jnp.where(odd, high, low)
     line = lax.broadcasted_iota(jnp.int32, (16, chans), 0)
 
     def patch(r, carry):
         start = aligned((r + 1) * cols, cols)
         end = aligned((r + 2) * cols - 16, 16)
-        left = silu(edges[pl.ds(r, 1), :]).astype(BF16).astype(F32)
-        right = silu(edges[pl.ds(2 * rows + r, 1), :]).astype(BF16).astype(F32)
-        old = act3[pl.ds(start, 16), :chans].astype(F32)
-        act3[pl.ds(start, 16), :chans] = jnp.where(line == 0, left, old).astype(BF16)
-        old = act3[pl.ds(end, 16), 2 * chans :].astype(F32)
-        act3[pl.ds(end, 16), 2 * chans :] = jnp.where(line == 15, right, old).astype(BF16)
-        x = cot[pl.ds(aligned(r * cols, cols), cols), :].astype(F32)
-        left, right = edges[pl.ds(rows + r, 1), :], edges[pl.ds(3 * rows + r, 1), :]
-        put_shifted(cot3, start, x, cols, left, right)
+        for out, base, fix in ((act3, 0, silu), (cot3, 2 * rows, same)):
+            left = fix(edges[pl.ds(base + rows + r, 1), :]).astype(BF16).astype(F32)
+            right = fix(edges[pl.ds(base + 4 * rows + r, 1), :]).astype(BF16).astype(F32)
+            old = out[pl.ds(start, 16), :chans].astype(F32)
+            out[pl.ds(start, 16), :chans] = jnp.where(line == 0, left, old).astype(BF16)
+            old = out[pl.ds(end, 16), 2 * chans :].astype(F32)
+            out[pl.ds(end, 16), 2 * chans :] = jnp.where(line == 15, right, old).astype(BF16)
         return carry
 
     lax.fori_loop(0, rows, patch, 0, unroll=4)
@@ -179,6 +224,10 @@
         got = conv_rows(act3, k_one, r * cols, count * cols, cols)
         hid[to, :] = got
         mid[to, :] = silu(got).astype(BF16)
+    for r, count in row_blocks(1, rows - 1):
+        to = pl.ds((r + 1) * cols, count * cols)
+        got = conv_rows(cot3, t_two, r * cols, count * cols, cols)
+        ghid[to, :] = (got * silu_grad(hid[to, :])).astype(BF16)
     own = slice(3 * cols, (rows - 1) * cols)
     turned[:, 2 * cols : (rows - 2) * cols] = mid[own, :].T
 
@@ -203,8 +252,8 @@
         part[base + (1 - half) * 2 * cols : base + (2 - half) * 2 * cols, :] = source[own, :]
         for r in range(2):
             x = fix(halo[(2 * n + r) * cols : (2 * n + r + 1) * cols])
-            corner = 4 * cols + 4 * n + 2 * r
-            left, right = fix(halo[corner : corner + 1]), fix(halo[corner + 1 : corner + 2])
+            corner = 4 * cols + 8 * n + 4 * r
+            left, right = fix(halo[corner + 1 : corner + 2]), fix(halo[corner + 2 : corner + 3])
             put_shifted(part, base + (half * 2 + r) * cols, x, cols, left, right)
 
 
@@ -218,7 +267,7 @@
 
 def outer_kernel(
     cols, near, far, k_one, _a, _c, _h, _m, _t,
-    act3, cot3, hid, mid, turned, keep, send, part, term,
+    act3, cot3, hid, mid, turned, keep, send, part,
 ):
     chans = mid.shape[1]
     rows = mid.shape[0] // cols - 2
@@ -237,30 +286,27 @@
         mid[to : to + 2 * cols, :] = value.astype(BF16)
     turned[:, : 2 * cols] = mid[cols : 3 * cols, :].T
     turned[:, (rows - 2) * cols :] = mid[(rows - 1) * cols : (rows + 1) * cols, :].T
+    own = core_order(turned)
+    half = chans // 2
     for i in range(3):
-        got = jnp.dot(
-            turned[...], cot3[i * cols : (i + rows) * cols, :], preferred_element_type=F32
-        )
+        got = jnp.dot(own, cot3[i * cols : (i + rows) * cols, :], preferred_element_type=F32)
         for j in range(3):
             tap = (2 - i) * 3 + 2 - j
-            term[tap * chans : (tap + 1) * chans, :] = got[:, j * chans : (j + 1) * chans]
-    split(term, keep, send)
-
-
-def split(term, keep, send):
-    half = keep.shape[0]
+            to, at = slice(tap * half, (tap + 1) * half), slice(j * chans, (j + 1) * chans)
+            keep[to, :] = got[:half, at]
+            send[to, :] = got[half:, at].astype(BF16)
+
+
+def core_order(turned):
+    half = turned.shape[0] // 2
     bit = lax.axis_index("lon") % 2
-    keep[...] = term[pl.ds(aligned(bit * half, 16), half), :]
-    send[...] = term[pl.ds(aligned((1 - bit) * half, 16), half), :].astype(BF16)
-
-
-def back_kernel(cols, near, far, t_two, cot3, hid, mid, ghid, turned, side_near, side_far, part, lines):
-    chans = mid.shape[1]
-    rows = mid.shape[0] // cols - 2
-    for r, count in row_blocks(1, rows - 1):
-        to = pl.ds((r + 1) * cols, count * cols)
-        got = conv_rows(cot3, t_two, r * cols, count * cols, cols)
-        ghid[to, :] = (got * silu_grad(hid[to, :])).astype(BF16)
+    mine, other = (pl.ds(aligned(x * half, 16), half) for x in (bit, 1 - bit))
+    return jnp.concatenate([turned[mine, :], turned[other, :]], axis=0)
+
+
+def grad_one_kernel(cols, near, far, t_two, cot3, act3, hid, _g, ghid, keep, send, turned, part):
+    chans, cells = turned.shape
+    rows = cells // cols
     put_halo(part, halo_rows(near, far), 1, cols, same, cot3)
     for half in range(2):
         to = slice(half * rows * cols, half * rows * cols + 2 * cols)
@@ -268,41 +314,73 @@
         value = jnp.where(edge_mask(half, cols, got.shape), got * silu_grad(hid[to, :]), 0.0)
         ghid[to, :] = value.astype(BF16)
     turned[...] = ghid[cols : (rows + 1) * cols, :].T
-    lanes = side_near.shape[0] // 2
-    odd = is_odd("lon")
-    for n, source in enumerate((mid, ghid)):
-        for r in range(rows + 2):
-            first = source[r * cols : r * cols + 16, :].astype(F32)[:1]
-            last = source[(r + 1) * cols - 16 : (r + 1) * cols, :].astype(F32)[15:]
-            at = n * lanes + r
-            lines[at : at + 1, :] = jnp.where(odd, first, last)
-            lines[2 * lanes + at : 2 * lanes + at + 1, :] = jnp.where(odd, last, first)
-        for base in (n * lanes, (2 + n) * lanes):
-            lines[base + rows + 2 : base + lanes, :] = jnp.zeros((lanes - rows - 2, chans), F32)
-    side_near[...] = lines[: 2 * lanes, :].astype(BF16)
-    side_far[...] = lines[2 * lanes :, :].astype(BF16)
-
-
-def grad_one_kernel(cols, turned, act3, keep, send, term):
-    chans, cells = turned.shape
+    own = core_order(turned)
+    half = chans // 2
     for i in range(3):
-        got = jnp.dot(
-            turned[...], act3[i * cols : i * cols + cells, :], preferred_element_type=F32
-        )
+        got = jnp.dot(own, act3[i * cols : i * cols + cells, :], preferred_element_type=F32)
         for j in range(3):
             tap = i * 3 + j
-            term[tap * chans : (tap + 1) * chans, :] = got[:, j * chans : (j + 1) * chans].T
-    split(term, keep, send)
-
-
-def last_kernel(backward, first, count, cols, near, far, value, weights, field, cot, *rest):
-    out, edges, shifted, result, sems = rest[-5:]
-    lanes = near.shape[0] // 2
+            to, at = slice(tap * chans, (tap + 1) * chans), slice(j * chans, (j + 1) * chans)
+            keep[to, :] = got[:half, at].T
+            send[to, :] = got[half:, at].T.astype(BF16)
+
+
+def rim_kernel(cols, own_near, own_far, near, far, lat_near, lat_far, k_one, t_two, mid, ghid):
+    rows = near.shape[0] // 4
+    chans = near.shape[1]
+    lanes = mid.shape[0] // 2
     odd = is_odd("lon")
-    part = slice(lanes, None) if backward else slice(0, lanes)
-    low, high = near[part, :].astype(F32), far[part, :].astype(F32)
-    edges[:lanes, :] = jnp.where(odd, low, high)
-    edges[lanes:, :] = jnp.where(odd, high, low)
+    pairs = [[x[...].astype(F32) for x in pair] for pair in ((own_far, own_near), (near, far))]
+    (first, last), (left, right) = [
+        (jnp.where(odd, b, a), jnp.where(odd, a, b)) for a, b in (pairs[0], pairs[1][::-1])
+    ]
+    halos = halo_rows(lat_near, lat_far)
+    lat = lax.axis_index("lat")
+    line = lax.broadcasted_iota(jnp.int32, (2 * lanes, chans), 0) % lanes
+    inside = jnp.logical_and(
+        jnp.logical_or(line > 0, lat > 0),
+        jnp.logical_or(line <= rows, lat < lax.axis_size("lat") - 1),
+    )
+
+    def column(n, source, k, spot, fix):
+        ends = []
+        for halo in halos:
+            for r in range(2):
+                at = spot(n, r)
+                ends.append(halo[at : at + 1])
+        base = (2 * n + k) * rows
+        filler = jnp.zeros((lanes - rows - 4, chans), F32)
+        lines = [*ends[:2], source[base : base + rows], *ends[2:], filler]
+        return fix(jnp.concatenate(lines, axis=0))
+
+    def corner(k):
+        return lambda n, r: 4 * cols + 8 * n + 4 * r + k
+
+    def main(col):
+        return lambda n, r: (2 * n + r) * cols + col
+
+    results = []
+    for n, (fix, weights) in enumerate(((silu, k_one), (same, t_two))):
+        sides = []
+        for spots in (
+            ((left, 0, corner(0)), (left, 1, corner(1)), (first, 0, main(0))),
+            ((last, 1, main(cols - 1)), (right, 0, corner(2)), (right, 1, corner(3))),
+        ):
+            three = jnp.concatenate(
+                [column(n, source, k, spot, fix) for source, k, spot in spots], axis=1
+            )
+            nine = [three, pltpu.roll(three, lanes - 1, 0), pltpu.roll(three, lanes - 2, 0)]
+            sides.append(jnp.concatenate(nine, axis=1))
+        both = jnp.concatenate(sides, axis=0).astype(BF16)
+        results.append(jnp.dot(both, weights[...], preferred_element_type=F32))
+    hid, gmid = results
+    mid[...] = jnp.where(inside, silu(hid), 0.0)
+    ghid[...] = jnp.where(inside, gmid * silu_grad(hid), 0.0)
+
+
+def last_kernel(backward, first, count, cols, edges, value, weights, field, cot, *rest):
+    out, shifted = rest
+    lanes = edges.shape[0] // 2
 
     def body(r, carry):
         x = value[pl.ds(aligned((first + r) * cols, cols), cols), :].astype(F32)
@@ -312,20 +390,15 @@
 
     lax.fori_loop(0, count + 2, body, 0, unroll=2)
     step = max(count // 2, 1)
-    copies = []
-    for n, r in enumerate(range(0, count, step)):
+    for r in range(0, count, step):
         at = slice((first + r) * cols, (first + r + step) * cols)
         to = slice(r * cols, (r + step) * cols)
         got = conv_rows(shifted, weights, r * cols, step * cols, cols)
         x = field[at, :].astype(F32)
         if backward:
-            result[to, :] = (cot[at, :].astype(F32) + got * silu_grad(x)).astype(BF16)
+            out[to, :] = (cot[at, :].astype(F32) + got * silu_grad(x)).astype(BF16)
         else:
-            result[to, :] = (x + got).astype(BF16)
-        copies.append(pltpu.make_async_copy(result.at[to, :], out.at[at, :], sems.at[n]))
-        copies[-1].start()
-    for copy in copies:
-        copy.wait()
+            out[to, :] = (x + got).astype(BF16)
 
 
 def place():
@@ -367,17 +440,27 @@
         out[chunk(partner(n), rows), :] = got[...]
 
 
+def scale_kernel(factor, own, got, out):
+    half = out.shape[1] // 2
+    bit = lax.axis_index("lon") % 2
+    for tap in range(9):
+        at = slice(tap * half, (tap + 1) * half)
+        for x, which in ((own, bit), (got, 1 - bit)):
+            to = pl.ds(aligned((2 * tap + which) * half, 16), half)
+            out[to, :] = x[at, :].astype(F32) * factor
+
+
 def final_kernel(factor, own, value, *rest):
     out, scaled, sems = rest[-3:]
-    half, chunks = value.shape[0], sems.shape[0]
-    bit = place()[1]
-    base = (bit if own else 1 - bit) * half
+    rows, half = value.shape
+    count = rows // sems.shape[0]
+    bit = lax.axis_index("lon") % 2
+    lanes = pl.ds(aligned((bit if own else 1 - bit) * half, half), half)
     copies = []
-    for n in range(chunks):
-        at = pl.ds(n * (half // chunks), half // chunks)
-        to = pl.ds(aligned(base + n * (half // chunks), 16), half // chunks)
+    for n in range(sems.shape[0]):
+        at = pl.ds(n * count, count)
         scaled[at, :] = value[at, :].astype(F32) * factor
-        copies.append(pltpu.make_async_copy(scaled.at[at, :], out.at[to, :], sems.at[n]))
+        copies.append(pltpu.make_async_copy(scaled.at[at, :], out.at[at, lanes], sems.at[n]))
         copies[-1].start()
     for copy in copies:
         copy.wait()
@@ -464,28 +547,32 @@
         elif kind == "join":
             outs = [((rows * lax.axis_size("lat"), chans), BF16)]
             self.sent = kernel_call(join_kernel, "join", outs, [*self.sent, *got], limit=16)
+        elif kind == "last" and self.result is None:
+            outs = [((2 * rows * lax.axis_size("lat"), chans), F32)]
+            body = functools.partial(scale_kernel, self.factor)
+            (self.result,) = kernel_call(body, "scaled", outs, [*self.sent, *got], limit=16)
+            self.sent = [self.result]
         elif kind == "last":
-            if self.result is None:
-                self.scale(self.sent[0], True)
-            self.sent = [self.scale(got[0], False)]
+            self.sent = self.scale(got[0], False)
         else:
             mine = self.keep if kind == "lat" else self.sent[0]
             outs = [((rows, chans), BF16)]
             self.sent = kernel_call(add_round_kernel, "add", outs, [mine, *got], limit=16)
 
-    def scale(self, value, own):
+    def scale(self, value, own, flush=()):
         rows, chans = value.shape
         ins = [value] if own else [value, in_hbm(self.result)]
-        (self.result,) = kernel_call(
+        self.result, *buffers = kernel_call(
             functools.partial(final_kernel, self.factor, own),
             "scaled",
-            [((2 * rows, chans), F32, "hbm")],
+            [((rows, 2 * chans), F32, "hbm")],
             ins,
             scratch=[pltpu.VMEM((rows, chans), F32), pltpu.SemaphoreType.DMA((4,))],
             aliases=None if own else {1: 0},
             limit=16,
+            flush=flush,
         )
-        return self.result
+        return [self.result, *buffers]
 
 
 class Turns:
@@ -523,23 +610,23 @@
     near_lat, far_lat = paired(lat_count, 0, False), paired(lat_count, 1, False)
 
     tile = ((cells, chans), BF16)
-    line = ((2 * rows, chans), BF16)
+    line = ((4 * rows, chans), BF16)
     field, cot, near, far = call(
         ends_kernel,
         "ends",
         [tile, tile, line, line],
         [in_hbm(field_in.reshape(cells, chans)), in_hbm(cotangent.reshape(cells, chans))],
-        scratch=[pltpu.VMEM((4 * rows, chans), F32), sems],
+        scratch=[pltpu.VMEM((8 * rows, chans), F32), sems],
     )
     lon_near = lax.ppermute(near, "lon", near_lon)
     lon_far = lax.ppermute(far, "lon", far_lon)
     wide = ((tall, 3 * chans), BF16)
     square = ((9 * chans, chans), BF16)
-    act3, k_one, k_two, t_one, t_two = call(
+    act3, cot3, k_one, k_two, t_one, t_two = call(
         prep_kernel,
         "prep",
-        [wide, square, square, square, square],
-        [field] + [in_hbm(k.reshape(9 * chans, chans)) for k in (kernel_one, kernel_two)],
+        [wide, wide, square, square, square, square],
+        [field, cot] + [in_hbm(k.reshape(9 * chans, chans)) for k in (kernel_one, kernel_two)],
         flops=flops,
         scratch=[sems],
     )
@@ -554,109 +641,116 @@
     high = ((tall, chans), F32)
     flat = ((tall, chans), BF16)
     turned = ((chans, cells), BF16)
-    act3, cot3, hid, mid, mid_t = call(
+    act3, cot3, hid, mid, ghid, mid_t = call(
         inner_kernel,
         "inner_rows",
-        [wide, wide, high, flat, turned],
-        [lon_near, lon_far, cot, k_one, *after([act3], send_near, send_far)],
-        flops=flops,
-        scratch=[pltpu.VMEM((4 * rows, chans), F32)],
-        aliases={4: 0},
+        [wide, wide, high, flat, flat, turned],
+        [lon_near, lon_far, k_one, t_two, *after([act3], send_near, send_far), cot3],
+        flops=2 * flops,
+        scratch=[pltpu.VMEM((8 * rows, chans), F32)],
+        aliases={4: 0, 5: 1},
     )
-    half = 9 * chans // 2
-    parts = [((half, chans), F32), ((half, chans), BF16)]
+    half = (9 * chans // 2, chans)
+    parts = [(half, F32), (half, BF16)]
     part = pltpu.VMEM((8 * cols, 3 * chans), BF16)
-    term = pltpu.VMEM((9 * chans, chans), F32)
     act3, cot3, hid, mid, _, keep, send = call(
         outer_kernel,
         "grad_two",
         [wide, wide, high, flat, turned] + parts,
         [lat_near, lat_far, k_one, act3, cot3, hid, mid, mid_t],
         flops=flops,
-        scratch=[part, term],
+        scratch=[part],
         aliases={3: 0, 4: 1, 5: 2, 6: 3, 7: 4},
     )
     turns = Turns()
     two = Summed(keep, send, factor)
     turns.start(two)
 
-    lanes = -(-(rows + 2) // 16) * 16
-    sides = ((2 * lanes, chans), BF16)
-
-    def grad_hid_part(waits):
+    lanes = -(-(rows + 4) // 8) * 8
+    rim = ((2 * lanes, chans), F32)
+
+    def rim_part(waits):
         return call(
-            back_kernel,
-            "grad_hid",
-            [flat, turned, sides, sides],
-            [*after([lat_near], *waits), lat_far, t_two, cot3, hid, mid],
-            flops=flops,
-            scratch=[part, pltpu.VMEM((4 * lanes, chans), F32)],
+            rim_kernel,
+            "rim",
+            [rim, rim],
+            [near, far, *after([lon_near, lon_far], *waits), lat_near, lat_far, k_one, t_two],
+            flops=flops // 16,
         )
 
     def grad_one_part(waits):
         return call(
             grad_one_kernel,
             "grad_one",
-            parts,
-            [*after([ghid_t], *waits), act3],
+            [flat] + [((9 * chans, chans // 2), kind) for kind in (F32, BF16)],
+            [*after([lat_near], *waits), lat_far, t_two, cot3, act3, hid, ghid],
             flops=flops,
-            scratch=[term],
+            scratch=[pltpu.VMEM((chans, cells), BF16), part],
+            aliases={6: 0},
         )
 
-    ghid, ghid_t, side_near, side_far = turns.run(grad_hid_part)
-    keep, send = turns.run(grad_one_part)
+    ghid, keep, send = turns.run(grad_one_part)
     one = Summed(keep, send, factor)
     turns.start(one)
     turns.finish(two)
     turns.start(two)
-    side_near, side_far = after([side_near, side_far], *turns.last)
-    got_near = lax.ppermute(side_near, "lon", near_lon)
-    got_far = lax.ppermute(side_far, "lon", far_lon)
     turns.finish(one)
     turns.start(one)
-    got_near, got_far = after([got_near, got_far], *turns.last)
-    turns.last = [got_near, got_far]
+    rims = turns.run(rim_part)
     turns.finish(two)
     turns.start(two)
 
     results = [None, None]
+    waiting = []
+
+    def flushed(buffers):
+        for (which, _, _), buffer in zip(waiting, buffers):
+            results[which] = buffer
+        waiting.clear()
+
+    def flushes():
+        return [(x, results[which], row, cells) for which, x, row in waiting]
 
     def piece(which, half, waits):
         count = rows // 2
-        ins = [got_near, got_far, *after([(mid, ghid)[which]], *waits)]
-        ins += [(k_two, t_one)[which], field, cot]
-        (results[which],) = call(
+        result, *buffers = call(
             functools.partial(last_kernel, bool(which), half * count, count),
             ("field_out", "grad_in")[which],
-            [((cells, chans), BF16, "hbm")],
-            ins + ([in_hbm(results[which])] if half else []),
+            [((count * cols, chans), BF16)],
+            [rims[which], *after([(mid, ghid)[which]], *waits)]
+            + [(k_two, t_one)[which], field, cot],
             flops=flops // 2,
-            scratch=[
-                pltpu.VMEM((2 * lanes, chans), F32),
-                pltpu.VMEM(((count + 2) * cols, 3 * chans), BF16),
-                pltpu.VMEM((count * cols, chans), BF16),
-                sems,
-            ],
-            aliases={len(ins): 0} if half else None,
+            scratch=[pltpu.VMEM(((count + 2) * cols, 3 * chans), BF16)],
+            flush=flushes(),
         )
-        return [results[which]]
-
-    def scaling(chain):
-        return lambda waits: [chain.scale(*after(chain.sent, *waits), True)]
+        flushed(buffers)
+        waiting.append((which, result, half * count * cols))
+        return [result, *buffers]
+
+    def own_half(waits):
+        more = [(two.result, None, 0, 9 * chans)]
+        value = after(one.sent, *waits)[0]
+        result, *buffers = one.scale(value, True, flushes() + more)
+        two.result = buffers.pop()
+        flushed(buffers)
+        return [result, *buffers, two.result]
 
     work = [functools.partial(piece, which, half) for which in (0, 1) for half in (0, 1)]
-    while one.steps:
-        if work:
-            turns.run(work.pop(0))
+    for turn in (0, one, two, 1, one, two, 2, one, two, 3):
+        if isinstance(turn, int):
+            turns.run(work[turn])
+        elif turn.steps:
+            turns.finish(turn)
+            if turn.steps:
+                turns.start(turn)
+    while len(one.steps) > 1 or two.steps:
         for chain in (one, two):
-            if chain.steps:
+            if len(chain.steps) > 1 or chain is two and chain.steps:
                 turns.finish(chain)
                 if chain.steps:
                     turns.start(chain)
-                if chain.steps and chain.steps[0][0] == "last":
-                    turns.run(scaling(chain))
-    while work:
-        turns.run(work.pop(0))
+    turns.run(own_half)
+    turns.finish(one)
     shape = (3, 3, chans, chans)
     return (
         results[0].reshape(rows, cols, chans),

time: 75 us -> 73.9 us (0.985)
  waiting for transfers between devices: 5.97 us -> 19.1 us
  starting transfers between devices: 34.8 us -> 25.8 us
  Pallas kernels: 32.9 us -> 27.9 us
    ppermute x20, waiting for transfers between devices: 4.3 us -> 19.1 us  [start(): self.got = [lax.ppermute(x, BOTH, p) for x, p in zip(sent, pairs)]]
    ppermute x20, starting transfers between devices: 29.1 us -> 20.9 us  [start(): self.got = [lax.ppermute(x, BOTH, p) for x, p in zip(sent, pairs)]]
    pallas_call x25 -> x24, Pallas kernels: 32.9 us -> 27.9 us  [kernel_call(): pl.pallas_call(body, out_shape=out_shape, in_specs=in_specs, out_specs=ou...]
    ppermute x2 -> x0, waiting for transfers between devices: 1.66 us -> none  [the longest x1 0.89 us: shards(): got_far = lax.ppermute(side_far, 'lon', far_lon)]
    ppermute x2 -> x0, starting transfers between devices: 0.96 us -> none  [the longest x1 0.96 us: shards(): got_near = lax.ppermute(side_near, 'lon', near_lon)]
  transfers between devices with their start and end apart: 26 -> 24, of which waited for: 6 -> 10; matrix products, arithmetic and copies ran while one was open for 0% -> 0% of each run, Pallas kernels for 36% -> 30%
where the time goes in v2:
time: 73.9 us; the launch traced here: 73.7 us
  Pallas kernels  27.9 us (38%)
  starting transfers between devices  25.8 us (35%)
  waiting for transfers between devices  19.1 us (26%)
  between operations  1.05 us (1%)
    pallas_call x24, Pallas kernels, kernel_call(): pl.pallas_call(body, out_shape=out_shape, in_specs=in_specs, out_specs=ou...  27.9 us
    ppermute x20, starting transfers between devices, start(): self.got = [lax.ppermute(x, BOTH, p) for x, p in zip(sent, pairs)]  20.9 us
    ppermute x20, waiting for transfers between devices, start(): self.got = [lax.ppermute(x, BOTH, p) for x, p in zip(sent, pairs)]  19.1 us
    ppermute x1, starting transfers between devices, shards(): lon_far = lax.ppermute(far, 'lon', far_lon)  2.71 us
  transfers between devices with their start and end apart: 24, of which 10 were waited for; matrix products, arithmetic and copies ran while one was open for 0% of the time, Pallas kernels for 30%

profile of v2, /device:TPU:1, one launch (start us, length us, event | category | flops | bytes accessed | tf_op | source)
XLA Modules:
  0.0 73.7 jit_solution(6973321614927763313)
XLA Ops:
  0.6 1.7 %ends.1 = (bf16[2048,256]{1,0:T(8,128)(2,1)S(1)}, bf16[2048,256]{1,0:T(8,128)(2,1)S(1)}, bf16[128,256]{1,0:T(8,128)(2,1)S(1)}, bf16[128,256]{1,0:T(8,128)(2,1)S(1)}) custom-call(bf16[2048,256]{1,0:T(8,128)(2,1)} %bitcast.10, bf16[2048,256]{1,0:T(8,128)(2,1)} %bitcast.11), custom_call_target="tpu_custom_call" | custom-call | bytes 2097152 | tf_op jit(solution)/shard_map/ends/pallas_call | solution.py:38
  2.4 2.7 %collective-permute-start.1 = (bf16[128,256]{1,0:T(8,128)(2,1)S(1)}, bf16[128,256]{1,0:T(8,128)(2,1)S(1)}, u32[]{:S(2)}, u32[]{:S(2)}) collective-permute-start(bf16[128,256]{1,0:T(8,128)(2,1)S(1)} %get-tuple-element.89.own_far), channel_id=1, source_target_pairs={{1,2},{2,1},{3,4},{4,3},{5,6},{6,5},{7,0},{0,7},{9,10},{10,9},{11,... | collective-permute-start | bytes 196616 | tf_op jit(solution)/shard_map/ppermute | solution.py:622
  5.1 2.3 %prep.1 = (bf16[2176,768]{1,0:T(8,128)(2,1)S(1)}, bf16[2176,768]{1,0:T(8,128)(2,1)S(1)}, bf16[2304,256]{1,0:T(8,128)(2,1)S(1)}, bf16[2304,256]{1,0:T(8,128)(2,1)...) custom-call(bf16[2048,256]{1,0:T(8,128)(2,1)S(1)} %get-tuple-element.90.field.refs_3_, ...), custom_call_target="tpu_custom_call" | custom-call | flops 2415919104 | bytes 4456448 | tf_op jit(solution)/shard_map/prep/pallas_call | solution.py:38
  7.5 1.4 %collective-permute-start.2 = (bf16[272,256]{1,0:T(8,128)(2,1)S(1)}, bf16[272,256]{1,0:T(8,128)(2,1)S(1)}, u32[]{:S(2)}, u32[]{:S(2)}) collective-permute-start(bf16[272,256]{1,0:T(8,128)(2,1)S(1)} %get-tuple-element.95), channel_id=1, source_target_pairs={{0,8},{8,0},{16,24},{24,16},{1,9},{9,1},{17,25},{25,17},{2,10},{10... | collective-permute-start | bytes 417800 | tf_op jit(solution)/shard_map/ppermute | solution.py:638
  9.6 5.4 %inner_rows.1 = (bf16[2176,768]{1,0:T(8,128)(2,1)S(1)}, bf16[2176,768]{1,0:T(8,128)(2,1)S(1)}, f32[2176,256]{1,0:T(8,128)S(1)}, bf16[2176,256]{1,0:T(8,128)(2,1)...) custom-call(bf16[128,256]{1,0:T(8,128)(2,1)S(1)} %collective-permute, ...), custom_call_target="tpu_custom_call", output_to_operand_aliasing={{0}: (4, {}), {1}: (5, {})} | custom-call | flops 4831838208 | bytes 9175040 | tf_op jit(solution)/shard_map/inner_rows/pallas_call | solution.py:38
  15.0 3.2 %grad_two.1 = (bf16[2176,768]{1,0:T(8,128)(2,1)S(1)}, bf16[2176,768]{1,0:T(8,128)(2,1)S(1)}, f32[2176,256]{1,0:T(8,128)S(1)}, bf16[2176,256]{1,0:T(8,128)(2,1)S(...) custom-call(bf16[272,256]{1,0:T(8,128)(2,1)S(1)} %collective-permute, ...), custom_call_target="tpu_custom_call", output_to_operand_aliasing={{0}: (3, {}), {1}: (4, {}), {2}: (5, {}), {3}: (6, {}), {4}... | custom-call | flops 2415919104 | bytes 12533760 | tf_op jit(solution)/shard_map/grad_two/pallas_call | solution.py:38
  18.2 2.7 %collective-permute-start.5 = (bf16[1152,256]{1,0:T(8,128)(2,1)S(1)}, bf16[1152,256]{1,0:T(8,128)(2,1)S(1)}, u32[]{:S(2)}, u32[]{:S(2)}) collective-permute-start(bf16[1152,256]{1,0:T(8,128)(2,1)S(1)} %get-tuple-element.106), channel_id=1, source_target_pairs={{0,1},{1,0},{2,3},{3,2},{4,5},{5,4},{6,7},{7,6},{8,9},{9,8},{10,11... | collective-permute-start | bytes 1769480 | tf_op jit(solution)/shard_map/ppermute | solution.py:534
  20.9 3.3 %grad_one.1 = (bf16[2176,256]{1,0:T(8,128)(2,1)S(1)}, f32[2304,128]{1,0:T(8,128)S(1)}, bf16[2304,128]{1,0:T(8,128)(2,1)S(1)}) custom-call(bf16[272,256]{1,0:T(8,128)(2,1)S(1)} %collective-permute-done.2.near.lat_near, bf16[272,256]{1,0:T(8,128)(2,1)S(1)} %collective-permute-done.3.far.lat_far, ...), custom_call_target="tpu_custom_call", output_to_operand_aliasing={{0}: (6, {})} | custom-call | flops 2415919104 | bytes 11485184 | tf_op jit(solution)/shard_map/grad_one/pallas_call | solution.py:38
  24.4 3.0 %collective-permute-start.6 = (bf16[288,256]{1,0:T(8,128)(2,1)S(1)}, bf16[288,256]{1,0:T(8,128)(2,1)S(1)}, u32[]{:S(2)}, u32[]{:S(2)}) collective-permute-start(bf16[288,256]{1,0:T(8,128)(2,1)S(1)} %get-tuple-element.121), channel_id=1, source_target_pairs={{0,8},{1,17},{2,10},{3,19},{4,12},{5,21},{6,14},{7,23},{8,0},{9,25... | collective-permute-start | bytes 442376 | tf_op jit(solution)/shard_map/ppermute | solution.py:534
  33.2 4.0 %collective-permute-done.8.rest_2_ = bf16[288,256]{1,0:T(8,128)(2,1)S(1)} collective-permute-done((bf16[288,256]{1,0:T(8,128)(2,1)S(1)}, bf16[288,256]{1,0:T(8,128)(2,1)S(1)}, u32[]{:S(2)}, u32[]{:S(2)}) %collective-permute-start.8) | collective-permute-done | bytes 147488 | tf_op jit(solution)/shard_map/ppermute | solution.py:534
  37.3 1.7 %field_out.2.refs_5_ = bf16[1024,256]{1,0:T(8,128)(2,1)S(1)} custom-call(f32[80,256]{1,0:T(8,128)S(1)} %get-tuple-element.135.edges.refs_0_, bf16[2176,256]{1,0:T(8,128)(2,1)S(1)} %get-tuple-element.147.value.refs_1_, bf16[2304,256]{1,0:T(8,128)(2,1)S(1)} %get-tuple-element.142.weights.refs_2_, bf16[2048,256]{1,0:T(8,128)(2,1)S(1)} %get-tuple-element.90.field.refs_3_, ...), custom_call_target="tpu_custom_call" | custom-call | flops 1207959552 | bytes 4472832 | tf_op jit(solution)/shard_map/field_out/pallas_call | solution.py:38
  39.1 4.3 %collective-permute-done.12.rest_2_ = bf16[576,128]{1,0:T(8,128)(2,1)S(1)} collective-permute-done((bf16[576,128]{1,0:T(8,128)(2,1)S(1)}, bf16[576,128]{1,0:T(8,128)(2,1)S(1)}, u32[]{:S(2)}, u32[]{:S(2)}) %collective-permute-start.12) | collective-permute-done | bytes 147488 | tf_op jit(solution)/shard_map/ppermute | solution.py:534
  43.9 2.1 %collective-permute-start.13 = (bf16[288,256]{1,0:T(8,128)(2,1)S(1)}, bf16[288,256]{1,0:T(8,128)(2,1)S(1)}, u32[]{:S(2)}, u32[]{:S(2)}) collective-permute-start(bf16[288,256]{1,0:T(8,128)(2,1)S(1)} %add.8.own), channel_id=1, source_target_pairs={{0,4},{1,3},{2,6},{3,1},{4,0},{5,7},{6,2},{7,5},{8,12},{9,11},{10,... | collective-permute-start | bytes 442376 | tf_op jit(solution)/shard_map/ppermute | solution.py:534
  46.0 1.9 %field_out.3 = (bf16[1024,256]{1,0:T(8,128)(2,1)S(1)}, bf16[2048,256]{1,0:T(8,128)(2,1)}) custom-call(f32[80,256]{1,0:T(8,128)S(1)} %get-tuple-element.135.edges.refs_0_, bf16[2176,256]{1,0:T(8,128)(2,1)S(1)} %get-tuple-element.147.value.refs_1_, bf16[2304,256]{1,0:T(8,128)(2,1)S(1)} %get-tuple-element.142.weights.refs_2_, ...), custom_call_target="tpu_custom_call" | custom-call | flops 1207959552 | bytes 4997120 | tf_op jit(solution)/shard_map/field_out/pallas_call | solution.py:38
  47.9 2.2 %collective-permute-done.14.rest_0_ = bf16[576,128]{1,0:T(8,128)(2,1)S(1)} collective-permute-done((bf16[576,128]{1,0:T(8,128)(2,1)S(1)}, bf16[576,128]{1,0:T(8,128)(2,1)S(1)}, u32[]{:S(2)}, u32[]{:S(2)}) %collective-permute-start.14) | collective-permute-done | bytes 147488 | tf_op jit(solution)/shard_map/ppermute | solution.py:534
  50.2 3.2 %collective-permute-done.13.rest_0_ = bf16[288,256]{1,0:T(8,128)(2,1)S(1)} collective-permute-done((bf16[288,256]{1,0:T(8,128)(2,1)S(1)}, bf16[288,256]{1,0:T(8,128)(2,1)S(1)}, u32[]{:S(2)}, u32[]{:S(2)}) %collective-permute-start.13) | collective-permute-done | bytes 147488 | tf_op jit(solution)/shard_map/ppermute | solution.py:534
  55.0 1.2 %collective-permute-start.19 = (bf16[288,256]{1,0:T(8,128)(2,1)S(1)}, bf16[288,256]{1,0:T(8,128)(2,1)S(1)}, u32[]{:S(2)}, u32[]{:S(2)}) collective-permute-start(bf16[288,256]{1,0:T(8,128)(2,1)S(1)} %add.10.value), channel_id=1, source_target_pairs={{0,8},{1,17},{2,10},{3,19},{4,12},{5,21},{6,14},{7,23},{8,0},{9,25... | collective-permute-start | bytes 442376 | tf_op jit(solution)/shard_map/ppermute | solution.py:534
  56.2 2.0 %grad_in.2 = (bf16[1024,256]{1,0:T(8,128)(2,1)S(1)}, bf16[2048,256]{1,0:T(8,128)(2,1)}) custom-call(f32[80,256]{1,0:T(8,128)S(1)} %get-tuple-element.133.refs_0_, bf16[2176,256]{1,0:T(8,128)(2,1)S(1)} %get-tuple-element.160.refs_1_, bf16[2304,256]{1,0:T(8,128)(2,1)S(1)} %get-tuple-element.153.refs_2_, ...), custom_call_target="tpu_custom_call", output_to_operand_aliasing={{1}: (6, {})} | custom-call | flops 1207959552 | bytes 6045696 | tf_op jit(solution)/shard_map/grad_in/pallas_call | solution.py:38
  59.7 1.2 %collective-permute-start.16 = (bf16[576,128]{1,0:T(8,128)(2,1)S(1)}, bf16[576,128]{1,0:T(8,128)(2,1)S(1)}, u32[]{:S(2)}, u32[]{:S(2)}) collective-permute-start(bf16[576,128]{1,0:T(8,128)(2,1)S(1)} %add.11.value), channel_id=1, source_target_pairs={{0,8},{1,17},{2,10},{3,19},{4,12},{5,21},{6,14},{7,23},{8,0},{9,25... | collective-permute-start | bytes 442376 | tf_op jit(solution)/shard_map/ppermute | solution.py:534
  61.5 2.6 %collective-permute-done.19.rest_0_ = bf16[288,256]{1,0:T(8,128)(2,1)S(1)} collective-permute-done((bf16[288,256]{1,0:T(8,128)(2,1)S(1)}, bf16[288,256]{1,0:T(8,128)(2,1)S(1)}, u32[]{:S(2)}, u32[]{:S(2)}) %collective-permute-start.19) | collective-permute-done | bytes 147488 | tf_op jit(solution)/shard_map/ppermute | solution.py:534
  64.2 1.9 %collective-permute-start.22 = (bf16[1152,256]{1,0:T(8,128)(2,1)S(1)}, bf16[1152,256]{1,0:T(8,128)(2,1)S(1)}, u32[]{:S(2)}, u32[]{:S(2)}) collective-permute-start(bf16[1152,256]{1,0:T(8,128)(2,1)S(1)} %join.2.own), channel_id=1, source_target_pairs={{0,1},{1,0},{2,3},{3,2},{4,5},{5,4},{6,7},{7,6},{8,9},{9,8},{10,11... | collective-permute-start | bytes 1769480 | tf_op jit(solution)/shard_map/ppermute | solution.py:534
  66.1 2.0 %grad_in.3 = (bf16[1024,256]{1,0:T(8,128)(2,1)S(1)}, bf16[2048,256]{1,0:T(8,128)(2,1)}) custom-call(f32[80,256]{1,0:T(8,128)S(1)} %get-tuple-element.133.refs_0_, bf16[2176,256]{1,0:T(8,128)(2,1)S(1)} %get-tuple-element.160.refs_1_, bf16[2304,256]{1,0:T(8,128)(2,1)S(1)} %get-tuple-element.153.refs_2_, bf16[2048,256]{1,0:T(8,128)(2,1)S(1)} %get-tuple-element.90.field.refs_3_, ...), custom_call_target="tpu_custom_call" | custom-call | flops 1207959552 | bytes 4997120 | tf_op jit(solution)/shard_map/grad_in/pallas_call | solution.py:38
  68.1 1.5 %collective-permute-done.16.rest_0_ = bf16[576,128]{1,0:T(8,128)(2,1)S(1)} collective-permute-done((bf16[576,128]{1,0:T(8,128)(2,1)S(1)}, bf16[576,128]{1,0:T(8,128)(2,1)S(1)}, u32[]{:S(2)}, u32[]{:S(2)}) %collective-permute-start.16) | collective-permute-done | bytes 147488 | tf_op jit(solution)/shard_map/ppermute | solution.py:534
  70.5 2.0 %scaled.4 = (f32[2304,256]{1,0:T(8,128)}, bf16[2048,256]{1,0:T(8,128)(2,1)}, f32[2304,256]{1,0:T(8,128)}) custom-call(bf16[2304,128]{1,0:T(8,128)(2,1)S(1)} %join.3.refs_0_, bf16[1024,256]{1,0:T(8,128)(2,1)S(1)} %get-tuple-element.161.refs_1_, bf16[2048,256]{1,0:T(8,128)(2,1)} %get-tuple-element.162.refs_2_, ...), custom_call_target="tpu_custom_call", output_to_operand_aliasing={{1}: (2, {})} | custom-call | bytes 4521984 | tf_op jit(solution)/shard_map/scaled/pallas_call | solution.py:38
  (48 shorter events, 13.2 us)
Async XLA Ops:
  2.3 5.1 %collective-permute-start = (bf16[128,256]{1,0:T(8,128)(2,1)S(1)}, bf16[128,256]{1,0:T(8,128)(2,1)S(1)}, u32[]{:S(2)}, u32[]{:S(2)}) collective-permute-start(bf16[128,256]{1,0:T(8,128)(2,1)S(1)} %get-tuple-element.88.own_near), channel_id=1, source_target_pairs={{0,1},{1,0},{2,3},{3,2},{4,5},{5,4},{6,7},{7,6},{8,9},{9,8},{10,11... | collective-permute-start | bytes 196616 | tf_op jit(solution)/shard_map/ppermute | solution.py:621
  2.4 5.0 %collective-permute-start.1 = (bf16[128,256]{1,0:T(8,128)(2,1)S(1)}, bf16[128,256]{1,0:T(8,128)(2,1)S(1)}, u32[]{:S(2)}, u32[]{:S(2)}) collective-permute-start(bf16[128,256]{1,0:T(8,128)(2,1)S(1)} %get-tuple-element.89.own_far), channel_id=1, source_target_pairs={{1,2},{2,1},{3,4},{4,3},{5,6},{6,5},{7,0},{0,7},{9,10},{10,9},{11,... | collective-permute-start | bytes 196616 | tf_op jit(solution)/shard_map/ppermute | solution.py:622
  7.5 7.5 %collective-permute-start.2 = (bf16[272,256]{1,0:T(8,128)(2,1)S(1)}, bf16[272,256]{1,0:T(8,128)(2,1)S(1)}, u32[]{:S(2)}, u32[]{:S(2)}) collective-permute-start(bf16[272,256]{1,0:T(8,128)(2,1)S(1)} %get-tuple-element.95), channel_id=1, source_target_pairs={{0,8},{8,0},{16,24},{24,16},{1,9},{9,1},{17,25},{25,17},{2,10},{10... | collective-permute-start | bytes 417800 | tf_op jit(solution)/shard_map/ppermute | solution.py:638
  8.9 6.1 %collective-permute-start.3 = (bf16[272,256]{1,0:T(8,128)(2,1)S(1)}, bf16[272,256]{1,0:T(8,128)(2,1)S(1)}, u32[]{:S(2)}, u32[]{:S(2)}) collective-permute-start(bf16[272,256]{1,0:T(8,128)(2,1)S(1)} %get-tuple-element.96), channel_id=1, source_target_pairs={{8,16},{16,8},{9,17},{17,9},{10,18},{18,10},{11,19},{19,11},{12,20... | collective-permute-start | bytes 417800 | tf_op jit(solution)/shard_map/ppermute | solution.py:639
  18.2 6.1 %collective-permute-start.5 = (bf16[1152,256]{1,0:T(8,128)(2,1)S(1)}, bf16[1152,256]{1,0:T(8,128)(2,1)S(1)}, u32[]{:S(2)}, u32[]{:S(2)}) collective-permute-start(bf16[1152,256]{1,0:T(8,128)(2,1)S(1)} %get-tuple-element.106), channel_id=1, source_target_pairs={{0,1},{1,0},{2,3},{3,2},{4,5},{5,4},{6,7},{7,6},{8,9},{9,8},{10,11... | collective-permute-start | bytes 1769480 | tf_op jit(solution)/shard_map/ppermute | solution.py:534
  24.2 5.4 %collective-permute-start.4 = (bf16[2304,128]{1,0:T(8,128)(2,1)S(1)}, bf16[2304,128]{1,0:T(8,128)(2,1)S(1)}, u32[]{:S(2)}, u32[]{:S(2)}) collective-permute-start(bf16[2304,128]{1,0:T(8,128)(2,1)S(1)} %get-tuple-element.115), channel_id=1, source_target_pairs={{0,1},{1,0},{2,3},{3,2},{4,5},{5,4},{6,7},{7,6},{8,9},{9,8},{10,11... | collective-permute-start | bytes 1769480 | tf_op jit(solution)/shard_map/ppermute | solution.py:534
  24.4 6.9 %collective-permute-start.6 = (bf16[288,256]{1,0:T(8,128)(2,1)S(1)}, bf16[288,256]{1,0:T(8,128)(2,1)S(1)}, u32[]{:S(2)}, u32[]{:S(2)}) collective-permute-start(bf16[288,256]{1,0:T(8,128)(2,1)S(1)} %get-tuple-element.121), channel_id=1, source_target_pairs={{0,8},{1,17},{2,10},{3,19},{4,12},{5,21},{6,14},{7,23},{8,0},{9,25... | collective-permute-start | bytes 442376 | tf_op jit(solution)/shard_map/ppermute | solution.py:534
  27.5 5.7 %collective-permute-start.7 = (bf16[288,256]{1,0:T(8,128)(2,1)S(1)}, bf16[288,256]{1,0:T(8,128)(2,1)S(1)}, u32[]{:S(2)}, u32[]{:S(2)}) collective-permute-start(bf16[288,256]{1,0:T(8,128)(2,1)S(1)} %get-tuple-element.122), channel_id=1, source_target_pairs={{0,16},{1,9},{2,18},{3,11},{4,20},{5,13},{6,22},{7,15},{8,24},{9,1... | collective-permute-start | bytes 442376 | tf_op jit(solution)/shard_map/ppermute | solution.py:534
  28.5 8.6 %collective-permute-start.8 = (bf16[288,256]{1,0:T(8,128)(2,1)S(1)}, bf16[288,256]{1,0:T(8,128)(2,1)S(1)}, u32[]{:S(2)}, u32[]{:S(2)}) collective-permute-start(bf16[288,256]{1,0:T(8,128)(2,1)S(1)} %get-tuple-element.123), channel_id=1, source_target_pairs={{0,24},{1,25},{2,26},{3,27},{4,28},{5,29},{6,30},{7,31},{8,16},{9,... | collective-permute-start | bytes 442376 | tf_op jit(solution)/shard_map/ppermute | solution.py:534
  29.7 9.2 %collective-permute-start.10 = (bf16[576,128]{1,0:T(8,128)(2,1)S(1)}, bf16[576,128]{1,0:T(8,128)(2,1)S(1)}, u32[]{:S(2)}, u32[]{:S(2)}) collective-permute-start(bf16[576,128]{1,0:T(8,128)(2,1)S(1)} %get-tuple-element.128), channel_id=1, source_target_pairs={{0,8},{1,17},{2,10},{3,19},{4,12},{5,21},{6,14},{7,23},{8,0},{9,25... | collective-permute-start | bytes 442376 | tf_op jit(solution)/shard_map/ppermute | solution.py:534
  30.3 8.8 %collective-permute-start.11 = (bf16[576,128]{1,0:T(8,128)(2,1)S(1)}, bf16[576,128]{1,0:T(8,128)(2,1)S(1)}, u32[]{:S(2)}, u32[]{:S(2)}) collective-permute-start(bf16[576,128]{1,0:T(8,128)(2,1)S(1)} %get-tuple-element.129), channel_id=1, source_target_pairs={{0,16},{1,9},{2,18},{3,11},{4,20},{5,13},{6,22},{7,15},{8,24},{9,1... | collective-permute-start | bytes 442376 | tf_op jit(solution)/shard_map/ppermute | solution.py:534
  31.4 12.1 %collective-permute-start.12 = (bf16[576,128]{1,0:T(8,128)(2,1)S(1)}, bf16[576,128]{1,0:T(8,128)(2,1)S(1)}, u32[]{:S(2)}, u32[]{:S(2)}) collective-permute-start(bf16[576,128]{1,0:T(8,128)(2,1)S(1)} %get-tuple-element.130), channel_id=1, source_target_pairs={{0,24},{1,25},{2,26},{3,27},{4,28},{5,29},{6,30},{7,31},{8,16},{9,... | collective-permute-start | bytes 442376 | tf_op jit(solution)/shard_map/ppermute | solution.py:534
  37.2 6.6 %collective-permute-start.9 = (bf16[288,256]{1,0:T(8,128)(2,1)S(1)}, bf16[288,256]{1,0:T(8,128)(2,1)S(1)}, u32[]{:S(2)}, u32[]{:S(2)}) collective-permute-start(bf16[288,256]{1,0:T(8,128)(2,1)S(1)} %add.6.own), channel_id=1, source_target_pairs={{0,2},{1,5},{2,0},{3,7},{4,6},{5,1},{6,4},{7,3},{8,10},{9,13},{10,... | collective-permute-start | bytes 442376 | tf_op jit(solution)/shard_map/ppermute | solution.py:534
  43.5 6.6 %collective-permute-start.14 = (bf16[576,128]{1,0:T(8,128)(2,1)S(1)}, bf16[576,128]{1,0:T(8,128)(2,1)S(1)}, u32[]{:S(2)}, u32[]{:S(2)}) collective-permute-start(bf16[576,128]{1,0:T(8,128)(2,1)S(1)} %add.7.own), channel_id=1, source_target_pairs={{0,2},{1,5},{2,0},{3,7},{4,6},{5,1},{6,4},{7,3},{8,10},{9,13},{10,... | collective-permute-start | bytes 442376 | tf_op jit(solution)/shard_map/ppermute | solution.py:534
  43.9 9.5 %collective-permute-start.13 = (bf16[288,256]{1,0:T(8,128)(2,1)S(1)}, bf16[288,256]{1,0:T(8,128)(2,1)S(1)}, u32[]{:S(2)}, u32[]{:S(2)}) collective-permute-start(bf16[288,256]{1,0:T(8,128)(2,1)S(1)} %add.8.own), channel_id=1, source_target_pairs={{0,4},{1,3},{2,6},{3,1},{4,0},{5,7},{6,2},{7,5},{8,12},{9,11},{10,... | collective-permute-start | bytes 442376 | tf_op jit(solution)/shard_map/ppermute | solution.py:534
  50.1 8.0 %collective-permute-start.15 = (bf16[576,128]{1,0:T(8,128)(2,1)S(1)}, bf16[576,128]{1,0:T(8,128)(2,1)S(1)}, u32[]{:S(2)}, u32[]{:S(2)}) collective-permute-start(bf16[576,128]{1,0:T(8,128)(2,1)S(1)} %add.9.own), channel_id=1, source_target_pairs={{0,4},{1,3},{2,6},{3,1},{4,0},{5,7},{6,2},{7,5},{8,12},{9,11},{10,... | collective-permute-start | bytes 442376 | tf_op jit(solution)/shard_map/ppermute | solution.py:534
  53.5 6.3 %collective-permute-start.21 = (bf16[288,256]{1,0:T(8,128)(2,1)S(1)}, bf16[288,256]{1,0:T(8,128)(2,1)S(1)}, u32[]{:S(2)}, u32[]{:S(2)}) collective-permute-start(bf16[288,256]{1,0:T(8,128)(2,1)S(1)} %add.10.value), channel_id=1, source_target_pairs={{0,24},{1,25},{2,26},{3,27},{4,28},{5,29},{6,30},{7,31},{8,16},{9,... | collective-permute-start | bytes 442376 | tf_op jit(solution)/shard_map/ppermute | solution.py:534
  53.9 7.7 %collective-permute-start.20 = (bf16[288,256]{1,0:T(8,128)(2,1)S(1)}, bf16[288,256]{1,0:T(8,128)(2,1)S(1)}, u32[]{:S(2)}, u32[]{:S(2)}) collective-permute-start(bf16[288,256]{1,0:T(8,128)(2,1)S(1)} %add.10.value), channel_id=1, source_target_pairs={{0,16},{1,9},{2,18},{3,11},{4,20},{5,13},{6,22},{7,15},{8,24},{9,1... | collective-permute-start | bytes 442376 | tf_op jit(solution)/shard_map/ppermute | solution.py:534
  55.0 9.2 %collective-permute-start.19 = (bf16[288,256]{1,0:T(8,128)(2,1)S(1)}, bf16[288,256]{1,0:T(8,128)(2,1)S(1)}, u32[]{:S(2)}, u32[]{:S(2)}) collective-permute-start(bf16[288,256]{1,0:T(8,128)(2,1)S(1)} %add.10.value), channel_id=1, source_target_pairs={{0,8},{1,17},{2,10},{3,19},{4,12},{5,21},{6,14},{7,23},{8,0},{9,25... | collective-permute-start | bytes 442376 | tf_op jit(solution)/shard_map/ppermute | solution.py:534
  58.2 9.9 %collective-permute-start.18 = (bf16[576,128]{1,0:T(8,128)(2,1)S(1)}, bf16[576,128]{1,0:T(8,128)(2,1)S(1)}, u32[]{:S(2)}, u32[]{:S(2)}) collective-permute-start(bf16[576,128]{1,0:T(8,128)(2,1)S(1)} %add.11.value), channel_id=1, source_target_pairs={{0,24},{1,25},{2,26},{3,27},{4,28},{5,29},{6,30},{7,31},{8,16},{9,... | collective-permute-start | bytes 442376 | tf_op jit(solution)/shard_map/ppermute | solution.py:534
  58.6 9.5 %collective-permute-start.17 = (bf16[576,128]{1,0:T(8,128)(2,1)S(1)}, bf16[576,128]{1,0:T(8,128)(2,1)S(1)}, u32[]{:S(2)}, u32[]{:S(2)}) collective-permute-start(bf16[576,128]{1,0:T(8,128)(2,1)S(1)} %add.11.value), channel_id=1, source_target_pairs={{0,16},{1,9},{2,18},{3,11},{4,20},{5,13},{6,22},{7,15},{8,24},{9,1... | collective-permute-start | bytes 442376 | tf_op jit(solution)/shard_map/ppermute | solution.py:534
  59.7 9.9 %collective-permute-start.16 = (bf16[576,128]{1,0:T(8,128)(2,1)S(1)}, bf16[576,128]{1,0:T(8,128)(2,1)S(1)}, u32[]{:S(2)}, u32[]{:S(2)}) collective-permute-start(bf16[576,128]{1,0:T(8,128)(2,1)S(1)} %add.11.value), channel_id=1, source_target_pairs={{0,8},{1,17},{2,10},{3,19},{4,12},{5,21},{6,14},{7,23},{8,0},{9,25... | collective-permute-start | bytes 442376 | tf_op jit(solution)/shard_map/ppermute | solution.py:534
  64.2 6.1 %collective-permute-start.22 = (bf16[1152,256]{1,0:T(8,128)(2,1)S(1)}, bf16[1152,256]{1,0:T(8,128)(2,1)S(1)}, u32[]{:S(2)}, u32[]{:S(2)}) collective-permute-start(bf16[1152,256]{1,0:T(8,128)(2,1)S(1)} %join.2.own), channel_id=1, source_target_pairs={{0,1},{1,0},{2,3},{3,2},{4,5},{5,4},{6,7},{7,6},{8,9},{9,8},{10,11... | collective-permute-start | bytes 1769480 | tf_op jit(solution)/shard_map/ppermute | solution.py:534
  69.7 2.8 %collective-permute-start.23 = (bf16[2304,128]{1,0:T(8,128)(2,1)S(1)}, bf16[2304,128]{1,0:T(8,128)(2,1)S(1)}, u32[]{:S(2)}, u32[]{:S(2)}) collective-permute-start(bf16[2304,128]{1,0:T(8,128)(2,1)S(1)} %join.3.refs_0_), channel_id=1, source_target_pairs={{0,1},{1,0},{2,3},{3,2},{4,5},{5,4},{6,7},{7,6},{8,9},{9,8},{10,11... | collective-permute-start | bytes 1769480 | tf_op jit(solution)/shard_map/ppermute | solution.py:534

commit v3 on v2

--- a/solution.py
+++ b/solution.py
@@ -162,7 +162,7 @@
         put_shifted(cot3, to, cot[pl.ds(at, cols), :].astype(F32), cols)
         return carry
 
-    lax.fori_loop(0, rows, body, 0, unroll=2)
+    lax.fori_loop(0, rows, body, 0, unroll=4)
     for copy in copies:
         copy.wait()
     for tap in range(9):
@@ -618,7 +618,6 @@
         [in_hbm(field_in.reshape(cells, chans)), in_hbm(cotangent.reshape(cells, chans))],
         scratch=[pltpu.VMEM((8 * rows, chans), F32), sems],
     )
-    lon_near = lax.ppermute(near, "lon", near_lon)
     lon_far = lax.ppermute(far, "lon", far_lon)
     wide = ((tall, 3 * chans), BF16)
     square = ((9 * chans, chans), BF16)
@@ -630,6 +629,8 @@
         flops=flops,
         scratch=[sems],
     )
+
+    lon_near = lax.ppermute(after([near], act3)[0], "lon", near_lon)
 
     strip = ((4 * cols + 16, chans), BF16)
     send_near, send_far = call(

time: 73.9 us -> 73.6 us (level)
  waiting for transfers between devices: 19.1 us -> 17.4 us
  starting transfers between devices: 25.8 us -> 27.1 us
    ppermute x20, waiting for transfers between devices: 19.1 us -> 16.4 us  [start(): self.got = [lax.ppermute(x, BOTH, p) for x, p in zip(sent, pairs)]]
    ppermute x1, starting transfers between devices: 0.12 us -> 1.92 us  [shards(): lon_near = lax.ppermute(after([near], act3)[0], 'lon', near_lon)]
    ppermute x1, waiting for transfers between devices: 0.01 us -> 0.9 us  [shards(): lon_near = lax.ppermute(after([near], act3)[0], 'lon', near_lon)]
where the time goes in v3:
time: 73.6 us; the launch traced here: 73.5 us
  Pallas kernels  28 us (38%)
  starting transfers between devices  27.1 us (37%)
  waiting for transfers between devices  17.4 us (24%)
  between operations  1.02 us (1%)
    pallas_call x24, Pallas kernels, kernel_call(): pl.pallas_call(body, out_shape=out_shape, in_specs=in_specs, out_specs=ou...  28 us
    ppermute x20, starting transfers between devices, start(): self.got = [lax.ppermute(x, BOTH, p) for x, p in zip(sent, pairs)]  20.5 us
    ppermute x20, waiting for transfers between devices, start(): self.got = [lax.ppermute(x, BOTH, p) for x, p in zip(sent, pairs)]  16.4 us
    ppermute x1, starting transfers between devices, shards(): lon_far = lax.ppermute(far, 'lon', far_lon)  2.75 us
    ppermute x1, starting transfers between devices, shards(): lon_near = lax.ppermute(after([near], act3)[0], 'lon', near_lon)  1.92 us
  transfers between devices with their start and end apart: 24, of which 10 were waited for; matrix products, arithmetic and copies ran while one was open for 0% of the time, Pallas kernels for 30%

profile of v3, /device:TPU:1, one launch (start us, length us, event | category | flops | bytes accessed | tf_op | source)
XLA Modules:
  0.0 73.5 jit_solution(3540614669393461833)
XLA Ops:
  0.6 1.7 %ends.1 = (bf16[2048,256]{1,0:T(8,128)(2,1)S(1)}, bf16[2048,256]{1,0:T(8,128)(2,1)S(1)}, bf16[128,256]{1,0:T(8,128)(2,1)S(1)}, bf16[128,256]{1,0:T(8,128)(2,1)S(1)}) custom-call(bf16[2048,256]{1,0:T(8,128)(2,1)} %bitcast.10, bf16[2048,256]{1,0:T(8,128)(2,1)} %bitcast.11), custom_call_target="tpu_custom_call" | custom-call | bytes 2097152 | tf_op jit(solution)/shard_map/ends/pallas_call | solution.py:38
  2.3 2.8 %collective-permute-start.1 = (bf16[128,256]{1,0:T(8,128)(2,1)S(1)}, bf16[128,256]{1,0:T(8,128)(2,1)S(1)}, u32[]{:S(2)}, u32[]{:S(2)}) collective-permute-start(bf16[128,256]{1,0:T(8,128)(2,1)S(1)} %get-tuple-element.90.own_far), channel_id=1, source_target_pairs={{1,2},{2,1},{3,4},{4,3},{5,6},{6,5},{7,0},{0,7},{9,10},{10,9},{11,... | collective-permute-start | bytes 196616 | tf_op jit(solution)/shard_map/ppermute | solution.py:621
  5.1 2.4 %prep.1 = (bf16[2176,768]{1,0:T(8,128)(2,1)S(1)}, bf16[2176,768]{1,0:T(8,128)(2,1)S(1)}, bf16[2304,256]{1,0:T(8,128)(2,1)S(1)}, bf16[2304,256]{1,0:T(8,128)(2,1)...) custom-call(bf16[2048,256]{1,0:T(8,128)(2,1)S(1)} %get-tuple-element.91.field.refs_3_, ...), custom_call_target="tpu_custom_call" | custom-call | flops 2415919104 | bytes 4456448 | tf_op jit(solution)/shard_map/prep/pallas_call | solution.py:38
  7.5 1.9 %collective-permute-start = (bf16[128,256]{1,0:T(8,128)(2,1)S(1)}, bf16[128,256]{1,0:T(8,128)(2,1)S(1)}, u32[]{:S(2)}, u32[]{:S(2)}) collective-permute-start(bf16[128,256]{1,0:T(8,128)(2,1)S(1)} %get-tuple-element.94.own_near), channel_id=1, source_target_pairs={{0,1},{1,0},{2,3},{3,2},{4,5},{5,4},{6,7},{7,6},{8,9},{9,8},{10,11... | collective-permute-start | bytes 196616 | tf_op jit(solution)/shard_map/ppermute | solution.py:633
  10.3 1.3 %collective-permute-start.2 = (bf16[272,256]{1,0:T(8,128)(2,1)S(1)}, bf16[272,256]{1,0:T(8,128)(2,1)S(1)}, u32[]{:S(2)}, u32[]{:S(2)}) collective-permute-start(bf16[272,256]{1,0:T(8,128)(2,1)S(1)} %get-tuple-element.97), channel_id=1, source_target_pairs={{0,8},{8,0},{16,24},{24,16},{1,9},{9,1},{17,25},{25,17},{2,10},{10... | collective-permute-start | bytes 417800 | tf_op jit(solution)/shard_map/ppermute | solution.py:639
  12.3 5.4 %inner_rows.1 = (bf16[2176,768]{1,0:T(8,128)(2,1)S(1)}, bf16[2176,768]{1,0:T(8,128)(2,1)S(1)}, f32[2176,256]{1,0:T(8,128)S(1)}, bf16[2176,256]{1,0:T(8,128)(2,1)...) custom-call(bf16[128,256]{1,0:T(8,128)(2,1)S(1)} %collective-permute, ...), custom_call_target="tpu_custom_call", output_to_operand_aliasing={{0}: (4, {}), {1}: (5, {})} | custom-call | flops 4831838208 | bytes 9175040 | tf_op jit(solution)/shard_map/inner_rows/pallas_call | solution.py:38
  17.8 3.2 %grad_two.1 = (bf16[2176,768]{1,0:T(8,128)(2,1)S(1)}, bf16[2176,768]{1,0:T(8,128)(2,1)S(1)}, f32[2176,256]{1,0:T(8,128)S(1)}, bf16[2176,256]{1,0:T(8,128)(2,1)S(...) custom-call(bf16[272,256]{1,0:T(8,128)(2,1)S(1)} %collective-permute, ...), custom_call_target="tpu_custom_call", output_to_operand_aliasing={{0}: (3, {}), {1}: (4, {}), {2}: (5, {}), {3}: (6, {}), {4}... | custom-call | flops 2415919104 | bytes 12533760 | tf_op jit(solution)/shard_map/grad_two/pallas_call | solution.py:38
  21.7 3.3 %grad_one.1 = (bf16[2176,256]{1,0:T(8,128)(2,1)S(1)}, f32[2304,128]{1,0:T(8,128)S(1)}, bf16[2304,128]{1,0:T(8,128)(2,1)S(1)}) custom-call(bf16[272,256]{1,0:T(8,128)(2,1)S(1)} %collective-permute-done.2.near.lat_near, bf16[272,256]{1,0:T(8,128)(2,1)S(1)} %collective-permute-done.3.far.lat_far, ...), custom_call_target="tpu_custom_call", output_to_operand_aliasing={{0}: (6, {})} | custom-call | flops 2415919104 | bytes 11485184 | tf_op jit(solution)/shard_map/grad_one/pallas_call | solution.py:38
  25.2 3.4 %collective-permute-start.6 = (bf16[288,256]{1,0:T(8,128)(2,1)S(1)}, bf16[288,256]{1,0:T(8,128)(2,1)S(1)}, u32[]{:S(2)}, u32[]{:S(2)}) collective-permute-start(bf16[288,256]{1,0:T(8,128)(2,1)S(1)} %get-tuple-element.123), channel_id=1, source_target_pairs={{0,8},{1,17},{2,10},{3,19},{4,12},{5,21},{6,14},{7,23},{8,0},{9,25... | collective-permute-start | bytes 442376 | tf_op jit(solution)/shard_map/ppermute | solution.py:534
  34.2 3.4 %collective-permute-done.8.rest_2_ = bf16[288,256]{1,0:T(8,128)(2,1)S(1)} collective-permute-done((bf16[288,256]{1,0:T(8,128)(2,1)S(1)}, bf16[288,256]{1,0:T(8,128)(2,1)S(1)}, u32[]{:S(2)}, u32[]{:S(2)}) %collective-permute-start.8) | collective-permute-done | bytes 147488 | tf_op jit(solution)/shard_map/ppermute | solution.py:534
  38.2 1.7 %field_out.2.refs_5_ = bf16[1024,256]{1,0:T(8,128)(2,1)S(1)} custom-call(f32[80,256]{1,0:T(8,128)S(1)} %get-tuple-element.137.edges.refs_0_, bf16[2176,256]{1,0:T(8,128)(2,1)S(1)} %get-tuple-element.149.value.refs_1_, bf16[2304,256]{1,0:T(8,128)(2,1)S(1)} %get-tuple-element.144.weights.refs_2_, bf16[2048,256]{1,0:T(8,128)(2,1)S(1)} %get-tuple-element.91.field.refs_3_, ...), custom_call_target="tpu_custom_call" | custom-call | flops 1207959552 | bytes 4472832 | tf_op jit(solution)/shard_map/field_out/pallas_call | solution.py:38
  40.2 3.8 %collective-permute-done.12.rest_2_ = bf16[576,128]{1,0:T(8,128)(2,1)S(1)} collective-permute-done((bf16[576,128]{1,0:T(8,128)(2,1)S(1)}, bf16[576,128]{1,0:T(8,128)(2,1)S(1)}, u32[]{:S(2)}, u32[]{:S(2)}) %collective-permute-start.12) | collective-permute-done | bytes 147488 | tf_op jit(solution)/shard_map/ppermute | solution.py:534
  44.6 1.4 %collective-permute-start.13 = (bf16[288,256]{1,0:T(8,128)(2,1)S(1)}, bf16[288,256]{1,0:T(8,128)(2,1)S(1)}, u32[]{:S(2)}, u32[]{:S(2)}) collective-permute-start(bf16[288,256]{1,0:T(8,128)(2,1)S(1)} %add.8.own), channel_id=1, source_target_pairs={{0,4},{1,3},{2,6},{3,1},{4,0},{5,7},{6,2},{7,5},{8,12},{9,11},{10,... | collective-permute-start | bytes 442376 | tf_op jit(solution)/shard_map/ppermute | solution.py:534
  46.0 1.9 %field_out.3 = (bf16[1024,256]{1,0:T(8,128)(2,1)S(1)}, bf16[2048,256]{1,0:T(8,128)(2,1)}) custom-call(f32[80,256]{1,0:T(8,128)S(1)} %get-tuple-element.137.edges.refs_0_, bf16[2176,256]{1,0:T(8,128)(2,1)S(1)} %get-tuple-element.149.value.refs_1_, bf16[2304,256]{1,0:T(8,128)(2,1)S(1)} %get-tuple-element.144.weights.refs_2_, ...), custom_call_target="tpu_custom_call" | custom-call | flops 1207959552 | bytes 4997120 | tf_op jit(solution)/shard_map/field_out/pallas_call | solution.py:38
  47.9 2.4 %collective-permute-done.14.rest_0_ = bf16[576,128]{1,0:T(8,128)(2,1)S(1)} collective-permute-done((bf16[576,128]{1,0:T(8,128)(2,1)S(1)}, bf16[576,128]{1,0:T(8,128)(2,1)S(1)}, u32[]{:S(2)}, u32[]{:S(2)}) %collective-permute-start.14) | collective-permute-done | bytes 147488 | tf_op jit(solution)/shard_map/ppermute | solution.py:534
  50.3 2.8 %collective-permute-done.13.rest_0_ = bf16[288,256]{1,0:T(8,128)(2,1)S(1)} collective-permute-done((bf16[288,256]{1,0:T(8,128)(2,1)S(1)}, bf16[288,256]{1,0:T(8,128)(2,1)S(1)}, u32[]{:S(2)}, u32[]{:S(2)}) %collective-permute-start.13) | collective-permute-done | bytes 147488 | tf_op jit(solution)/shard_map/ppermute | solution.py:534
  53.8 1.5 %collective-permute-start.20 = (bf16[288,256]{1,0:T(8,128)(2,1)S(1)}, bf16[288,256]{1,0:T(8,128)(2,1)S(1)}, u32[]{:S(2)}, u32[]{:S(2)}) collective-permute-start(bf16[288,256]{1,0:T(8,128)(2,1)S(1)} %add.10.value), channel_id=1, source_target_pairs={{0,16},{1,9},{2,18},{3,11},{4,20},{5,13},{6,22},{7,15},{8,24},{9,1... | collective-permute-start | bytes 442376 | tf_op jit(solution)/shard_map/ppermute | solution.py:534
  55.9 2.0 %grad_in.2 = (bf16[1024,256]{1,0:T(8,128)(2,1)S(1)}, bf16[2048,256]{1,0:T(8,128)(2,1)}) custom-call(f32[80,256]{1,0:T(8,128)S(1)} %get-tuple-element.135.refs_0_, bf16[2176,256]{1,0:T(8,128)(2,1)S(1)} %get-tuple-element.162.refs_1_, bf16[2304,256]{1,0:T(8,128)(2,1)S(1)} %get-tuple-element.155.refs_2_, ...), custom_call_target="tpu_custom_call", output_to_operand_aliasing={{1}: (6, {})} | custom-call | flops 1207959552 | bytes 6045696 | tf_op jit(solution)/shard_map/grad_in/pallas_call | solution.py:38
  58.6 1.5 %collective-permute-start.17 = (bf16[576,128]{1,0:T(8,128)(2,1)S(1)}, bf16[576,128]{1,0:T(8,128)(2,1)S(1)}, u32[]{:S(2)}, u32[]{:S(2)}) collective-permute-start(bf16[576,128]{1,0:T(8,128)(2,1)S(1)} %add.11.value), channel_id=1, source_target_pairs={{0,16},{1,9},{2,18},{3,11},{4,20},{5,13},{6,22},{7,15},{8,24},{9,1... | collective-permute-start | bytes 442376 | tf_op jit(solution)/shard_map/ppermute | solution.py:534
  60.9 2.5 %collective-permute-done.19.rest_0_ = bf16[288,256]{1,0:T(8,128)(2,1)S(1)} collective-permute-done((bf16[288,256]{1,0:T(8,128)(2,1)S(1)}, bf16[288,256]{1,0:T(8,128)(2,1)S(1)}, u32[]{:S(2)}, u32[]{:S(2)}) %collective-permute-start.19) | collective-permute-done | bytes 147488 | tf_op jit(solution)/shard_map/ppermute | solution.py:534
  63.4 2.5 %collective-permute-start.22 = (bf16[1152,256]{1,0:T(8,128)(2,1)S(1)}, bf16[1152,256]{1,0:T(8,128)(2,1)S(1)}, u32[]{:S(2)}, u32[]{:S(2)}) collective-permute-start(bf16[1152,256]{1,0:T(8,128)(2,1)S(1)} %join.2.own), channel_id=1, source_target_pairs={{0,1},{1,0},{2,3},{3,2},{4,5},{5,4},{6,7},{7,6},{8,9},{9,8},{10,11... | collective-permute-start | bytes 1769480 | tf_op jit(solution)/shard_map/ppermute | solution.py:534
  65.9 2.0 %grad_in.3 = (bf16[1024,256]{1,0:T(8,128)(2,1)S(1)}, bf16[2048,256]{1,0:T(8,128)(2,1)}) custom-call(f32[80,256]{1,0:T(8,128)S(1)} %get-tuple-element.135.refs_0_, bf16[2176,256]{1,0:T(8,128)(2,1)S(1)} %get-tuple-element.162.refs_1_, bf16[2304,256]{1,0:T(8,128)(2,1)S(1)} %get-tuple-element.155.refs_2_, bf16[2048,256]{1,0:T(8,128)(2,1)S(1)} %get-tuple-element.91.field.refs_3_, ...), custom_call_target="tpu_custom_call" | custom-call | flops 1207959552 | bytes 4997120 | tf_op jit(solution)/shard_map/grad_in/pallas_call | solution.py:38
  68.6 1.4 %collective-permute-start.23 = (bf16[2304,128]{1,0:T(8,128)(2,1)S(1)}, bf16[2304,128]{1,0:T(8,128)(2,1)S(1)}, u32[]{:S(2)}, u32[]{:S(2)}) collective-permute-start(bf16[2304,128]{1,0:T(8,128)(2,1)S(1)} %join.3.refs_0_), channel_id=1, source_target_pairs={{0,1},{1,0},{2,3},{3,2},{4,5},{5,4},{6,7},{7,6},{8,9},{9,8},{10,11... | collective-permute-start | bytes 1769480 | tf_op jit(solution)/shard_map/ppermute | solution.py:534
  70.2 2.0 %scaled.4 = (f32[2304,256]{1,0:T(8,128)}, bf16[2048,256]{1,0:T(8,128)(2,1)}, f32[2304,256]{1,0:T(8,128)}) custom-call(bf16[2304,128]{1,0:T(8,128)(2,1)S(1)} %join.3.refs_0_, bf16[1024,256]{1,0:T(8,128)(2,1)S(1)} %get-tuple-element.163.refs_1_, bf16[2048,256]{1,0:T(8,128)(2,1)} %get-tuple-element.164.refs_2_, ...), custom_call_target="tpu_custom_call", output_to_operand_aliasing={{1}: (2, {})} | custom-call | bytes 4521984 | tf_op jit(solution)/shard_map/scaled/pallas_call | solution.py:38
  (48 shorter events, 14.5 us)
Async XLA Ops:
  2.3 7.1 %collective-permute-start.1 = (bf16[128,256]{1,0:T(8,128)(2,1)S(1)}, bf16[128,256]{1,0:T(8,128)(2,1)S(1)}, u32[]{:S(2)}, u32[]{:S(2)}) collective-permute-start(bf16[128,256]{1,0:T(8,128)(2,1)S(1)} %get-tuple-element.90.own_far), channel_id=1, source_target_pairs={{1,2},{2,1},{3,4},{4,3},{5,6},{6,5},{7,0},{0,7},{9,10},{10,9},{11,... | collective-permute-start | bytes 196616 | tf_op jit(solution)/shard_map/ppermute | solution.py:621
  7.5 2.8 %collective-permute-start = (bf16[128,256]{1,0:T(8,128)(2,1)S(1)}, bf16[128,256]{1,0:T(8,128)(2,1)S(1)}, u32[]{:S(2)}, u32[]{:S(2)}) collective-permute-start(bf16[128,256]{1,0:T(8,128)(2,1)S(1)} %get-tuple-element.94.own_near), channel_id=1, source_target_pairs={{0,1},{1,0},{2,3},{3,2},{4,5},{5,4},{6,7},{7,6},{8,9},{9,8},{10,11... | collective-permute-start | bytes 196616 | tf_op jit(solution)/shard_map/ppermute | solution.py:633
  10.3 7.4 %collective-permute-start.2 = (bf16[272,256]{1,0:T(8,128)(2,1)S(1)}, bf16[272,256]{1,0:T(8,128)(2,1)S(1)}, u32[]{:S(2)}, u32[]{:S(2)}) collective-permute-start(bf16[272,256]{1,0:T(8,128)(2,1)S(1)} %get-tuple-element.97), channel_id=1, source_target_pairs={{0,8},{8,0},{16,24},{24,16},{1,9},{9,1},{17,25},{25,17},{2,10},{10... | collective-permute-start | bytes 417800 | tf_op jit(solution)/shard_map/ppermute | solution.py:639
  11.6 6.1 %collective-permute-start.3 = (bf16[272,256]{1,0:T(8,128)(2,1)S(1)}, bf16[272,256]{1,0:T(8,128)(2,1)S(1)}, u32[]{:S(2)}, u32[]{:S(2)}) collective-permute-start(bf16[272,256]{1,0:T(8,128)(2,1)S(1)} %get-tuple-element.98), channel_id=1, source_target_pairs={{8,16},{16,8},{9,17},{17,9},{10,18},{18,10},{11,19},{19,11},{12,20... | collective-permute-start | bytes 417800 | tf_op jit(solution)/shard_map/ppermute | solution.py:640
  21.0 4.1 %collective-permute-start.5 = (bf16[1152,256]{1,0:T(8,128)(2,1)S(1)}, bf16[1152,256]{1,0:T(8,128)(2,1)S(1)}, u32[]{:S(2)}, u32[]{:S(2)}) collective-permute-start(bf16[1152,256]{1,0:T(8,128)(2,1)S(1)} %get-tuple-element.108), channel_id=1, source_target_pairs={{0,1},{1,0},{2,3},{3,2},{4,5},{5,4},{6,7},{7,6},{8,9},{9,8},{10,11... | collective-permute-start | bytes 1769480 | tf_op jit(solution)/shard_map/ppermute | solution.py:534
  25.0 5.4 %collective-permute-start.4 = (bf16[2304,128]{1,0:T(8,128)(2,1)S(1)}, bf16[2304,128]{1,0:T(8,128)(2,1)S(1)}, u32[]{:S(2)}, u32[]{:S(2)}) collective-permute-start(bf16[2304,128]{1,0:T(8,128)(2,1)S(1)} %get-tuple-element.117), channel_id=1, source_target_pairs={{0,1},{1,0},{2,3},{3,2},{4,5},{5,4},{6,7},{7,6},{8,9},{9,8},{10,11... | collective-permute-start | bytes 1769480 | tf_op jit(solution)/shard_map/ppermute | solution.py:534
  25.2 6.9 %collective-permute-start.6 = (bf16[288,256]{1,0:T(8,128)(2,1)S(1)}, bf16[288,256]{1,0:T(8,128)(2,1)S(1)}, u32[]{:S(2)}, u32[]{:S(2)}) collective-permute-start(bf16[288,256]{1,0:T(8,128)(2,1)S(1)} %get-tuple-element.123), channel_id=1, source_target_pairs={{0,8},{1,17},{2,10},{3,19},{4,12},{5,21},{6,14},{7,23},{8,0},{9,25... | collective-permute-start | bytes 442376 | tf_op jit(solution)/shard_map/ppermute | solution.py:534
  28.6 5.7 %collective-permute-start.7 = (bf16[288,256]{1,0:T(8,128)(2,1)S(1)}, bf16[288,256]{1,0:T(8,128)(2,1)S(1)}, u32[]{:S(2)}, u32[]{:S(2)}) collective-permute-start(bf16[288,256]{1,0:T(8,128)(2,1)S(1)} %get-tuple-element.124), channel_id=1, source_target_pairs={{0,16},{1,9},{2,18},{3,11},{4,20},{5,13},{6,22},{7,15},{8,24},{9,1... | collective-permute-start | bytes 442376 | tf_op jit(solution)/shard_map/ppermute | solution.py:534
  29.3 8.4 %collective-permute-start.8 = (bf16[288,256]{1,0:T(8,128)(2,1)S(1)}, bf16[288,256]{1,0:T(8,128)(2,1)S(1)}, u32[]{:S(2)}, u32[]{:S(2)}) collective-permute-start(bf16[288,256]{1,0:T(8,128)(2,1)S(1)} %get-tuple-element.125), channel_id=1, source_target_pairs={{0,24},{1,25},{2,26},{3,27},{4,28},{5,29},{6,30},{7,31},{8,16},{9,... | collective-permute-start | bytes 442376 | tf_op jit(solution)/shard_map/ppermute | solution.py:534
  30.5 9.5 %collective-permute-start.10 = (bf16[576,128]{1,0:T(8,128)(2,1)S(1)}, bf16[576,128]{1,0:T(8,128)(2,1)S(1)}, u32[]{:S(2)}, u32[]{:S(2)}) collective-permute-start(bf16[576,128]{1,0:T(8,128)(2,1)S(1)} %get-tuple-element.130), channel_id=1, source_target_pairs={{0,8},{1,17},{2,10},{3,19},{4,12},{5,21},{6,14},{7,23},{8,0},{9,25... | collective-permute-start | bytes 442376 | tf_op jit(solution)/shard_map/ppermute | solution.py:534
  31.4 8.8 %collective-permute-start.11 = (bf16[576,128]{1,0:T(8,128)(2,1)S(1)}, bf16[576,128]{1,0:T(8,128)(2,1)S(1)}, u32[]{:S(2)}, u32[]{:S(2)}) collective-permute-start(bf16[576,128]{1,0:T(8,128)(2,1)S(1)} %get-tuple-element.131), channel_id=1, source_target_pairs={{0,16},{1,9},{2,18},{3,11},{4,20},{5,13},{6,22},{7,15},{8,24},{9,1... | collective-permute-start | bytes 442376 | tf_op jit(solution)/shard_map/ppermute | solution.py:534
  32.1 11.9 %collective-permute-start.12 = (bf16[576,128]{1,0:T(8,128)(2,1)S(1)}, bf16[576,128]{1,0:T(8,128)(2,1)S(1)}, u32[]{:S(2)}, u32[]{:S(2)}) collective-permute-start(bf16[576,128]{1,0:T(8,128)(2,1)S(1)} %get-tuple-element.132), channel_id=1, source_target_pairs={{0,24},{1,25},{2,26},{3,27},{4,28},{5,29},{6,30},{7,31},{8,16},{9,... | collective-permute-start | bytes 442376 | tf_op jit(solution)/shard_map/ppermute | solution.py:534
  37.7 6.9 %collective-permute-start.9 = (bf16[288,256]{1,0:T(8,128)(2,1)S(1)}, bf16[288,256]{1,0:T(8,128)(2,1)S(1)}, u32[]{:S(2)}, u32[]{:S(2)}) collective-permute-start(bf16[288,256]{1,0:T(8,128)(2,1)S(1)} %add.6.own), channel_id=1, source_target_pairs={{0,2},{1,5},{2,0},{3,7},{4,6},{5,1},{6,4},{7,3},{8,10},{9,13},{10,... | collective-permute-start | bytes 442376 | tf_op jit(solution)/shard_map/ppermute | solution.py:534
  44.0 6.2 %collective-permute-start.14 = (bf16[576,128]{1,0:T(8,128)(2,1)S(1)}, bf16[576,128]{1,0:T(8,128)(2,1)S(1)}, u32[]{:S(2)}, u32[]{:S(2)}) collective-permute-start(bf16[576,128]{1,0:T(8,128)(2,1)S(1)} %add.7.own), channel_id=1, source_target_pairs={{0,2},{1,5},{2,0},{3,7},{4,6},{5,1},{6,4},{7,3},{8,10},{9,13},{10,... | collective-permute-start | bytes 442376 | tf_op jit(solution)/shard_map/ppermute | solution.py:534
  44.6 8.6 %collective-permute-start.13 = (bf16[288,256]{1,0:T(8,128)(2,1)S(1)}, bf16[288,256]{1,0:T(8,128)(2,1)S(1)}, u32[]{:S(2)}, u32[]{:S(2)}) collective-permute-start(bf16[288,256]{1,0:T(8,128)(2,1)S(1)} %add.8.own), channel_id=1, source_target_pairs={{0,4},{1,3},{2,6},{3,1},{4,0},{5,7},{6,2},{7,5},{8,12},{9,11},{10,... | collective-permute-start | bytes 442376 | tf_op jit(solution)/shard_map/ppermute | solution.py:534
  50.3 7.6 %collective-permute-start.15 = (bf16[576,128]{1,0:T(8,128)(2,1)S(1)}, bf16[576,128]{1,0:T(8,128)(2,1)S(1)}, u32[]{:S(2)}, u32[]{:S(2)}) collective-permute-start(bf16[576,128]{1,0:T(8,128)(2,1)S(1)} %add.9.own), channel_id=1, source_target_pairs={{0,4},{1,3},{2,6},{3,1},{4,0},{5,7},{6,2},{7,5},{8,12},{9,11},{10,... | collective-permute-start | bytes 442376 | tf_op jit(solution)/shard_map/ppermute | solution.py:534
  53.2 6.8 %collective-permute-start.21 = (bf16[288,256]{1,0:T(8,128)(2,1)S(1)}, bf16[288,256]{1,0:T(8,128)(2,1)S(1)}, u32[]{:S(2)}, u32[]{:S(2)}) collective-permute-start(bf16[288,256]{1,0:T(8,128)(2,1)S(1)} %add.10.value), channel_id=1, source_target_pairs={{0,24},{1,25},{2,26},{3,27},{4,28},{5,29},{6,30},{7,31},{8,16},{9,... | collective-permute-start | bytes 442376 | tf_op jit(solution)/shard_map/ppermute | solution.py:534
  53.8 7.1 %collective-permute-start.20 = (bf16[288,256]{1,0:T(8,128)(2,1)S(1)}, bf16[288,256]{1,0:T(8,128)(2,1)S(1)}, u32[]{:S(2)}, u32[]{:S(2)}) collective-permute-start(bf16[288,256]{1,0:T(8,128)(2,1)S(1)} %add.10.value), channel_id=1, source_target_pairs={{0,16},{1,9},{2,18},{3,11},{4,20},{5,13},{6,22},{7,15},{8,24},{9,1... | collective-permute-start | bytes 442376 | tf_op jit(solution)/shard_map/ppermute | solution.py:534
  55.3 8.1 %collective-permute-start.19 = (bf16[288,256]{1,0:T(8,128)(2,1)S(1)}, bf16[288,256]{1,0:T(8,128)(2,1)S(1)}, u32[]{:S(2)}, u32[]{:S(2)}) collective-permute-start(bf16[288,256]{1,0:T(8,128)(2,1)S(1)} %add.10.value), channel_id=1, source_target_pairs={{0,8},{1,17},{2,10},{3,19},{4,12},{5,21},{6,14},{7,23},{8,0},{9,25... | collective-permute-start | bytes 442376 | tf_op jit(solution)/shard_map/ppermute | solution.py:534
  57.9 10.0 %collective-permute-start.18 = (bf16[576,128]{1,0:T(8,128)(2,1)S(1)}, bf16[576,128]{1,0:T(8,128)(2,1)S(1)}, u32[]{:S(2)}, u32[]{:S(2)}) collective-permute-start(bf16[576,128]{1,0:T(8,128)(2,1)S(1)} %add.11.value), channel_id=1, source_target_pairs={{0,24},{1,25},{2,26},{3,27},{4,28},{5,29},{6,30},{7,31},{8,16},{9,... | collective-permute-start | bytes 442376 | tf_op jit(solution)/shard_map/ppermute | solution.py:534
  58.6 9.4 %collective-permute-start.17 = (bf16[576,128]{1,0:T(8,128)(2,1)S(1)}, bf16[576,128]{1,0:T(8,128)(2,1)S(1)}, u32[]{:S(2)}, u32[]{:S(2)}) collective-permute-start(bf16[576,128]{1,0:T(8,128)(2,1)S(1)} %add.11.value), channel_id=1, source_target_pairs={{0,16},{1,9},{2,18},{3,11},{4,20},{5,13},{6,22},{7,15},{8,24},{9,1... | collective-permute-start | bytes 442376 | tf_op jit(solution)/shard_map/ppermute | solution.py:534
  60.0 8.5 %collective-permute-start.16 = (bf16[576,128]{1,0:T(8,128)(2,1)S(1)}, bf16[576,128]{1,0:T(8,128)(2,1)S(1)}, u32[]{:S(2)}, u32[]{:S(2)}) collective-permute-start(bf16[576,128]{1,0:T(8,128)(2,1)S(1)} %add.11.value), channel_id=1, source_target_pairs={{0,8},{1,17},{2,10},{3,19},{4,12},{5,21},{6,14},{7,23},{8,0},{9,25... | collective-permute-start | bytes 442376 | tf_op jit(solution)/shard_map/ppermute | solution.py:534
  63.4 6.6 %collective-permute-start.22 = (bf16[1152,256]{1,0:T(8,128)(2,1)S(1)}, bf16[1152,256]{1,0:T(8,128)(2,1)S(1)}, u32[]{:S(2)}, u32[]{:S(2)}) collective-permute-start(bf16[1152,256]{1,0:T(8,128)(2,1)S(1)} %join.2.own), channel_id=1, source_target_pairs={{0,1},{1,0},{2,3},{3,2},{4,5},{5,4},{6,7},{7,6},{8,9},{9,8},{10,11... | collective-permute-start | bytes 1769480 | tf_op jit(solution)/shard_map/ppermute | solution.py:534
  68.6 3.6 %collective-permute-start.23 = (bf16[2304,128]{1,0:T(8,128)(2,1)S(1)}, bf16[2304,128]{1,0:T(8,128)(2,1)S(1)}, u32[]{:S(2)}, u32[]{:S(2)}) collective-permute-start(bf16[2304,128]{1,0:T(8,128)(2,1)S(1)} %join.3.refs_0_), channel_id=1, source_target_pairs={{0,1},{1,0},{2,3},{3,2},{4,5},{5,4},{6,7},{7,6},{8,9},{9,8},{10,11... | collective-permute-start | bytes 1769480 | tf_op jit(solution)/shard_map/ppermute | solution.py:534

commit v4 on v3

--- a/solution.py
+++ b/solution.py
@@ -389,7 +389,7 @@
         return carry
 
     lax.fori_loop(0, count + 2, body, 0, unroll=2)
-    step = max(count // 2, 1)
+    step = count
     for r in range(0, count, step):
         at = slice((first + r) * cols, (first + r + step) * cols)
         to = slice(r * cols, (r + step) * cols)

time: 73.6 us -> 73.6 us (level)
  no operation moved by 1% of the time
where the time goes in v4:
time: 73.6 us; the launch traced here: 73.5 us
  Pallas kernels  27.8 us (38%)
  starting transfers between devices  27 us (37%)
  waiting for transfers between devices  17.6 us (24%)
  between operations  1.02 us (1%)
    pallas_call x24, Pallas kernels, kernel_call(): pl.pallas_call(body, out_shape=out_shape, in_specs=in_specs, out_specs=ou...  27.8 us
    ppermute x20, starting transfers between devices, start(): self.got = [lax.ppermute(x, BOTH, p) for x, p in zip(sent, pairs)]  20.4 us
    ppermute x20, waiting for transfers between devices, start(): self.got = [lax.ppermute(x, BOTH, p) for x, p in zip(sent, pairs)]  16.7 us
    ppermute x1, starting transfers between devices, shards(): lon_far = lax.ppermute(far, 'lon', far_lon)  2.75 us
    ppermute x1, starting transfers between devices, shards(): lon_near = lax.ppermute(after([near], act3)[0], 'lon', near_lon)  1.92 us
  transfers between devices with their start and end apart: 24, of which 10 were waited for; matrix products, arithmetic and copies ran while one was open for 0% of the time, Pallas kernels for 30%

profile of v4, /device:TPU:1, one launch (start us, length us, event | category | flops | bytes accessed | tf_op | source)
XLA Modules:
  0.0 73.5 jit_solution(10071935879435134106)
XLA Ops:
  0.6 1.7 %ends.1 = (bf16[2048,256]{1,0:T(8,128)(2,1)S(1)}, bf16[2048,256]{1,0:T(8,128)(2,1)S(1)}, bf16[128,256]{1,0:T(8,128)(2,1)S(1)}, bf16[128,256]{1,0:T(8,128)(2,1)S(1)}) custom-call(bf16[2048,256]{1,0:T(8,128)(2,1)} %bitcast.10, bf16[2048,256]{1,0:T(8,128)(2,1)} %bitcast.11), custom_call_target="tpu_custom_call" | custom-call | bytes 2097152 | tf_op jit(solution)/shard_map/ends/pallas_call | solution.py:38
  2.3 2.8 %collective-permute-start.1 = (bf16[128,256]{1,0:T(8,128)(2,1)S(1)}, bf16[128,256]{1,0:T(8,128)(2,1)S(1)}, u32[]{:S(2)}, u32[]{:S(2)}) collective-permute-start(bf16[128,256]{1,0:T(8,128)(2,1)S(1)} %get-tuple-element.90.own_far), channel_id=1, source_target_pairs={{1,2},{2,1},{3,4},{4,3},{5,6},{6,5},{7,0},{0,7},{9,10},{10,9},{11,... | collective-permute-start | bytes 196616 | tf_op jit(solution)/shard_map/ppermute | solution.py:621
  5.1 2.4 %prep.1 = (bf16[2176,768]{1,0:T(8,128)(2,1)S(1)}, bf16[2176,768]{1,0:T(8,128)(2,1)S(1)}, bf16[2304,256]{1,0:T(8,128)(2,1)S(1)}, bf16[2304,256]{1,0:T(8,128)(2,1)...) custom-call(bf16[2048,256]{1,0:T(8,128)(2,1)S(1)} %get-tuple-element.91.field.refs_3_, ...), custom_call_target="tpu_custom_call" | custom-call | flops 2415919104 | bytes 4456448 | tf_op jit(solution)/shard_map/prep/pallas_call | solution.py:38
  7.5 1.9 %collective-permute-start = (bf16[128,256]{1,0:T(8,128)(2,1)S(1)}, bf16[128,256]{1,0:T(8,128)(2,1)S(1)}, u32[]{:S(2)}, u32[]{:S(2)}) collective-permute-start(bf16[128,256]{1,0:T(8,128)(2,1)S(1)} %get-tuple-element.94.own_near), channel_id=1, source_target_pairs={{0,1},{1,0},{2,3},{3,2},{4,5},{5,4},{6,7},{7,6},{8,9},{9,8},{10,11... | collective-permute-start | bytes 196616 | tf_op jit(solution)/shard_map/ppermute | solution.py:633
  10.3 1.3 %collective-permute-start.2 = (bf16[272,256]{1,0:T(8,128)(2,1)S(1)}, bf16[272,256]{1,0:T(8,128)(2,1)S(1)}, u32[]{:S(2)}, u32[]{:S(2)}) collective-permute-start(bf16[272,256]{1,0:T(8,128)(2,1)S(1)} %get-tuple-element.97), channel_id=1, source_target_pairs={{0,8},{8,0},{16,24},{24,16},{1,9},{9,1},{17,25},{25,17},{2,10},{10... | collective-permute-start | bytes 417800 | tf_op jit(solution)/shard_map/ppermute | solution.py:639
  12.3 5.4 %inner_rows.1 = (bf16[2176,768]{1,0:T(8,128)(2,1)S(1)}, bf16[2176,768]{1,0:T(8,128)(2,1)S(1)}, f32[2176,256]{1,0:T(8,128)S(1)}, bf16[2176,256]{1,0:T(8,128)(2,1)...) custom-call(bf16[128,256]{1,0:T(8,128)(2,1)S(1)} %collective-permute, ...), custom_call_target="tpu_custom_call", output_to_operand_aliasing={{0}: (4, {}), {1}: (5, {})} | custom-call | flops 4831838208 | bytes 9175040 | tf_op jit(solution)/shard_map/inner_rows/pallas_call | solution.py:38
  17.8 3.2 %grad_two.1 = (bf16[2176,768]{1,0:T(8,128)(2,1)S(1)}, bf16[2176,768]{1,0:T(8,128)(2,1)S(1)}, f32[2176,256]{1,0:T(8,128)S(1)}, bf16[2176,256]{1,0:T(8,128)(2,1)S(...) custom-call(bf16[272,256]{1,0:T(8,128)(2,1)S(1)} %collective-permute, ...), custom_call_target="tpu_custom_call", output_to_operand_aliasing={{0}: (3, {}), {1}: (4, {}), {2}: (5, {}), {3}: (6, {}), {4}... | custom-call | flops 2415919104 | bytes 12533760 | tf_op jit(solution)/shard_map/grad_two/pallas_call | solution.py:38
  21.7 3.3 %grad_one.1 = (bf16[2176,256]{1,0:T(8,128)(2,1)S(1)}, f32[2304,128]{1,0:T(8,128)S(1)}, bf16[2304,128]{1,0:T(8,128)(2,1)S(1)}) custom-call(bf16[272,256]{1,0:T(8,128)(2,1)S(1)} %collective-permute-done.2.near.lat_near, bf16[272,256]{1,0:T(8,128)(2,1)S(1)} %collective-permute-done.3.far.lat_far, ...), custom_call_target="tpu_custom_call", output_to_operand_aliasing={{0}: (6, {})} | custom-call | flops 2415919104 | bytes 11485184 | tf_op jit(solution)/shard_map/grad_one/pallas_call | solution.py:38
  25.2 3.4 %collective-permute-start.6 = (bf16[288,256]{1,0:T(8,128)(2,1)S(1)}, bf16[288,256]{1,0:T(8,128)(2,1)S(1)}, u32[]{:S(2)}, u32[]{:S(2)}) collective-permute-start(bf16[288,256]{1,0:T(8,128)(2,1)S(1)} %get-tuple-element.123), channel_id=1, source_target_pairs={{0,8},{1,17},{2,10},{3,19},{4,12},{5,21},{6,14},{7,23},{8,0},{9,25... | collective-permute-start | bytes 442376 | tf_op jit(solution)/shard_map/ppermute | solution.py:534
  34.2 3.4 %collective-permute-done.8.rest_2_ = bf16[288,256]{1,0:T(8,128)(2,1)S(1)} collective-permute-done((bf16[288,256]{1,0:T(8,128)(2,1)S(1)}, bf16[288,256]{1,0:T(8,128)(2,1)S(1)}, u32[]{:S(2)}, u32[]{:S(2)}) %collective-permute-start.8) | collective-permute-done | bytes 147488 | tf_op jit(solution)/shard_map/ppermute | solution.py:534
  38.2 1.7 %field_out.2.refs_5_ = bf16[1024,256]{1,0:T(8,128)(2,1)S(1)} custom-call(f32[80,256]{1,0:T(8,128)S(1)} %get-tuple-element.137.edges.refs_0_, bf16[2176,256]{1,0:T(8,128)(2,1)S(1)} %get-tuple-element.149.value.refs_1_, bf16[2304,256]{1,0:T(8,128)(2,1)S(1)} %get-tuple-element.144.weights.refs_2_, bf16[2048,256]{1,0:T(8,128)(2,1)S(1)} %get-tuple-element.91.field.refs_3_, ...), custom_call_target="tpu_custom_call" | custom-call | flops 1207959552 | bytes 4472832 | tf_op jit(solution)/shard_map/field_out/pallas_call | solution.py:38
  40.2 3.8 %collective-permute-done.12.rest_2_ = bf16[576,128]{1,0:T(8,128)(2,1)S(1)} collective-permute-done((bf16[576,128]{1,0:T(8,128)(2,1)S(1)}, bf16[576,128]{1,0:T(8,128)(2,1)S(1)}, u32[]{:S(2)}, u32[]{:S(2)}) %collective-permute-start.12) | collective-permute-done | bytes 147488 | tf_op jit(solution)/shard_map/ppermute | solution.py:534
  44.6 1.4 %collective-permute-start.13 = (bf16[288,256]{1,0:T(8,128)(2,1)S(1)}, bf16[288,256]{1,0:T(8,128)(2,1)S(1)}, u32[]{:S(2)}, u32[]{:S(2)}) collective-permute-start(bf16[288,256]{1,0:T(8,128)(2,1)S(1)} %add.8.own), channel_id=1, source_target_pairs={{0,4},{1,3},{2,6},{3,1},{4,0},{5,7},{6,2},{7,5},{8,12},{9,11},{10,... | collective-permute-start | bytes 442376 | tf_op jit(solution)/shard_map/ppermute | solution.py:534
  46.0 1.9 %field_out.3 = (bf16[1024,256]{1,0:T(8,128)(2,1)S(1)}, bf16[2048,256]{1,0:T(8,128)(2,1)}) custom-call(f32[80,256]{1,0:T(8,128)S(1)} %get-tuple-element.137.edges.refs_0_, bf16[2176,256]{1,0:T(8,128)(2,1)S(1)} %get-tuple-element.149.value.refs_1_, bf16[2304,256]{1,0:T(8,128)(2,1)S(1)} %get-tuple-element.144.weights.refs_2_, ...), custom_call_target="tpu_custom_call" | custom-call | flops 1207959552 | bytes 4997120 | tf_op jit(solution)/shard_map/field_out/pallas_call | solution.py:38
  47.9 2.3 %collective-permute-done.14.rest_0_ = bf16[576,128]{1,0:T(8,128)(2,1)S(1)} collective-permute-done((bf16[576,128]{1,0:T(8,128)(2,1)S(1)}, bf16[576,128]{1,0:T(8,128)(2,1)S(1)}, u32[]{:S(2)}, u32[]{:S(2)}) %collective-permute-start.14) | collective-permute-done | bytes 147488 | tf_op jit(solution)/shard_map/ppermute | solution.py:534
  50.3 2.8 %collective-permute-done.13.rest_0_ = bf16[288,256]{1,0:T(8,128)(2,1)S(1)} collective-permute-done((bf16[288,256]{1,0:T(8,128)(2,1)S(1)}, bf16[288,256]{1,0:T(8,128)(2,1)S(1)}, u32[]{:S(2)}, u32[]{:S(2)}) %collective-permute-start.13) | collective-permute-done | bytes 147488 | tf_op jit(solution)/shard_map/ppermute | solution.py:534
  53.8 1.5 %collective-permute-start.20 = (bf16[288,256]{1,0:T(8,128)(2,1)S(1)}, bf16[288,256]{1,0:T(8,128)(2,1)S(1)}, u32[]{:S(2)}, u32[]{:S(2)}) collective-permute-start(bf16[288,256]{1,0:T(8,128)(2,1)S(1)} %add.10.value), channel_id=1, source_target_pairs={{0,16},{1,9},{2,18},{3,11},{4,20},{5,13},{6,22},{7,15},{8,24},{9,1... | collective-permute-start | bytes 442376 | tf_op jit(solution)/shard_map/ppermute | solution.py:534
  55.9 1.9 %grad_in.2 = (bf16[1024,256]{1,0:T(8,128)(2,1)S(1)}, bf16[2048,256]{1,0:T(8,128)(2,1)}) custom-call(f32[80,256]{1,0:T(8,128)S(1)} %get-tuple-element.135.refs_0_, bf16[2176,256]{1,0:T(8,128)(2,1)S(1)} %get-tuple-element.162.refs_1_, bf16[2304,256]{1,0:T(8,128)(2,1)S(1)} %get-tuple-element.155.refs_2_, ...), custom_call_target="tpu_custom_call", output_to_operand_aliasing={{1}: (6, {})} | custom-call | flops 1207959552 | bytes 6045696 | tf_op jit(solution)/shard_map/grad_in/pallas_call | solution.py:38
  58.5 1.5 %collective-permute-start.17 = (bf16[576,128]{1,0:T(8,128)(2,1)S(1)}, bf16[576,128]{1,0:T(8,128)(2,1)S(1)}, u32[]{:S(2)}, u32[]{:S(2)}) collective-permute-start(bf16[576,128]{1,0:T(8,128)(2,1)S(1)} %add.11.value), channel_id=1, source_target_pairs={{0,16},{1,9},{2,18},{3,11},{4,20},{5,13},{6,22},{7,15},{8,24},{9,1... | collective-permute-start | bytes 442376 | tf_op jit(solution)/shard_map/ppermute | solution.py:534
  60.9 2.6 %collective-permute-done.19.rest_0_ = bf16[288,256]{1,0:T(8,128)(2,1)S(1)} collective-permute-done((bf16[288,256]{1,0:T(8,128)(2,1)S(1)}, bf16[288,256]{1,0:T(8,128)(2,1)S(1)}, u32[]{:S(2)}, u32[]{:S(2)}) %collective-permute-start.19) | collective-permute-done | bytes 147488 | tf_op jit(solution)/shard_map/ppermute | solution.py:534
  63.5 2.4 %collective-permute-start.22 = (bf16[1152,256]{1,0:T(8,128)(2,1)S(1)}, bf16[1152,256]{1,0:T(8,128)(2,1)S(1)}, u32[]{:S(2)}, u32[]{:S(2)}) collective-permute-start(bf16[1152,256]{1,0:T(8,128)(2,1)S(1)} %join.2.own), channel_id=1, source_target_pairs={{0,1},{1,0},{2,3},{3,2},{4,5},{5,4},{6,7},{7,6},{8,9},{9,8},{10,11... | collective-permute-start | bytes 1769480 | tf_op jit(solution)/shard_map/ppermute | solution.py:534
  65.9 1.9 %grad_in.3 = (bf16[1024,256]{1,0:T(8,128)(2,1)S(1)}, bf16[2048,256]{1,0:T(8,128)(2,1)}) custom-call(f32[80,256]{1,0:T(8,128)S(1)} %get-tuple-element.135.refs_0_, bf16[2176,256]{1,0:T(8,128)(2,1)S(1)} %get-tuple-element.162.refs_1_, bf16[2304,256]{1,0:T(8,128)(2,1)S(1)} %get-tuple-element.155.refs_2_, bf16[2048,256]{1,0:T(8,128)(2,1)S(1)} %get-tuple-element.91.field.refs_3_, ...), custom_call_target="tpu_custom_call" | custom-call | flops 1207959552 | bytes 4997120 | tf_op jit(solution)/shard_map/grad_in/pallas_call | solution.py:38
  68.6 1.4 %collective-permute-start.23 = (bf16[2304,128]{1,0:T(8,128)(2,1)S(1)}, bf16[2304,128]{1,0:T(8,128)(2,1)S(1)}, u32[]{:S(2)}, u32[]{:S(2)}) collective-permute-start(bf16[2304,128]{1,0:T(8,128)(2,1)S(1)} %join.3.refs_0_), channel_id=1, source_target_pairs={{0,1},{1,0},{2,3},{3,2},{4,5},{5,4},{6,7},{7,6},{8,9},{9,8},{10,11... | collective-permute-start | bytes 1769480 | tf_op jit(solution)/shard_map/ppermute | solution.py:534
  70.2 2.0 %scaled.4 = (f32[2304,256]{1,0:T(8,128)}, bf16[2048,256]{1,0:T(8,128)(2,1)}, f32[2304,256]{1,0:T(8,128)}) custom-call(bf16[2304,128]{1,0:T(8,128)(2,1)S(1)} %join.3.refs_0_, bf16[1024,256]{1,0:T(8,128)(2,1)S(1)} %get-tuple-element.163.refs_1_, bf16[2048,256]{1,0:T(8,128)(2,1)} %get-tuple-element.164.refs_2_, ...), custom_call_target="tpu_custom_call", output_to_operand_aliasing={{1}: (2, {})} | custom-call | bytes 4521984 | tf_op jit(solution)/shard_map/scaled/pallas_call | solution.py:38
  (48 shorter events, 14.7 us)
Async XLA Ops:
  2.3 7.1 %collective-permute-start.1 = (bf16[128,256]{1,0:T(8,128)(2,1)S(1)}, bf16[128,256]{1,0:T(8,128)(2,1)S(1)}, u32[]{:S(2)}, u32[]{:S(2)}) collective-permute-start(bf16[128,256]{1,0:T(8,128)(2,1)S(1)} %get-tuple-element.90.own_far), channel_id=1, source_target_pairs={{1,2},{2,1},{3,4},{4,3},{5,6},{6,5},{7,0},{0,7},{9,10},{10,9},{11,... | collective-permute-start | bytes 196616 | tf_op jit(solution)/shard_map/ppermute | solution.py:621
  7.5 2.8 %collective-permute-start = (bf16[128,256]{1,0:T(8,128)(2,1)S(1)}, bf16[128,256]{1,0:T(8,128)(2,1)S(1)}, u32[]{:S(2)}, u32[]{:S(2)}) collective-permute-start(bf16[128,256]{1,0:T(8,128)(2,1)S(1)} %get-tuple-element.94.own_near), channel_id=1, source_target_pairs={{0,1},{1,0},{2,3},{3,2},{4,5},{5,4},{6,7},{7,6},{8,9},{9,8},{10,11... | collective-permute-start | bytes 196616 | tf_op jit(solution)/shard_map/ppermute | solution.py:633
  10.3 7.4 %collective-permute-start.2 = (bf16[272,256]{1,0:T(8,128)(2,1)S(1)}, bf16[272,256]{1,0:T(8,128)(2,1)S(1)}, u32[]{:S(2)}, u32[]{:S(2)}) collective-permute-start(bf16[272,256]{1,0:T(8,128)(2,1)S(1)} %get-tuple-element.97), channel_id=1, source_target_pairs={{0,8},{8,0},{16,24},{24,16},{1,9},{9,1},{17,25},{25,17},{2,10},{10... | collective-permute-start | bytes 417800 | tf_op jit(solution)/shard_map/ppermute | solution.py:639
  11.6 6.1 %collective-permute-start.3 = (bf16[272,256]{1,0:T(8,128)(2,1)S(1)}, bf16[272,256]{1,0:T(8,128)(2,1)S(1)}, u32[]{:S(2)}, u32[]{:S(2)}) collective-permute-start(bf16[272,256]{1,0:T(8,128)(2,1)S(1)} %get-tuple-element.98), channel_id=1, source_target_pairs={{8,16},{16,8},{9,17},{17,9},{10,18},{18,10},{11,19},{19,11},{12,20... | collective-permute-start | bytes 417800 | tf_op jit(solution)/shard_map/ppermute | solution.py:640
  21.0 4.1 %collective-permute-start.5 = (bf16[1152,256]{1,0:T(8,128)(2,1)S(1)}, bf16[1152,256]{1,0:T(8,128)(2,1)S(1)}, u32[]{:S(2)}, u32[]{:S(2)}) collective-permute-start(bf16[1152,256]{1,0:T(8,128)(2,1)S(1)} %get-tuple-element.108), channel_id=1, source_target_pairs={{0,1},{1,0},{2,3},{3,2},{4,5},{5,4},{6,7},{7,6},{8,9},{9,8},{10,11... | collective-permute-start | bytes 1769480 | tf_op jit(solution)/shard_map/ppermute | solution.py:534
  25.0 5.4 %collective-permute-start.4 = (bf16[2304,128]{1,0:T(8,128)(2,1)S(1)}, bf16[2304,128]{1,0:T(8,128)(2,1)S(1)}, u32[]{:S(2)}, u32[]{:S(2)}) collective-permute-start(bf16[2304,128]{1,0:T(8,128)(2,1)S(1)} %get-tuple-element.117), channel_id=1, source_target_pairs={{0,1},{1,0},{2,3},{3,2},{4,5},{5,4},{6,7},{7,6},{8,9},{9,8},{10,11... | collective-permute-start | bytes 1769480 | tf_op jit(solution)/shard_map/ppermute | solution.py:534
  25.2 6.9 %collective-permute-start.6 = (bf16[288,256]{1,0:T(8,128)(2,1)S(1)}, bf16[288,256]{1,0:T(8,128)(2,1)S(1)}, u32[]{:S(2)}, u32[]{:S(2)}) collective-permute-start(bf16[288,256]{1,0:T(8,128)(2,1)S(1)} %get-tuple-element.123), channel_id=1, source_target_pairs={{0,8},{1,17},{2,10},{3,19},{4,12},{5,21},{6,14},{7,23},{8,0},{9,25... | collective-permute-start | bytes 442376 | tf_op jit(solution)/shard_map/ppermute | solution.py:534
  28.6 5.7 %collective-permute-start.7 = (bf16[288,256]{1,0:T(8,128)(2,1)S(1)}, bf16[288,256]{1,0:T(8,128)(2,1)S(1)}, u32[]{:S(2)}, u32[]{:S(2)}) collective-permute-start(bf16[288,256]{1,0:T(8,128)(2,1)S(1)} %get-tuple-element.124), channel_id=1, source_target_pairs={{0,16},{1,9},{2,18},{3,11},{4,20},{5,13},{6,22},{7,15},{8,24},{9,1... | collective-permute-start | bytes 442376 | tf_op jit(solution)/shard_map/ppermute | solution.py:534
  29.3 8.4 %collective-permute-start.8 = (bf16[288,256]{1,0:T(8,128)(2,1)S(1)}, bf16[288,256]{1,0:T(8,128)(2,1)S(1)}, u32[]{:S(2)}, u32[]{:S(2)}) collective-permute-start(bf16[288,256]{1,0:T(8,128)(2,1)S(1)} %get-tuple-element.125), channel_id=1, source_target_pairs={{0,24},{1,25},{2,26},{3,27},{4,28},{5,29},{6,30},{7,31},{8,16},{9,... | collective-permute-start | bytes 442376 | tf_op jit(solution)/shard_map/ppermute | solution.py:534
  30.5 9.5 %collective-permute-start.10 = (bf16[576,128]{1,0:T(8,128)(2,1)S(1)}, bf16[576,128]{1,0:T(8,128)(2,1)S(1)}, u32[]{:S(2)}, u32[]{:S(2)}) collective-permute-start(bf16[576,128]{1,0:T(8,128)(2,1)S(1)} %get-tuple-element.130), channel_id=1, source_target_pairs={{0,8},{1,17},{2,10},{3,19},{4,12},{5,21},{6,14},{7,23},{8,0},{9,25... | collective-permute-start | bytes 442376 | tf_op jit(solution)/shard_map/ppermute | solution.py:534
  31.4 8.8 %collective-permute-start.11 = (bf16[576,128]{1,0:T(8,128)(2,1)S(1)}, bf16[576,128]{1,0:T(8,128)(2,1)S(1)}, u32[]{:S(2)}, u32[]{:S(2)}) collective-permute-start(bf16[576,128]{1,0:T(8,128)(2,1)S(1)} %get-tuple-element.131), channel_id=1, source_target_pairs={{0,16},{1,9},{2,18},{3,11},{4,20},{5,13},{6,22},{7,15},{8,24},{9,1... | collective-permute-start | bytes 442376 | tf_op jit(solution)/shard_map/ppermute | solution.py:534
  32.1 11.9 %collective-permute-start.12 = (bf16[576,128]{1,0:T(8,128)(2,1)S(1)}, bf16[576,128]{1,0:T(8,128)(2,1)S(1)}, u32[]{:S(2)}, u32[]{:S(2)}) collective-permute-start(bf16[576,128]{1,0:T(8,128)(2,1)S(1)} %get-tuple-element.132), channel_id=1, source_target_pairs={{0,24},{1,25},{2,26},{3,27},{4,28},{5,29},{6,30},{7,31},{8,16},{9,... | collective-permute-start | bytes 442376 | tf_op jit(solution)/shard_map/ppermute | solution.py:534
  37.7 6.9 %collective-permute-start.9 = (bf16[288,256]{1,0:T(8,128)(2,1)S(1)}, bf16[288,256]{1,0:T(8,128)(2,1)S(1)}, u32[]{:S(2)}, u32[]{:S(2)}) collective-permute-start(bf16[288,256]{1,0:T(8,128)(2,1)S(1)} %add.6.own), channel_id=1, source_target_pairs={{0,2},{1,5},{2,0},{3,7},{4,6},{5,1},{6,4},{7,3},{8,10},{9,13},{10,... | collective-permute-start | bytes 442376 | tf_op jit(solution)/shard_map/ppermute | solution.py:534
  44.0 6.2 %collective-permute-start.14 = (bf16[576,128]{1,0:T(8,128)(2,1)S(1)}, bf16[576,128]{1,0:T(8,128)(2,1)S(1)}, u32[]{:S(2)}, u32[]{:S(2)}) collective-permute-start(bf16[576,128]{1,0:T(8,128)(2,1)S(1)} %add.7.own), channel_id=1, source_target_pairs={{0,2},{1,5},{2,0},{3,7},{4,6},{5,1},{6,4},{7,3},{8,10},{9,13},{10,... | collective-permute-start | bytes 442376 | tf_op jit(solution)/shard_map/ppermute | solution.py:534
  44.6 8.6 %collective-permute-start.13 = (bf16[288,256]{1,0:T(8,128)(2,1)S(1)}, bf16[288,256]{1,0:T(8,128)(2,1)S(1)}, u32[]{:S(2)}, u32[]{:S(2)}) collective-permute-start(bf16[288,256]{1,0:T(8,128)(2,1)S(1)} %add.8.own), channel_id=1, source_target_pairs={{0,4},{1,3},{2,6},{3,1},{4,0},{5,7},{6,2},{7,5},{8,12},{9,11},{10,... | collective-permute-start | bytes 442376 | tf_op jit(solution)/shard_map/ppermute | solution.py:534
  50.3 7.5 %collective-permute-start.15 = (bf16[576,128]{1,0:T(8,128)(2,1)S(1)}, bf16[576,128]{1,0:T(8,128)(2,1)S(1)}, u32[]{:S(2)}, u32[]{:S(2)}) collective-permute-start(bf16[576,128]{1,0:T(8,128)(2,1)S(1)} %add.9.own), channel_id=1, source_target_pairs={{0,4},{1,3},{2,6},{3,1},{4,0},{5,7},{6,2},{7,5},{8,12},{9,11},{10,... | collective-permute-start | bytes 442376 | tf_op jit(solution)/shard_map/ppermute | solution.py:534
  53.2 6.7 %collective-permute-start.21 = (bf16[288,256]{1,0:T(8,128)(2,1)S(1)}, bf16[288,256]{1,0:T(8,128)(2,1)S(1)}, u32[]{:S(2)}, u32[]{:S(2)}) collective-permute-start(bf16[288,256]{1,0:T(8,128)(2,1)S(1)} %add.10.value), channel_id=1, source_target_pairs={{0,24},{1,25},{2,26},{3,27},{4,28},{5,29},{6,30},{7,31},{8,16},{9,... | collective-permute-start | bytes 442376 | tf_op jit(solution)/shard_map/ppermute | solution.py:534
  53.8 7.1 %collective-permute-start.20 = (bf16[288,256]{1,0:T(8,128)(2,1)S(1)}, bf16[288,256]{1,0:T(8,128)(2,1)S(1)}, u32[]{:S(2)}, u32[]{:S(2)}) collective-permute-start(bf16[288,256]{1,0:T(8,128)(2,1)S(1)} %add.10.value), channel_id=1, source_target_pairs={{0,16},{1,9},{2,18},{3,11},{4,20},{5,13},{6,22},{7,15},{8,24},{9,1... | collective-permute-start | bytes 442376 | tf_op jit(solution)/shard_map/ppermute | solution.py:534
  55.3 8.2 %collective-permute-start.19 = (bf16[288,256]{1,0:T(8,128)(2,1)S(1)}, bf16[288,256]{1,0:T(8,128)(2,1)S(1)}, u32[]{:S(2)}, u32[]{:S(2)}) collective-permute-start(bf16[288,256]{1,0:T(8,128)(2,1)S(1)} %add.10.value), channel_id=1, source_target_pairs={{0,8},{1,17},{2,10},{3,19},{4,12},{5,21},{6,14},{7,23},{8,0},{9,25... | collective-permute-start | bytes 442376 | tf_op jit(solution)/shard_map/ppermute | solution.py:534
  57.8 10.0 %collective-permute-start.18 = (bf16[576,128]{1,0:T(8,128)(2,1)S(1)}, bf16[576,128]{1,0:T(8,128)(2,1)S(1)}, u32[]{:S(2)}, u32[]{:S(2)}) collective-permute-start(bf16[576,128]{1,0:T(8,128)(2,1)S(1)} %add.11.value), channel_id=1, source_target_pairs={{0,24},{1,25},{2,26},{3,27},{4,28},{5,29},{6,30},{7,31},{8,16},{9,... | collective-permute-start | bytes 442376 | tf_op jit(solution)/shard_map/ppermute | solution.py:534
  58.5 9.4 %collective-permute-start.17 = (bf16[576,128]{1,0:T(8,128)(2,1)S(1)}, bf16[576,128]{1,0:T(8,128)(2,1)S(1)}, u32[]{:S(2)}, u32[]{:S(2)}) collective-permute-start(bf16[576,128]{1,0:T(8,128)(2,1)S(1)} %add.11.value), channel_id=1, source_target_pairs={{0,16},{1,9},{2,18},{3,11},{4,20},{5,13},{6,22},{7,15},{8,24},{9,1... | collective-permute-start | bytes 442376 | tf_op jit(solution)/shard_map/ppermute | solution.py:534
  59.9 8.6 %collective-permute-start.16 = (bf16[576,128]{1,0:T(8,128)(2,1)S(1)}, bf16[576,128]{1,0:T(8,128)(2,1)S(1)}, u32[]{:S(2)}, u32[]{:S(2)}) collective-permute-start(bf16[576,128]{1,0:T(8,128)(2,1)S(1)} %add.11.value), channel_id=1, source_target_pairs={{0,8},{1,17},{2,10},{3,19},{4,12},{5,21},{6,14},{7,23},{8,0},{9,25... | collective-permute-start | bytes 442376 | tf_op jit(solution)/shard_map/ppermute | solution.py:534
  63.5 6.5 %collective-permute-start.22 = (bf16[1152,256]{1,0:T(8,128)(2,1)S(1)}, bf16[1152,256]{1,0:T(8,128)(2,1)S(1)}, u32[]{:S(2)}, u32[]{:S(2)}) collective-permute-start(bf16[1152,256]{1,0:T(8,128)(2,1)S(1)} %join.2.own), channel_id=1, source_target_pairs={{0,1},{1,0},{2,3},{3,2},{4,5},{5,4},{6,7},{7,6},{8,9},{9,8},{10,11... | collective-permute-start | bytes 1769480 | tf_op jit(solution)/shard_map/ppermute | solution.py:534
  68.6 3.6 %collective-permute-start.23 = (bf16[2304,128]{1,0:T(8,128)(2,1)S(1)}, bf16[2304,128]{1,0:T(8,128)(2,1)S(1)}, u32[]{:S(2)}, u32[]{:S(2)}) collective-permute-start(bf16[2304,128]{1,0:T(8,128)(2,1)S(1)} %join.3.refs_0_), channel_id=1, source_target_pairs={{0,1},{1,0},{2,3},{3,2},{4,5},{5,4},{6,7},{7,6},{8,9},{9,8},{10,11... | collective-permute-start | bytes 1769480 | tf_op jit(solution)/shard_map/ppermute | solution.py:534
